TPU v7x, 256 devices: a whole 4x4x8 slice. The times are simulated.
256 devices in a mesh: row: 16 (over z, x_hi), col: 16 (over x_lo, y, core).
Axes of the slice: x: 4 (x_hi: 2, x_lo: 2; x = x_hi * 2 + x_lo), y: 4, z: 8, core: 2. Of those that a mesh axis runs over, the one named last changes fastest.
Arguments:
- inputs: bfloat16 [2048, 8192], P('row', 'col'), may hold values from -6 to 6
- cotangent: bfloat16 [2048, 32768], P('col', 'row'), may hold values from -6 to 6
- sparse_blocks: bfloat16 [16, 16, 16, 4096], P('col', 'row'), may hold values from -0.25 to 0.25
- block_index: int32 [16, 16, 16], P('col', 'row'), may hold values from 0 to 255, as said below
- u_factor: bfloat16 [8192, 256], P('col'), may hold values from -0.0625 to 0.0625
- v_factor: bfloat16 [256, 32768], P(None, 'row'), may hold values from -0.375 to 0.375
Outputs:
- hidden: bfloat16 [2048, 32768], P('col', 'row')
- input_grad: bfloat16 [2048, 8192], P('row', 'col')
- blocks_grad: bfloat16 [16, 16, 16, 4096], P('col', 'row')
- u_grad: float32 [8192, 256], P('col', 'row')
- v_grad: float32 [256, 32768], P('col', 'row')
Inputs may be any that keep to these rules, and one draw needn't show every extreme that they name: `block_index`: within one shard (c, r) the 16 positions are distinct, each in 0 to 255.
All inputs are finite; a program needn't handle non-finite values.
Results may differ from a plain program's by a relative error of at most 0.015.
Values may be sent and summed in bfloat16 or wider, within the bound.
No kernel may reach another device: no remote copies, remote signals or barrier semaphores. Data moves between devices by JAX's collectives and lax.ppermute only.
A program may use at most 128 MiB of HBM per device.

v0:
```python
import jax
import jax.numpy as jnp
from jax import lax
from jax.sharding import PartitionSpec as P

BS = 64


def gelu_value(z):
    return 0.5 * z * (1.0 + lax.erf(z * 0.7071067811865476))


def gelu_slope(z):
    return (
        0.5 * (1.0 + lax.erf(z * 0.7071067811865476))
        + z * jnp.exp(-0.5 * z * z) * 0.3989422804014327
    )


def paired_product(form, coarse, fine):
    return jnp.einsum(form, coarse.astype(jnp.float32), fine, precision=lax.Precision.HIGHEST)


def on_device(inputs, cotangent, sparse_blocks, block_index, u_factor, v_factor):
    width_c = inputs.shape[1]
    width_r = cotangent.shape[1]
    brows = width_c // BS
    bcols = width_r // BS
    index = block_index.reshape(-1)
    onehot_rows = (index[:, None] // bcols == jnp.arange(brows, dtype=jnp.int32)[None, :]).astype(
        jnp.bfloat16
    )
    onehot_cols = (index[:, None] % bcols == jnp.arange(bcols, dtype=jnp.int32)[None, :]).astype(
        jnp.bfloat16
    )
    weights = sparse_blocks.reshape(-1, BS, BS)
    gathered = lax.all_gather(inputs, "row", axis=0, tiled=True)
    count = gathered.shape[0]
    x_blocks = gathered.reshape(count, brows, BS)
    picked = jnp.einsum(
        "tkf,bk->btf", x_blocks, onehot_rows, preferred_element_type=jnp.float32
    ).astype(jnp.bfloat16)
    rank_part = jnp.dot(gathered, u_factor, preferred_element_type=jnp.float32)
    products = jnp.einsum("btf,bfg->btg", picked, weights, preferred_element_type=jnp.float32)
    sparse_part = jnp.einsum("btg,bc->tcg", products, onehot_cols.astype(jnp.float32)).reshape(
        count, width_r
    )
    z_sparse = lax.psum_scatter(
        sparse_part.astype(jnp.bfloat16), "col", scatter_dimension=0, tiled=True
    ).astype(jnp.float32)
    p_low = lax.psum_scatter(rank_part, "col", scatter_dimension=0, tiled=True).astype(jnp.bfloat16)
    z_local = z_sparse + jnp.dot(p_low, v_factor, preferred_element_type=jnp.float32)
    hidden = gelu_value(z_local).astype(jnp.bfloat16)
    dz_local = (cotangent.astype(jnp.float32) * gelu_slope(z_local)).astype(jnp.bfloat16)
    factor_part = jnp.dot(p_low.T, dz_local, preferred_element_type=jnp.float32)
    v_grad = lax.psum_scatter(factor_part, "col", scatter_dimension=0, tiled=True)
    dz_all = lax.all_gather(dz_local, "col", axis=0, tiled=True)
    dz_blocks = dz_all.reshape(count, bcols, BS)
    dz_picked = jnp.einsum(
        "tcg,bc->btg", dz_blocks, onehot_cols, preferred_element_type=jnp.float32
    ).astype(jnp.bfloat16)
    block_grads = jnp.einsum("btf,btg->bfg", picked, dz_picked, preferred_element_type=jnp.float32)
    blocks_grad = block_grads.reshape(sparse_blocks.shape).astype(jnp.bfloat16)
    back = jnp.einsum("btg,bfg->btf", dz_picked, weights, preferred_element_type=jnp.float32)
    x_sparse = jnp.einsum("btf,bk->tkf", back, onehot_rows.astype(jnp.float32)).reshape(
        count, width_c
    )
    q_part = jnp.einsum("tf,rf->tr", dz_all, v_factor, preferred_element_type=jnp.float32)
    x_part = x_sparse + paired_product("fr,tr->tf", u_factor, q_part)
    input_grad = lax.psum_scatter(x_part, "row", scatter_dimension=0, tiled=True).astype(
        jnp.bfloat16
    )
    u_part = paired_product("tf,tr->fr", gathered, q_part)
    u_grad = lax.psum_scatter(u_part, "row", scatter_dimension=1, tiled=True)
    return (hidden, input_grad, blocks_grad, u_grad, v_grad)


def solution(mesh):
    in_specs = (
        P("row", "col"),
        P("col", "row"),
        P("col", "row", None, None),
        P("col", "row", None),
        P("col", None),
        P(None, "row"),
    )
    out_specs = (
        P("col", "row"),
        P("row", "col"),
        P("col", "row", None, None),
        P("col", "row"),
        P("col", "row"),
    )
    return jax.shard_map(
        on_device, mesh=mesh, in_specs=in_specs, out_specs=out_specs, check_vma=False
    )
```

profile of v0, /device:TPU:1, one launch (start us, length us, event | category | flops | bytes accessed | tf_op | source)
XLA Modules:
  0.0 844.0 jit_solution(14653182877109291951)
XLA Ops:
  7.2 0.0 copy-start
  7.2 0.0 all-gather.3.cloned.1.call-start
  7.2 1.7 copy.14
  9.0 0.0 all-gather.3.cloned.1.call-update
  9.0 0.0 copy-start.9
  9.0 0.0 reduce-scatter.8.cloned.1.call-start
  9.1 87.7 %all-gather.3.cloned.1.call-done = bf16[2048,512]{0,1:T(8,128)(2,1)} async-done(((bf16[128,512]{0,1:T(8,128)(2,1)}), bf16[2048,512]{0,1:T(8,128)(2,1)}) %all-gather.3.cloned.1.call-update) | async-done | bytes 2097168 | tf_op jit(solution)/shard_map/all_gather | solution.py:37
  96.8 3.8 fusion.46
  100.6 0.0 reduce-scatter.8.cloned.1.call-update
  100.7 0.0 reduce-scatter.6.cloned.1.call-start
  100.7 0.2 reshape.126
  101.0 1.9 convolution_convert_fusion
  102.9 5.6 fusion.15
  108.4 5.9 convert_bitcast_fusion
  114.3 11.3 %copy.16 = bf16[2048,32,64]{0,2,1:T(8,128)(2,1)} copy(bf16[2048,32,64]{0,1,2:T(8,128)(2,1)} %convert_bitcast_fusion) | data formatting | bytes 16777216 | tf_op jit(solution)/shard_map/convert_element_type | solution.py:49
  125.7 12.3 %copy.17 = bf16[2048,2048]{1,0:T(8,128)(2,1)} copy(bf16[2048,2048]{0,1:T(8,128)(2,1)} %bitcast.47) | data formatting | bytes 16777216 | tf_op jit(solution)/shard_map/convert_element_type | solution.py:49
  138.0 0.0 reduce-scatter.6.cloned.1.call-update
  138.0 0.0 all-gather.5.cloned.1.call-start
  138.0 25.0 %reduce-scatter.8.cloned.1.call-done = f32[128,256]{1,0:T(8,128)} async-done(((f32[2048,256]{1,0:T(8,128)}), f32[128,256]{1,0:T(8,128)}) %reduce-scatter.8.cloned.1.call-update) | async-done | bytes 131088 | tf_op jit(solution)/shard_map/reduce_scatter | solution.py:51
  163.0 78.1 %reduce-scatter.6.cloned.1.call-done = bf16[128,2048]{1,0:T(8,128)(2,1)} async-done(((bf16[2048,2048]{1,0:T(8,128)(2,1)}), bf16[128,2048]{1,0:T(8,128)(2,1)}) %reduce-scatter.6.cloned.1.call-update) | async-done | bytes 524304 | tf_op jit(solution)/shard_map/reduce_scatter | solution.py:48
  241.1 3.0 fusion.32
  244.1 0.0 all-gather.5.cloned.1.call-update
  244.1 0.0 reduce-scatter.10.cloned.1.call-start
  244.2 57.4 %all-gather.5.cloned.1.call-done = bf16[2048,2048]{1,0:T(8,128)(2,1)} async-done(((bf16[128,2048]{1,0:T(8,128)(2,1)}), bf16[2048,2048]{1,0:T(8,128)(2,1)}) %all-gather.5.cloned.1.call-update) | async-done | bytes 8388624 | tf_op jit(solution)/shard_map/all_gather | solution.py:57
  301.6 11.9 %copy.18 = bf16[2048,2048]{0,1:T(8,128)(2,1)} copy(bf16[2048,2048]{1,0:T(8,128)(2,1)} %all-gather.5.cloned.1.call-done) | data formatting | bytes 16777216 | tf_op jit(solution)/shard_map/all_gather | solution.py:57
  313.6 12.4 %fusion.8 = bf16[16,2048,64]{1,0,2:T(8,128)(2,1)S(1)} fusion(bf16[2048,32,64]{0,2,1:T(8,128)(2,1)} %bitcast.48, s32[16]{0:T(128)S(1)} %get-tuple-element.7), kind=kOutput, calls=%fused_computation.7 | convolution fusion | flops 136315392 | bytes 12582976 | tf_op jit(solution)/shard_map/tcg,bc->btg/dot_general | solution.py:59
  325.9 5.9 fusion.11
  331.8 4.6 fusion.18
  336.4 4.4 copy.20
  340.9 5.5 copy.21
  346.4 0.0 copy-start.6
  346.4 6.0 fusion.47
  352.4 1.3 copy-done.5
  353.8 3.9 convolution_add_fusion
  357.7 0.0 reduce-scatter.10.cloned.1.call-update
  357.7 0.0 reduce-scatter.14.cloned.1.call-start
  357.8 0.8 copy-done.8
  358.6 2.8 fusion.33
  361.4 0.0 reduce-scatter.14.cloned.1.call-update
  361.4 0.0 reduce-scatter.12.cloned.1.call-start
  361.5 5.9 convolution_bitcast_fusion
  367.4 0.0 reduce-scatter.12.cloned.1.call-update
  367.4 8.1 fusion.22
  375.4 0.9 convert_element_type.65
  376.4 189.8 %reduce-scatter.10.cloned.1.call-done = f32[128,512]{1,0:T(8,128)} async-done(((f32[2048,512]{1,0:T(8,128)}), f32[128,512]{1,0:T(8,128)}) %reduce-scatter.10.cloned.1.call-update) | async-done | bytes 262160 | tf_op jit(solution)/shard_map/reduce_scatter | solution.py:70
  566.2 1.6 convert_element_type.63
  567.8 66.6 %reduce-scatter.14.cloned.1.call-done = f32[16,2048]{1,0:T(8,128)} async-done(((f32[256,2048]{1,0:T(8,128)}), f32[16,2048]{1,0:T(8,128)}) %reduce-scatter.14.cloned.1.call-update) | async-done | bytes 131088 | tf_op jit(solution)/shard_map/reduce_scatter | solution.py:56
  634.4 202.5 %reduce-scatter.12.cloned.1.call-done = f32[512,16]{0,1:T(8,128)} async-done(((f32[512,256]{0,1:T(8,128)}), f32[512,16]{0,1:T(8,128)}) %reduce-scatter.12.cloned.1.call-update) | async-done | bytes 32784 | tf_op jit(solution)/shard_map/reduce_scatter | solution.py:74
  (16 shorter events, 0.0 us)
Async XLA Ops:
  7.2 233.9 %copy-start = (bf16[256,2048]{1,0:T(8,128)(2,1)S(1)}, bf16[256,2048]{1,0:T(8,128)(2,1)}, u32[]{:S(2)}) copy-start(bf16[256,2048]{1,0:T(8,128)(2,1)} %param.11) | copy-start | bytes 3145732
  7.2 89.6 %all-gather.3.cloned.1.call-start = ((), (), s32[]{:S(2)}) async-start(), calls=%async_computation.5 | async-start | bytes 2228224 | tf_op jit(solution)/shard_map/all_gather | solution.py:37
  9.0 91.7 %copy-start.7 = (bf16[1,1,16,4096]{3,2,1,0:T(8,128)(2,1)S(1)}, bf16[1,1,16,4096]{3,2,1,0:T(8,128)(2,1)}, u32[]{:S(2)}) copy-start(bf16[1,1,16,4096]{3,2,1,0:T(8,128)(2,1)} %param.8) | copy-start | bytes 393220
  9.0 92.0 %copy-start.9 = (s32[1,1,16]{2,1,0:T(1,128)S(1)}, s32[1,1,16]{2,1,0:T(1,128)}, u32[]{:S(2)}) copy-start(s32[1,1,16]{2,1,0:T(1,128)} %param.9) | copy-start | bytes 196
  9.0 154.0 %reduce-scatter.8.cloned.1.call-start = ((), (), s32[]{:S(2)}) async-start(), calls=%async_computation.7 | async-start | bytes 2228224 | tf_op jit(solution)/shard_map/reduce_scatter | solution.py:51
  96.8 4.2 copy-start.1
  100.7 140.4 %reduce-scatter.6.cloned.1.call-start = ((), (), s32[]{:S(2)}) async-start(), calls=%async_computation.6 | async-start | bytes 8912896 | tf_op jit(solution)/shard_map/reduce_scatter | solution.py:48
  102.9 5.6 copy-start.2
  138.0 163.6 %all-gather.5.cloned.1.call-start = ((), (), s32[]{:S(2)}) async-start(), calls=%async_computation.8 | async-start | bytes 8912896 | tf_op jit(solution)/shard_map/all_gather | solution.py:57
  244.1 322.0 %reduce-scatter.10.cloned.1.call-start = ((), (), s32[]{:S(2)}) async-start(), calls=%async_computation.9 | async-start | bytes 4456448 | tf_op jit(solution)/shard_map/reduce_scatter | solution.py:70
  325.9 5.9 copy-start.3
  346.4 7.4 copy-start.4
  346.4 7.4 copy-start.6
  352.4 1.3 copy-start.5
  357.7 0.9 copy-start.8
  357.7 276.7 %reduce-scatter.14.cloned.1.call-start = ((), (), s32[]{:S(2)}) async-start(), calls=%async_computation.11 | async-start | bytes 2228224 | tf_op jit(solution)/shard_map/reduce_scatter | solution.py:56
  361.4 475.5 %reduce-scatter.12.cloned.1.call-start = ((), (), s32[]{:S(2)}) async-start(), calls=%async_computation.10 | async-start | bytes 557056 | tf_op jit(solution)/shard_map/reduce_scatter | solution.py:74
Sparse Core Ops, SparseCore 0:
  11.1 85.6 all-gather.2
  100.8 62.1 reduce-scatter.7
  165.5 75.4 reduce-scatter.5
  244.3 57.3 all-gather.4
  357.8 208.2 reduce-scatter.9
  569.3 65.0 reduce-scatter.13
  639.3 197.5 reduce-scatter.11
where the time goes:
time: 856 us; the launch traced here: 844 us
  waiting for transfers between devices  707 us (83%)
  matrix products  69.7 us (8%)
  local copies, waits for them, and re-layouts  50.6 us (6%)
  between operations  14.5 us (2%)
    reduce_scatter x1, waiting for transfers between devices, on_device(): u_grad = lax.psum_scatter(u_part, 'row', scatter_dimension=1, tiled=True)  203 us
    reduce_scatter x1, waiting for transfers between devices, on_device(): lax.psum_scatter(x_part, 'row', scatter_dimension=0, tiled=True)  190 us
    all_gather x1, waiting for transfers between devices, on_device(): gathered = lax.all_gather(inputs, 'row', axis=0, tiled=True)  87.7 us
    reduce_scatter x1, waiting for transfers between devices, on_device(): lax.psum_scatter(sparse_part.astype(jnp.bfloat16), 'col', scatter_dimensi...  78.1 us
    reduce_scatter x1, waiting for transfers between devices, on_device(): lax.psum_scatter(factor_part, 'col', scatter_dimension=0, tiled=True)  66.6 us
    all_gather x1, waiting for transfers between devices, on_device(): dz_all = lax.all_gather(dz_local, 'col', axis=0, tiled=True)  57.4 us
    reduce_scatter x1, waiting for transfers between devices, on_device(): lax.psum_scatter(rank_part, 'col', scatter_dimension=0, tiled=True)  25 us
    convert_element_type x2, local copies, waits for them, and re-layouts, on_device(): sparse_part.astype(jnp.bfloat16)  23.6 us
  transfers between devices with their start and end apart: 7, of which 7 were waited for; matrix products, arithmetic and copies ran while one was open for 7% of the time, Pallas kernels for 0%

commit v1 on v0

v1 whole, which is shorter than its diff:
```python
import functools

import jax
import jax.numpy as jnp
from jax import lax
from jax.experimental import pallas as pl
from jax.experimental.pallas import tpu as pltpu
from jax.sharding import Mesh, PartitionSpec as P

BS = 64
NB = 16
SH = 16
NZ = 8
NK = 8
FEAT = 512
WIDTH = 2048
TOK = 128
RANK = 256
RS = RANK // SH
WROWS = FEAT + 16
VROWS = WIDTH // TOK * RS
UROWS = FEAT // TOK * RS
BCOLS = WIDTH // BS

ROW = ("z", "xh")
COL = ("xl", "y", "core")
ALL = ROW + COL

NN = (((1,), (0,)), ((), ()))
NT = (((1,), (1,)), ((), ()))
F32 = jnp.float32
BF16 = jnp.bfloat16


def dot(a, b, dims):
    return lax.dot_general(a, b, dims, preferred_element_type=F32)


def gelu_pair(z):
    half = 0.5 * (1.0 + lax.erf(z * 0.7071067811865476))
    slope = half + z * jnp.exp(-0.5 * z * z) * 0.3989422804014327
    return z * half, slope


def block_start(position):
    return pl.multiple_of(position * BS, BS)


def x_slot(place, s):
    return (((s >> 1) - place[0]) & (NZ - 1)) * 2 + ((s & 1) ^ place[1])


def x_shard(place, slot):
    return (((slot >> 1) + place[0]) & (NZ - 1)) * 2 + ((slot & 1) ^ place[1])


def w_slot(place, s):
    return ((s & 1) ^ place[2]) * NK + (s >> 1)


def forward_kernel(place, index, *refs):
    x_parts = refs[: 2 * NZ]
    w_own, w_other, p_t, v, cot, hidden, dz_t, q_t, x, w, z_t, sems = refs[2 * NZ :]
    copies = [
        pltpu.make_async_copy(w_own, w.at[:NK], sems.at[2 * NZ]),
        pltpu.make_async_copy(w_other, w.at[NK:], sems.at[2 * NZ + 1]),
    ]
    for slot in range(2 * NZ):
        copies.append(pltpu.make_async_copy(x_parts[slot], x.at[slot], sems.at[slot]))
    for copy in copies:
        copy.start()
    z_t[...] = jnp.zeros_like(z_t)
    for copy in copies:
        copy.wait()

    def shard(slot, carry):
        s = w_slot(place, x_shard(place, slot))
        sums = []
        for pair in range(NB // 2):
            both = w[s, pair * BS : (pair + 1) * BS, :].T
            for side in range(2):
                b = index[s, 2 * pair + side]
                x_block = x[slot, pl.ds(block_start(b // BCOLS), BS), :]
                sums.append((b % BCOLS, dot(both[side * BS : (side + 1) * BS], x_block, NN)))
        for where, value in sums:
            z_t[pl.ds(block_start(where), BS), :] += value
        return carry

    lax.fori_loop(0, SH, shard, 0)
    p = p_t[...].T
    for j in range(WIDTH // TOK):
        part = slice(j * TOK, (j + 1) * TOK)
        z = z_t[part, :].T + dot(p, v[:, part], NN)
        value, slope = gelu_pair(z)
        hidden[:, part] = value.astype(BF16)
        dz = cot[:, part].astype(F32) * slope
        dz_t[part, :] = dz.T.astype(BF16)
    q_t[...] = dot(v[...], dz_t[...], NN)


def back_kernel(slots, place, index, w, dz_t, *refs):
    outs = refs[: len(slots)]
    total, done = refs[len(slots) :]

    def shard(i, carry):
        slot = (i + slots[0]) & (2 * NZ - 1)
        s = w_slot(place, x_shard(place, slot))
        total[...] = jnp.zeros_like(total)
        sums = []
        for pair in range(NB // 2):
            both = w[s, pair * BS : (pair + 1) * BS, :]
            for side in range(2):
                b = index[s, 2 * pair + side]
                dz_block = dz_t[pl.ds(block_start(b % BCOLS), BS), :]
                sums.append((b // BCOLS, dot(both[:, side * BS : (side + 1) * BS], dz_block, NN)))
        for where, value in sums:
            total[pl.ds(block_start(where), BS), :] += value
        done[i] = total[...].astype(BF16)
        return carry

    lax.fori_loop(0, len(slots), shard, 0)
    for i in range(len(slots)):
        outs[i][...] = done[i]


def grad_rows(place, index, x, dz_t, p_t, out, half, other):
    core = place[2] ^ half

    def plus(value, k, first):
        if other is not None:
            value += other[k, first : first + value.shape[0], :].astype(F32)
        return value.astype(BF16)

    def shard(k, carry):
        slot = x_slot(place, 2 * k + core)
        for pair in range(NB // 2):
            halves = []
            for side in range(2):
                b = index[half * NK + k, 2 * pair + side]
                x_block = x[slot, pl.ds(block_start(b // BCOLS), BS), :]
                dz_block = dz_t[pl.ds(block_start(b % BCOLS), BS), :]
                halves.append(dot(x_block, dz_block, NT))
            both = jnp.concatenate(halves, axis=1)
            out[k, pair * BS : (pair + 1) * BS, :] = plus(both, k, pair * BS)
        return carry

    lax.fori_loop(0, NK, shard, 0)
    p = jnp.concatenate([p_t[2 * k + core] for k in range(NK)], axis=0)
    for j in range(WIDTH // TOK):
        part = dot(p, dz_t[j * TOK : (j + 1) * TOK, :], NT)
        first = FEAT + j * RS
        for k in range(NK):
            out[k, first : first + RS, :] = plus(part[k * RS : (k + 1) * RS], k, first)


def grad_other_kernel(place, index, x, dz_t, p_t, out):
    grad_rows(place, index, x, dz_t, p_t, out, 1, None)


def grad_own_kernel(place, index, x, dz_t, p_t, q_t, other, out):
    grad_rows(place, index, x, dz_t, p_t, out, 0, other)
    q = q_t[place[3]]

    def shard(k, carry):
        for half in range(2):
            u = dot(q, x[x_slot(place, 2 * k + (place[2] ^ half))], NT).astype(BF16)
            for j in range(FEAT // TOK):
                first = FEAT + VROWS + half * UROWS + j * RS
                out[k, first : first + RS, :] = u[:, j * TOK : (j + 1) * TOK]
        return carry

    lax.fori_loop(0, NK, shard, 0)


def call(kernel, out_shape, flops, bytes_accessed, operands, scratch=(), free=0):
    vmem = pl.BlockSpec(memory_space=pltpu.VMEM)
    smem = pl.BlockSpec(memory_space=pltpu.SMEM)
    anywhere = pl.BlockSpec(memory_space=pltpu.HBM)
    many = isinstance(out_shape, tuple)
    return pl.pallas_call(
        kernel,
        out_shape=out_shape,
        in_specs=[smem] * 2 + [anywhere] * free + [vmem] * (len(operands) - 2 - free),
        out_specs=(vmem,) * len(out_shape) if many else vmem,
        scratch_shapes=list(scratch),
        compiler_params=pltpu.CompilerParams(vmem_limit_bytes=16 << 20),
        cost_estimate=pl.CostEstimate(
            flops=flops, bytes_accessed=bytes_accessed, transcendentals=0
        ),
    )(*operands)


def shape(*dims, kind=BF16):
    return jax.ShapeDtypeStruct(dims, kind)


def add(*terms):
    return sum(t.astype(F32) for t in terms).astype(BF16)


def shift(x, by):
    return lax.ppermute(x, "z", [(i, (i + by) % NZ) for i in range(NZ)])


def gather_ring(own):
    held = {0: own}
    for step in range(1, NZ // 2):
        held[-step] = shift(held[1 - step], 1)
        held[step] = shift(held[step - 1], -1)
    return held


def meet(x, axis, flip):
    count = {"z": 8, "xh": 2, "xl": 2, "y": 4, "core": 2}[axis]
    return lax.ppermute(x, axis, [(i, i ^ flip) for i in range(count)])


def on_device(inputs, cotangent, sparse_blocks, block_index, u_factor, v_factor):
    turn = [(r * SH + c, c * SH + r) for r in range(SH) for c in range(SH)]
    place = jnp.stack(
        [lax.axis_index("z"), lax.axis_index("xh"), lax.axis_index("core"), lax.axis_index(ROW)]
    ).astype(jnp.int32)

    w_pairs = sparse_blocks.reshape(NB // 2, 2, BS, BS).transpose(0, 2, 1, 3).reshape(FEAT, 2 * BS)
    index_row = jnp.zeros((16, TOK), BF16).at[0, :NB].set(block_index.reshape(NB).astype(BF16))
    w_mine, mine = lax.optimization_barrier((jnp.concatenate([w_pairs, index_row]), inputs.T))
    w_own = lax.all_gather(w_mine, ("xl", "y"), axis=0)

    turned = lax.ppermute(mine, ALL, turn)
    p = lax.dot_general(u_factor, mine, (((0,), (0,)), ((), ())), preferred_element_type=F32)
    p = p + meet(p, "core", 1)
    turned, p = lax.optimization_barrier((turned, p))
    rings = [gather_ring(turned), gather_ring(meet(turned, "xh", 1))]
    rings[0][4] = shift(rings[0][-3], 1)
    rings[1][4] = shift(rings[1][3], -1)
    x_parts = [rings[j][rel if rel <= 4 else rel - NZ] for rel in range(NZ) for j in range(2)]
    for axis, flip in (("xl", 1), ("y", 1), ("y", 2)):
        p = p + meet(p, axis, flip)
    thirds = [ring[i] for ring in rings for i in (3, -3)]
    w_own, p, _ = lax.optimization_barrier((w_own, p.astype(BF16), thirds))
    w_other = meet(w_own, "core", 1)
    p_t = lax.ppermute(p, ALL, turn)
    index = jnp.concatenate([w_own[:, FEAT, :NB], w_other[:, FEAT, :NB]]).astype(jnp.int32)

    hidden, dz_t, q, x_all, w_all = call(
        forward_kernel,
        (
            shape(TOK, WIDTH),
            shape(WIDTH, TOK),
            shape(RANK, TOK, kind=F32),
            shape(SH, FEAT, TOK),
            shape(SH, WROWS, TOK),
        ),
        800_000_000,
        10 << 20,
        (place, index, *x_parts, w_own, w_other, p_t, v_factor, cotangent),
        [pltpu.VMEM((WIDTH, TOK), F32), pltpu.SemaphoreType.DMA((2 * NZ + 2,))],
        free=2 * NZ + 2,
    )
    back = {}
    for slots in (range(6, 12), range(12, 22)):
        parts = call(
            functools.partial(back_kernel, slots),
            (shape(FEAT, TOK),) * len(slots),
            20_000_000 * len(slots),
            len(slots) << 19,
            (place, index, w_all, dz_t),
            [pltpu.VMEM((FEAT, TOK), F32), pltpu.VMEM((len(slots), FEAT, TOK), BF16)],
        )
        back.update({slot % (2 * NZ): part for slot, part in zip(slots, parts)})

    def own(rel, j):
        return back[2 * (rel % NZ) + j]

    q, _ = lax.optimization_barrier((q, back[0]))
    for axis, flip in (("z", 1), ("z", 2), ("z", 4), ("xh", 1)):
        q = q + meet(q.astype(BF16), axis, flip).astype(F32)
    q_t = q.astype(BF16)

    p_slices = p_t.reshape(SH, RS, TOK)
    grads = call(
        grad_other_kernel,
        shape(NK, FEAT + VROWS, TOK),
        200_000_000,
        4 << 20,
        (place, index, x_all, dz_t, p_slices),
    )
    grads = call(
        grad_own_kernel,
        shape(NK, FEAT + VROWS + 2 * UROWS, TOK),
        300_000_000,
        6 << 20,
        (place, index, x_all, dz_t, p_slices, q_t.reshape(SH, RS, TOK), meet(grads, "core", 1)),
    )
    up = [own(3, 0), own(3, 1)]
    down = [own(-3, 0), own(-3, 1)]
    up[0] = add(up[0], shift(own(4, 0), 1))
    down[1] = add(down[1], shift(own(4, 1), -1))
    for rel in (2, 1):
        if rel == 1:
            grads, up[0] = lax.optimization_barrier((grads, up[0]))
        for j in range(2):
            up[j] = add(own(rel, j), shift(up[j], 1))
            down[j] = add(own(-rel, j), shift(down[j], -1))
    other = add(own(0, 1), shift(up[1], 1), shift(down[1], -1))
    total = add(own(0, 0), shift(up[0], 1), shift(down[0], -1), meet(other, "xh", 1))
    x_grad_t = lax.ppermute(total, ALL, turn)
    grads_in = lax.all_to_all(grads, ("xl", "y"), 0, 0)

    q_turned = lax.ppermute(q_t, ALL, turn)
    x_low = lax.dot_general(
        q_turned, u_factor, (((0,), (1,)), ((), ())), preferred_element_type=F32
    )
    input_grad = add(x_grad_t.T, x_low)

    grads_sum = jnp.sum(grads_in.astype(F32), axis=0)
    blocks_grad = (
        grads_sum[:FEAT]
        .astype(BF16)
        .reshape(NB // 2, BS, 2, BS)
        .transpose(0, 2, 1, 3)
        .reshape(sparse_blocks.shape)
    )
    v_grad = (
        grads_sum[FEAT : FEAT + VROWS]
        .reshape(WIDTH // TOK, RS, TOK)
        .transpose(1, 0, 2)
        .reshape(RS, WIDTH)
    )
    u_own = grads_sum[FEAT + VROWS : FEAT + VROWS + UROWS]
    u_other = grads_sum[FEAT + VROWS + UROWS :]
    u_grad = (
        (u_own + meet(u_other, "core", 1))
        .reshape(FEAT // TOK, RS, TOK)
        .transpose(0, 2, 1)
        .reshape(FEAT, RS)
    )
    return hidden, input_grad, blocks_grad, u_grad, v_grad


def solution(mesh):
    fine = Mesh(mesh.devices.reshape(8, 2, 2, 4, 2), ALL)
    in_specs = (
        P(ROW, COL),
        P(COL, ROW),
        P(COL, ROW, None, None),
        P(COL, ROW, None),
        P(COL, None),
        P(None, ROW),
    )
    out_specs = (
        P(COL, ROW),
        P(ROW, COL),
        P(COL, ROW, None, None),
        P(COL, ROW),
        P(COL, ROW),
    )
    return jax.shard_map(
        on_device, mesh=fine, in_specs=in_specs, out_specs=out_specs, check_vma=False
    )
```

time: 856 us -> 215 us (0.25); the launches traced: 844 us -> 212 us
  waiting for transfers between devices: 707 us -> 31.5 us
  starting transfers between devices: 0.29 us -> 114 us
  matrix products: 69.7 us -> 0.51 us
  local copies, waits for them, and re-layouts: 50.6 us -> 19.1 us
  Pallas kernels: 0 us -> 27.1 us
    reduce_scatter x5 -> x0, waiting for transfers between devices: 562 us -> none  [the longest x1 203 us: on_device(): u_grad = lax.psum_scatter(u_part, 'row', scatter_dimension=1, tiled=True)]
    all_gather x2 -> x1, waiting for transfers between devices: 145 us -> 0.01 us  [on_device(): w_own = lax.all_gather(w_mine, ('xl', 'y'), axis=0)]
    ppermute x0 -> x45, starting transfers between devices: none -> 110 us  [the longest x28 49.4 us: shift(): return lax.ppermute(x, 'z', [(i, (i + by) % NZ) for i in range(NZ)])]
    dot_general x13 -> x2, matrix products: 69.7 us -> 0.51 us  [the longest x1 0.28 us: on_device(): lax.dot_general(u_factor, mine, (((0,), (0,)), ((), ())), preferred_eleme...]
    ppermute x0 -> x45, waiting for transfers between devices: none -> 31.5 us  [the longest x1 10.1 us: on_device(): x_grad_t = lax.ppermute(total, ALL, turn)]
    pallas_call x0 -> x5, Pallas kernels: none -> 27.1 us  [call(): pl.pallas_call(kernel, out_shape=out_shape, in_specs=[smem] * 2 + [anywhe...]
    convert_element_type x3 -> x0, local copies, waits for them, and re-layouts: 24.5 us -> none  [the longest x2 23.6 us: on_device(): sparse_part.astype(jnp.bfloat16)]
    all_gather x1 -> x0, local copies, waits for them, and re-layouts: 11.9 us -> none  [on_device(): dz_all = lax.all_gather(dz_local, 'col', axis=0, tiled=True)]
  transfers between devices with their start and end apart: 7 -> 47, of which waited for: 7 -> 12; matrix products, arithmetic and copies ran while one was open for 7% -> 4% of each run, Pallas kernels for 0% -> 6%
where the time goes in v1:
time: 215 us; the launch traced here: 212 us
  starting transfers between devices  114 us (53%)
  waiting for transfers between devices  31.5 us (15%)
  Pallas kernels  27.1 us (13%)
  local copies, waits for them, and re-layouts  19.1 us (9%)
  between operations  14.6 us (7%)
  other arithmetic  5.52 us (3%)
    ppermute x28, starting transfers between devices, shift(): return lax.ppermute(x, 'z', [(i, (i + by) % NZ) for i in range(NZ)])  49.4 us
    ppermute x13, starting transfers between devices, meet(): return lax.ppermute(x, axis, [(i, i ^ flip) for i in range(count)])  33.6 us
    pallas_call x5, Pallas kernels, call(): pl.pallas_call(kernel, out_shape=out_shape, in_specs=[smem] * 2 + [anywhe...  27.1 us
    unnamed x48, local copies, waits for them, and re-layouts  13.9 us
    ppermute x1, starting transfers between devices, on_device(): q_turned = lax.ppermute(q_t, ALL, turn)  10.2 us
    ppermute x1, waiting for transfers between devices, on_device(): x_grad_t = lax.ppermute(total, ALL, turn)  10.1 us
    ppermute x1, starting transfers between devices, on_device(): x_grad_t = lax.ppermute(total, ALL, turn)  9.59 us
    ppermute x28, waiting for transfers between devices, shift(): return lax.ppermute(x, 'z', [(i, (i + by) % NZ) for i in range(NZ)])  6.59 us
  transfers between devices with their start and end apart: 47, of which 12 were waited for; matrix products, arithmetic and copies ran while one was open for 4% of the time, Pallas kernels for 6%

profile of v1, /device:TPU:1, one launch (start us, length us, event | category | flops | bytes accessed | tf_op | source)
XLA Modules:
  0.0 212.2 jit_solution(5926969183445952557)
XLA Ops:
  7.9 1.0 copy.23
  9.0 1.3 reshape.77
  11.7 3.3 %collective-permute-start.1 = (f32[256,128]{1,0:T(8,128)S(1)}, f32[256,128]{1,0:T(8,128)S(1)}, u32[]{:S(2)}, u32[]{:S(2)}) collective-permute-start(f32[256,128]{1,0:T(8,128)S(1)} %convolution_bitcast_fusion), channel_id=1, source_target_pairs={{0,1},{1,0},{2,3},{3,2},{4,5},{5,4},{6,7},{7,6},{8,9},{9,8},{10,11... | collective-permute-start | bytes 393224 | tf_op jit(solution)/shard_map/ppermute | solution.py:215
  15.0 2.8 %collective-permute-start = (bf16[512,128]{1,0:T(8,128)(2,1)S(1)}, bf16[512,128]{1,0:T(8,128)(2,1)S(1)}, u32[]{:S(2)}, u32[]{:S(2)}) collective-permute-start(bf16[512,128]{1,0:T(8,128)(2,1)S(1)} %bitcast.58), channel_id=1, source_target_pairs={{0,0},{1,16},{2,32},{3,48},{4,64},{5,80},{6,96},{7,112},{8,128},{9... | collective-permute-start | bytes 393224 | tf_op jit(solution)/shard_map/ppermute | solution.py:229
  17.9 6.1 %collective-permute-done.refs_0_ = bf16[512,128]{1,0:T(8,128)(2,1)S(1)} collective-permute-done((bf16[512,128]{1,0:T(8,128)(2,1)S(1)}, bf16[512,128]{1,0:T(8,128)(2,1)S(1)}, u32[]{:S(2)}, u32[]{:S(2)}) %collective-permute-start) | collective-permute-done | bytes 131104 | tf_op jit(solution)/shard_map/ppermute | solution.py:229
  24.0 5.8 %collective-permute-start.2 = (f32[256,128]{1,0:T(8,128)S(1)}, f32[256,128]{1,0:T(8,128)S(1)}, u32[]{:S(2)}, u32[]{:S(2)}) collective-permute-start(f32[256,128]{1,0:T(8,128)S(1)} %add.83), channel_id=1, source_target_pairs={{0,8},{8,0},{1,9},{9,1},{2,10},{10,2},{3,11},{11,3},{4,12},{12,4},... | collective-permute-start | bytes 393224 | tf_op jit(solution)/shard_map/ppermute | solution.py:215
  29.8 4.8 %collective-permute-start.8 = (bf16[512,128]{1,0:T(8,128)(2,1)S(1)}, bf16[512,128]{1,0:T(8,128)(2,1)S(1)}, u32[]{:S(2)}, u32[]{:S(2)}) collective-permute-start(bf16[512,128]{1,0:T(8,128)(2,1)S(1)} %collective-permute-done.refs_0_), channel_id=1, source_target_pairs={{0,32},{32,64},{64,96},{96,128},{128,160},{160,192},{192,224},{224... | collective-permute-start | bytes 393224 | tf_op jit(solution)/shard_map/ppermute | solution.py:202
  34.6 6.7 %collective-permute-start.5 = (bf16[512,128]{1,0:T(8,128)(2,1)S(1)}, bf16[512,128]{1,0:T(8,128)(2,1)S(1)}, u32[]{:S(2)}, u32[]{:S(2)}) collective-permute-start(bf16[512,128]{1,0:T(8,128)(2,1)S(1)} %collective-permute-done.refs_0_), channel_id=1, source_target_pairs={{0,224},{32,0},{64,32},{96,64},{128,96},{160,128},{192,160},{224,1... | collective-permute-start | bytes 393224 | tf_op jit(solution)/shard_map/ppermute | solution.py:202
  41.4 8.2 %collective-permute-start.12 = (bf16[512,128]{1,0:T(8,128)(2,1)S(1)}, bf16[512,128]{1,0:T(8,128)(2,1)S(1)}, u32[]{:S(2)}, u32[]{:S(2)}) collective-permute-start(bf16[512,128]{1,0:T(8,128)(2,1)S(1)} %collective-permute-done.11.refs_1_), channel_id=1, source_target_pairs={{0,224},{32,0},{64,32},{96,64},{128,96},{160,128},{192,160},{224,1... | collective-permute-start | bytes 393224 | tf_op jit(solution)/shard_map/ppermute | solution.py:202
  49.8 2.7 %collective-permute-start.6 = (bf16[512,128]{1,0:T(8,128)(2,1)S(1)}, bf16[512,128]{1,0:T(8,128)(2,1)S(1)}, u32[]{:S(2)}, u32[]{:S(2)}) collective-permute-start(bf16[512,128]{1,0:T(8,128)(2,1)S(1)} %collective-permute-done.5.refs_2_), channel_id=1, source_target_pairs={{0,224},{32,0},{64,32},{96,64},{128,96},{160,128},{192,160},{224,1... | collective-permute-start | bytes 393224 | tf_op jit(solution)/shard_map/ppermute | solution.py:202
  52.4 1.0 collective-permute-done.15.refs_15_
  53.4 2.7 %collective-permute-start.13 = (bf16[512,128]{1,0:T(8,128)(2,1)S(1)}, bf16[512,128]{1,0:T(8,128)(2,1)S(1)}, u32[]{:S(2)}, u32[]{:S(2)}) collective-permute-start(bf16[512,128]{1,0:T(8,128)(2,1)S(1)} %collective-permute-done.12.refs_3_), channel_id=1, source_target_pairs={{0,224},{32,0},{64,32},{96,64},{128,96},{160,128},{192,160},{224,1... | collective-permute-start | bytes 393224 | tf_op jit(solution)/shard_map/ppermute | solution.py:202
  56.4 2.6 %collective-permute-start.7 = (bf16[512,128]{1,0:T(8,128)(2,1)S(1)}, bf16[512,128]{1,0:T(8,128)(2,1)S(1)}, u32[]{:S(2)}, u32[]{:S(2)}) collective-permute-start(bf16[512,128]{1,0:T(8,128)(2,1)S(1)} %collective-permute-done.6.refs_4_), channel_id=1, source_target_pairs={{0,224},{32,0},{64,32},{96,64},{128,96},{160,128},{192,160},{224,1... | collective-permute-start | bytes 393224 | tf_op jit(solution)/shard_map/ppermute | solution.py:202
  60.0 2.4 %collective-permute-start.14 = (bf16[512,128]{1,0:T(8,128)(2,1)S(1)}, bf16[512,128]{1,0:T(8,128)(2,1)}, u32[]{:S(2)}, u32[]{:S(2)}) collective-permute-start(bf16[512,128]{1,0:T(8,128)(2,1)S(1)} %collective-permute-done.13.refs_5_), channel_id=1, source_target_pairs={{0,224},{32,0},{64,32},{96,64},{128,96},{160,128},{192,160},{224,1... | collective-permute-start | bytes 393224 | tf_op jit(solution)/shard_map/ppermute | solution.py:202
  63.9 1.7 collective-permute-done.17.refs_11_
  66.3 2.9 %collective-permute-start.18 = (bf16[8,528,128]{2,1,0:T(8,128)(2,1)}, bf16[8,528,128]{2,1,0:T(8,128)(2,1)S(1)}, u32[]{:S(2)}, u32[]{:S(2)}) collective-permute-start(bf16[8,528,128]{2,1,0:T(8,128)(2,1)} %bitcast.48), channel_id=1, source_target_pairs={{0,1},{1,0},{2,3},{3,2},{4,5},{5,4},{6,7},{7,6},{8,9},{9,8},{10,11... | collective-permute-start | bytes 3244040 | tf_op jit(solution)/shard_map/ppermute | solution.py:215
  69.1 2.2 %collective-permute-start.19 = (bf16[512,128]{1,0:T(8,128)(2,1)}, bf16[512,128]{1,0:T(8,128)(2,1)S(1)}, u32[]{:S(2)}, u32[]{:S(2)}) collective-permute-start(bf16[512,128]{1,0:T(8,128)(2,1)} %copy-done.16), channel_id=1, source_target_pairs={{0,32},{32,64},{64,96},{96,128},{128,160},{160,192},{192,224},{224... | collective-permute-start | bytes 393224 | tf_op jit(solution)/shard_map/ppermute | solution.py:202
  73.0 4.7 %collective-permute-start.21 = (bf16[256,128]{1,0:T(8,128)(2,1)S(1)}, bf16[256,128]{1,0:T(8,128)(2,1)S(1)}, u32[]{:S(2)}, u32[]{:S(2)}) collective-permute-start(bf16[256,128]{1,0:T(8,128)(2,1)S(1)} %add_convert_fusion.13), channel_id=1, source_target_pairs={{0,0},{1,16},{2,32},{3,48},{4,64},{5,80},{6,96},{7,112},{8,128},{9... | collective-permute-start | bytes 196616 | tf_op jit(solution)/shard_map/ppermute | solution.py:242
  77.8 2.3 %collective-permute-done.21.refs_18_ = bf16[256,128]{1,0:T(8,128)(2,1)S(1)} collective-permute-done((bf16[256,128]{1,0:T(8,128)(2,1)S(1)}, bf16[256,128]{1,0:T(8,128)(2,1)S(1)}, u32[]{:S(2)}, u32[]{:S(2)}) %collective-permute-start.21) | collective-permute-done | bytes 65568 | tf_op jit(solution)/shard_map/ppermute | solution.py:242
  80.1 1.2 copy-done.1
  89.5 10.6 %shard_map.101 = (bf16[128,2048]{1,0:T(8,128)(2,1)}, bf16[2048,128]{1,0:T(8,128)(2,1)S(1)}, f32[256,128]{1,0:T(8,128)S(1)}, bf16[16,512,128]{2,1,0:T(8,128)(2,1)S(1)}, bf16[16,528,128]{2,1,0:T(8,128)(2,1)S(1)}) custom-call(s32[4]{0:T(128)S(1)} %pad_add_fusion.place, s32[16,16]{1,0:T(8,128)S(1)} %maximum_convert_fusion.index, ...), custom_call_target="tpu_custom_call" | custom-call | flops 800000000 | bytes 10485760 | tf_op jit(solution)/shard_map/pallas_call | solution.py:180
  100.1 3.7 %shard_map.102 = (bf16[512,128]{1,0:T(8,128)(2,1)S(1)}, bf16[512,128]{1,0:T(8,128)(2,1)S(1)}, bf16[512,128]{1,0:T(8,128)(2,1)S(1)}, bf16[512,128]{1,0:T(8,128)(2...) custom-call(s32[4]{0:T(128)S(1)} %pad_add_fusion.place, ...), custom_call_target="tpu_custom_call" | custom-call | flops 200000000 | bytes 5242880 | tf_op jit(solution)/shard_map/pallas_call | solution.py:180
  103.8 6.6 %collective-permute-start.22 = (bf16[256,128]{1,0:T(8,128)(2,1)S(1)}, bf16[256,128]{1,0:T(8,128)(2,1)S(1)}, u32[]{:S(2)}, u32[]{:S(2)}) collective-permute-start(bf16[256,128]{1,0:T(8,128)(2,1)S(1)} %convert_element_type.180), channel_id=1, source_target_pairs={{0,32},{32,0},{64,96},{96,64},{128,160},{160,128},{192,224},{224,1... | collective-permute-start | bytes 196616 | tf_op jit(solution)/shard_map/ppermute | solution.py:215
  110.4 1.7 collective-permute-done.22
  112.0 6.5 %collective-permute-start.23 = (bf16[256,128]{1,0:T(8,128)(2,1)S(1)}, bf16[256,128]{1,0:T(8,128)(2,1)S(1)}, u32[]{:S(2)}, u32[]{:S(2)}) collective-permute-start(bf16[256,128]{1,0:T(8,128)(2,1)S(1)} %fusion.3), channel_id=1, source_target_pairs={{0,64},{32,96},{64,0},{96,32},{128,192},{160,224},{192,128},{224,1... | collective-permute-start | bytes 196616 | tf_op jit(solution)/shard_map/ppermute | solution.py:215
  118.5 2.4 %shard_map.105 = (bf16[512,128]{1,0:T(8,128)(2,1)S(1)}, bf16[512,128]{1,0:T(8,128)(2,1)S(1)}, bf16[512,128]{1,0:T(8,128)(2,1)S(1)}, bf16[512,128]{1,0:T(8,128)(2...) custom-call(s32[4]{0:T(128)S(1)} %pad_add_fusion.place, s32[16,16]{1,0:T(8,128)S(1)} %maximum_convert_fusion.index, ...), custom_call_target="tpu_custom_call" | custom-call | flops 120000000 | bytes 3145728 | tf_op jit(solution)/shard_map/pallas_call | solution.py:180
  121.4 2.3 %collective-permute-start.31 = (bf16[512,128]{1,0:T(8,128)(2,1)S(1)}, bf16[512,128]{1,0:T(8,128)(2,1)S(1)}, u32[]{:S(2)}, u32[]{:S(2)}) collective-permute-start(bf16[512,128]{1,0:T(8,128)(2,1)S(1)} %get-tuple-element.67), channel_id=1, source_target_pairs={{0,224},{32,0},{64,32},{96,64},{128,96},{160,128},{192,160},{224,1... | collective-permute-start | bytes 393224 | tf_op jit(solution)/shard_map/ppermute | solution.py:202
  123.7 2.7 %collective-permute-start.37 = (bf16[512,128]{1,0:T(8,128)(2,1)S(1)}, bf16[512,128]{1,0:T(8,128)(2,1)S(1)}, u32[]{:S(2)}, u32[]{:S(2)}) collective-permute-start(bf16[512,128]{1,0:T(8,128)(2,1)S(1)} %get-tuple-element.75), channel_id=1, source_target_pairs={{0,224},{32,0},{64,32},{96,64},{128,96},{160,128},{192,160},{224,1... | collective-permute-start | bytes 393224 | tf_op jit(solution)/shard_map/ppermute | solution.py:202
  126.4 3.8 %shard_map.103 = bf16[8,768,128]{2,1,0:T(8,128)(2,1)S(1)} custom-call(s32[4]{0:T(128)S(1)} %pad_add_fusion.place, s32[16,16]{1,0:T(8,128)S(1)} %maximum_convert_fusion.index, bf16[16,512,128]{2,1,0:T(8,128)(2,1)S(1)} %get-tuple-element.58.x, bf16[2048,128]{1,0:T(8,128)(2,1)S(1)} %get-tuple-element.55.dz_t, bf16[16,16,128]{2,1,0:T(8,128)(2,1)S(1)} %bitcast.51), custom_call_target="tpu_custom_call" | custom-call | flops 200000000 | bytes 4194304 | tf_op jit(solution)/shard_map/pallas_call | solution.py:180
  130.2 2.2 %collective-permute-start.26 = (bf16[8,768,128]{2,1,0:T(8,128)(2,1)S(1)}, bf16[8,768,128]{2,1,0:T(8,128)(2,1)S(1)}, u32[]{:S(2)}, u32[]{:S(2)}) collective-permute-start(bf16[8,768,128]{2,1,0:T(8,128)(2,1)S(1)} %shard_map.103), channel_id=1, source_target_pairs={{0,1},{1,0},{2,3},{3,2},{4,5},{5,4},{6,7},{7,6},{8,9},{9,8},{10,11... | collective-permute-start | bytes 4718600 | tf_op jit(solution)/shard_map/ppermute | solution.py:215
  133.4 2.7 %collective-permute-start.32 = (bf16[512,128]{1,0:T(8,128)(2,1)S(1)}, bf16[512,128]{1,0:T(8,128)(2,1)S(1)}, u32[]{:S(2)}, u32[]{:S(2)}) collective-permute-start(bf16[512,128]{1,0:T(8,128)(2,1)S(1)} %add_convert_fusion.8), channel_id=1, source_target_pairs={{0,224},{32,0},{64,32},{96,64},{128,96},{160,128},{192,160},{224,1... | collective-permute-start | bytes 393224 | tf_op jit(solution)/shard_map/ppermute | solution.py:202
  136.8 3.3 %collective-permute-done.24 = bf16[256,128]{1,0:T(8,128)(2,1)S(1)} collective-permute-done((bf16[256,128]{1,0:T(8,128)(2,1)S(1)}, bf16[256,128]{1,0:T(8,128)(2,1)S(1)}, u32[]{:S(2)}, u32[]{:S(2)}) %collective-permute-start.24) | collective-permute-done | bytes 65568 | tf_op jit(solution)/shard_map/ppermute | solution.py:215
  140.2 2.9 %collective-permute-start.25 = (bf16[256,128]{1,0:T(8,128)(2,1)S(1)}, bf16[256,128]{1,0:T(8,128)(2,1)S(1)}, u32[]{:S(2)}, u32[]{:S(2)}) collective-permute-start(bf16[256,128]{1,0:T(8,128)(2,1)S(1)} %fusion.4), channel_id=1, source_target_pairs={{0,16},{16,0},{1,17},{17,1},{2,18},{18,2},{3,19},{19,3},{4,20},{20... | collective-permute-start | bytes 196616 | tf_op jit(solution)/shard_map/ppermute | solution.py:215
  143.7 1.2 collective-permute-done.25
  144.9 2.7 %collective-permute-start.38 = (bf16[512,128]{1,0:T(8,128)(2,1)}, bf16[512,128]{1,0:T(8,128)(2,1)}, u32[]{:S(2)}, u32[]{:S(2)}) collective-permute-start(bf16[512,128]{1,0:T(8,128)(2,1)} %add_convert_fusion.4), channel_id=1, source_target_pairs={{0,224},{32,0},{64,32},{96,64},{128,96},{160,128},{192,160},{224,1... | collective-permute-start | bytes 393224 | tf_op jit(solution)/shard_map/ppermute | solution.py:202
  147.7 6.6 %shard_map.104 = bf16[8,896,128]{2,1,0:T(8,128)(2,1)} custom-call(s32[4]{0:T(128)S(1)} %pad_add_fusion.place, s32[16,16]{1,0:T(8,128)S(1)} %maximum_convert_fusion.index, bf16[16,512,128]{2,1,0:T(8,128)(2,1)S(1)} %get-tuple-element.58.x, bf16[2048,128]{1,0:T(8,128)(2,1)S(1)} %get-tuple-element.55.dz_t, bf16[16,16,128]{2,1,0:T(8,128)(2,1)S(1)} %bitcast.52, ...), custom_call_target="tpu_custom_call" | custom-call | flops 300000000 | bytes 6291456 | tf_op jit(solution)/shard_map/pallas_call | solution.py:180
  154.3 3.6 %all-to-all-start = ((bf16[8,896,128]{2,1,0:T(8,128)(2,1)}), bf16[8,896,128]{2,1,0:T(8,128)(2,1)S(1)}, u32[]{:S(2)}, u32[]{:S(2)}) async-start(bf16[8,896,128]{2,1,0:T(8,128)(2,1)} %shard_map.104), calls=%async_computation | async-start | bytes 3670016 | tf_op jit(solution)/shard_map/all_to_all | solution.py:308
  157.9 0.9 add_convert_fusion.3
  158.9 0.9 add_convert_fusion.5
  159.9 1.5 collective-permute-start.36
  161.4 1.3 collective-permute-done.39
  162.8 1.3 collective-permute-start.40
  164.2 1.4 collective-permute-start.29
  165.6 2.3 %collective-permute-done.40 = bf16[512,128]{1,0:T(8,128)(2,1)S(1)} collective-permute-done((bf16[512,128]{1,0:T(8,128)(2,1)S(1)}, bf16[512,128]{1,0:T(8,128)(2,1)S(1)}, u32[]{:S(2)}, u32[]{:S(2)}) %collective-permute-start.40) | collective-permute-done | bytes 131104 | tf_op jit(solution)/shard_map/ppermute | solution.py:202
  168.0 2.7 %collective-permute-start.41 = (bf16[512,128]{1,0:T(8,128)(2,1)S(1)}, bf16[512,128]{1,0:T(8,128)(2,1)S(1)}, u32[]{:S(2)}, u32[]{:S(2)}) collective-permute-start(bf16[512,128]{1,0:T(8,128)(2,1)S(1)} %add_convert_fusion.1), channel_id=1, source_target_pairs={{0,16},{16,0},{1,17},{17,1},{2,18},{18,2},{3,19},{19,3},{4,20},{20... | collective-permute-start | bytes 393224 | tf_op jit(solution)/shard_map/ppermute | solution.py:215
  170.9 10.2 %collective-permute-start.43 = (bf16[256,128]{1,0:T(8,128)(2,1)S(1)}, bf16[256,128]{1,0:T(8,128)(2,1)S(1)}, u32[]{:S(2)}, u32[]{:S(2)}) collective-permute-start(bf16[256,128]{1,0:T(8,128)(2,1)S(1)} %add_convert_fusion.12), channel_id=1, source_target_pairs={{0,0},{1,16},{2,32},{3,48},{4,64},{5,80},{6,96},{7,112},{8,128},{9... | collective-permute-start | bytes 196616 | tf_op jit(solution)/shard_map/ppermute | solution.py:310
  181.4 9.6 %collective-permute-start.42 = (bf16[512,128]{1,0:T(8,128)(2,1)S(1)}, bf16[512,128]{1,0:T(8,128)(2,1)S(1)}, u32[]{:S(2)}, u32[]{:S(2)}) collective-permute-start(bf16[512,128]{1,0:T(8,128)(2,1)S(1)} %add_convert_fusion), channel_id=1, source_target_pairs={{0,0},{1,16},{2,32},{3,48},{4,64},{5,80},{6,96},{7,112},{8,128},{9... | collective-permute-start | bytes 393224 | tf_op jit(solution)/shard_map/ppermute | solution.py:307
  191.4 10.1 %collective-permute-done.42 = bf16[512,128]{1,0:T(8,128)(2,1)S(1)} collective-permute-done((bf16[512,128]{1,0:T(8,128)(2,1)S(1)}, bf16[512,128]{1,0:T(8,128)(2,1)S(1)}, u32[]{:S(2)}, u32[]{:S(2)}) %collective-permute-start.42) | collective-permute-done | bytes 131104 | tf_op jit(solution)/shard_map/ppermute | solution.py:307
  (143 shorter events, 23.5 us)
Async XLA Ops:
  7.2 59.1 %all-gather.3.cloned.1.call-start = ((), (), s32[]{:S(2)}) async-start(), calls=%async_computation.1 | async-start | bytes 1216512 | tf_op jit(solution)/shard_map/all_gather | solution.py:227
  8.9 71.1 %copy-start.2 = (bf16[256,2048]{1,0:T(8,128)(2,1)S(1)}, bf16[256,2048]{1,0:T(8,128)(2,1)}, u32[]{:S(2)}) copy-start(bf16[256,2048]{1,0:T(8,128)(2,1)} %refs_19_.1) | copy-start | bytes 3145732
  11.7 6.2 %collective-permute-start.1 = (f32[256,128]{1,0:T(8,128)S(1)}, f32[256,128]{1,0:T(8,128)S(1)}, u32[]{:S(2)}, u32[]{:S(2)}) collective-permute-start(f32[256,128]{1,0:T(8,128)S(1)} %convolution_bitcast_fusion), channel_id=1, source_target_pairs={{0,1},{1,0},{2,3},{3,2},{4,5},{5,4},{6,7},{7,6},{8,9},{9,8},{10,11... | collective-permute-start | bytes 393224 | tf_op jit(solution)/shard_map/ppermute | solution.py:215
  15.0 9.0 %collective-permute-start = (bf16[512,128]{1,0:T(8,128)(2,1)S(1)}, bf16[512,128]{1,0:T(8,128)(2,1)S(1)}, u32[]{:S(2)}, u32[]{:S(2)}) collective-permute-start(bf16[512,128]{1,0:T(8,128)(2,1)S(1)} %bitcast.58), channel_id=1, source_target_pairs={{0,0},{1,16},{2,32},{3,48},{4,64},{5,80},{6,96},{7,112},{8,128},{9... | collective-permute-start | bytes 393224 | tf_op jit(solution)/shard_map/ppermute | solution.py:229
  24.0 17.3 %collective-permute-start.11 = (bf16[512,128]{1,0:T(8,128)(2,1)S(1)}, bf16[512,128]{1,0:T(8,128)(2,1)S(1)}, u32[]{:S(2)}, u32[]{:S(2)}) collective-permute-start(bf16[512,128]{1,0:T(8,128)(2,1)S(1)} %collective-permute-done.refs_0_), channel_id=1, source_target_pairs={{0,16},{16,0},{1,17},{17,1},{2,18},{18,2},{3,19},{19,3},{4,20},{20... | collective-permute-start | bytes 393224 | tf_op jit(solution)/shard_map/ppermute | solution.py:215
  24.0 25.5 %collective-permute-start.2 = (f32[256,128]{1,0:T(8,128)S(1)}, f32[256,128]{1,0:T(8,128)S(1)}, u32[]{:S(2)}, u32[]{:S(2)}) collective-permute-start(f32[256,128]{1,0:T(8,128)S(1)} %add.83), channel_id=1, source_target_pairs={{0,8},{8,0},{1,9},{9,1},{2,10},{10,2},{3,11},{11,3},{4,12},{12,4},... | collective-permute-start | bytes 393224 | tf_op jit(solution)/shard_map/ppermute | solution.py:215
  29.8 19.9 %collective-permute-start.8 = (bf16[512,128]{1,0:T(8,128)(2,1)S(1)}, bf16[512,128]{1,0:T(8,128)(2,1)S(1)}, u32[]{:S(2)}, u32[]{:S(2)}) collective-permute-start(bf16[512,128]{1,0:T(8,128)(2,1)S(1)} %collective-permute-done.refs_0_), channel_id=1, source_target_pairs={{0,32},{32,64},{64,96},{96,128},{128,160},{160,192},{192,224},{224... | collective-permute-start | bytes 393224 | tf_op jit(solution)/shard_map/ppermute | solution.py:202
  34.6 15.2 %collective-permute-start.5 = (bf16[512,128]{1,0:T(8,128)(2,1)S(1)}, bf16[512,128]{1,0:T(8,128)(2,1)S(1)}, u32[]{:S(2)}, u32[]{:S(2)}) collective-permute-start(bf16[512,128]{1,0:T(8,128)(2,1)S(1)} %collective-permute-done.refs_0_), channel_id=1, source_target_pairs={{0,224},{32,0},{64,32},{96,64},{128,96},{160,128},{192,160},{224,1... | collective-permute-start | bytes 393224 | tf_op jit(solution)/shard_map/ppermute | solution.py:202
  41.3 12.1 %collective-permute-start.15 = (bf16[512,128]{1,0:T(8,128)(2,1)S(1)}, bf16[512,128]{1,0:T(8,128)(2,1)S(1)}, u32[]{:S(2)}, u32[]{:S(2)}) collective-permute-start(bf16[512,128]{1,0:T(8,128)(2,1)S(1)} %collective-permute-done.11.refs_1_), channel_id=1, source_target_pairs={{0,32},{32,64},{64,96},{96,128},{128,160},{160,192},{192,224},{224... | collective-permute-start | bytes 393224 | tf_op jit(solution)/shard_map/ppermute | solution.py:202
  41.4 12.1 %collective-permute-start.12 = (bf16[512,128]{1,0:T(8,128)(2,1)S(1)}, bf16[512,128]{1,0:T(8,128)(2,1)S(1)}, u32[]{:S(2)}, u32[]{:S(2)}) collective-permute-start(bf16[512,128]{1,0:T(8,128)(2,1)S(1)} %collective-permute-done.11.refs_1_), channel_id=1, source_target_pairs={{0,224},{32,0},{64,32},{96,64},{128,96},{160,128},{192,160},{224,1... | collective-permute-start | bytes 393224 | tf_op jit(solution)/shard_map/ppermute | solution.py:202
  49.6 6.5 %collective-permute-start.3 = (f32[256,128]{1,0:T(8,128)S(1)}, f32[256,128]{1,0:T(8,128)S(1)}, u32[]{:S(2)}, u32[]{:S(2)}) collective-permute-start(f32[256,128]{1,0:T(8,128)S(1)} %add.84), channel_id=1, source_target_pairs={{0,2},{2,0},{4,6},{6,4},{1,3},{3,1},{5,7},{7,5},{8,10},{10,8},{12,... | collective-permute-start | bytes 393224 | tf_op jit(solution)/shard_map/ppermute | solution.py:215
  49.7 6.6 %collective-permute-start.9 = (bf16[512,128]{1,0:T(8,128)(2,1)S(1)}, bf16[512,128]{1,0:T(8,128)(2,1)S(1)}, u32[]{:S(2)}, u32[]{:S(2)}) collective-permute-start(bf16[512,128]{1,0:T(8,128)(2,1)S(1)} %collective-permute-done.8.refs_14_), channel_id=1, source_target_pairs={{0,32},{32,64},{64,96},{96,128},{128,160},{160,192},{192,224},{224... | collective-permute-start | bytes 393224 | tf_op jit(solution)/shard_map/ppermute | solution.py:202
  49.8 6.6 %collective-permute-start.6 = (bf16[512,128]{1,0:T(8,128)(2,1)S(1)}, bf16[512,128]{1,0:T(8,128)(2,1)S(1)}, u32[]{:S(2)}, u32[]{:S(2)}) collective-permute-start(bf16[512,128]{1,0:T(8,128)(2,1)S(1)} %collective-permute-done.5.refs_2_), channel_id=1, source_target_pairs={{0,224},{32,0},{64,32},{96,64},{128,96},{160,128},{192,160},{224,1... | collective-permute-start | bytes 393224 | tf_op jit(solution)/shard_map/ppermute | solution.py:202
  53.4 5.7 %collective-permute-start.16 = (bf16[512,128]{1,0:T(8,128)(2,1)S(1)}, bf16[512,128]{1,0:T(8,128)(2,1)S(1)}, u32[]{:S(2)}, u32[]{:S(2)}) collective-permute-start(bf16[512,128]{1,0:T(8,128)(2,1)S(1)} %collective-permute-done.15.refs_15_), channel_id=1, source_target_pairs={{0,32},{32,64},{64,96},{96,128},{128,160},{160,192},{192,224},{224... | collective-permute-start | bytes 393224 | tf_op jit(solution)/shard_map/ppermute | solution.py:202
  53.4 6.6 %collective-permute-start.13 = (bf16[512,128]{1,0:T(8,128)(2,1)S(1)}, bf16[512,128]{1,0:T(8,128)(2,1)S(1)}, u32[]{:S(2)}, u32[]{:S(2)}) collective-permute-start(bf16[512,128]{1,0:T(8,128)(2,1)S(1)} %collective-permute-done.12.refs_3_), channel_id=1, source_target_pairs={{0,224},{32,0},{64,32},{96,64},{128,96},{160,128},{192,160},{224,1... | collective-permute-start | bytes 393224 | tf_op jit(solution)/shard_map/ppermute | solution.py:202
  56.1 7.0 %collective-permute-start.4 = (f32[256,128]{1,0:T(8,128)S(1)}, f32[256,128]{1,0:T(8,128)S(1)}, u32[]{:S(2)}, u32[]{:S(2)}) collective-permute-start(f32[256,128]{1,0:T(8,128)S(1)} %add.85), channel_id=1, source_target_pairs={{0,4},{2,6},{4,0},{6,2},{1,5},{3,7},{5,1},{7,3},{8,12},{10,14},{12... | collective-permute-start | bytes 393224 | tf_op jit(solution)/shard_map/ppermute | solution.py:215
  56.3 6.9 %collective-permute-start.10 = (bf16[512,128]{1,0:T(8,128)(2,1)S(1)}, bf16[512,128]{1,0:T(8,128)(2,1)S(1)}, u32[]{:S(2)}, u32[]{:S(2)}) collective-permute-start(bf16[512,128]{1,0:T(8,128)(2,1)S(1)} %collective-permute-done.9.refs_12_), channel_id=1, source_target_pairs={{0,32},{32,64},{64,96},{96,128},{128,160},{160,192},{192,224},{224... | collective-permute-start | bytes 393224 | tf_op jit(solution)/shard_map/ppermute | solution.py:202
  56.4 6.7 %collective-permute-start.7 = (bf16[512,128]{1,0:T(8,128)(2,1)S(1)}, bf16[512,128]{1,0:T(8,128)(2,1)S(1)}, u32[]{:S(2)}, u32[]{:S(2)}) collective-permute-start(bf16[512,128]{1,0:T(8,128)(2,1)S(1)} %collective-permute-done.6.refs_4_), channel_id=1, source_target_pairs={{0,224},{32,0},{64,32},{96,64},{128,96},{160,128},{192,160},{224,1... | collective-permute-start | bytes 393224 | tf_op jit(solution)/shard_map/ppermute | solution.py:202
  59.1 6.5 %collective-permute-start.17 = (bf16[512,128]{1,0:T(8,128)(2,1)S(1)}, bf16[512,128]{1,0:T(8,128)(2,1)S(1)}, u32[]{:S(2)}, u32[]{:S(2)}) collective-permute-start(bf16[512,128]{1,0:T(8,128)(2,1)S(1)} %collective-permute-done.16.refs_13_), channel_id=1, source_target_pairs={{0,32},{32,64},{64,96},{96,128},{128,160},{160,192},{192,224},{224... | collective-permute-start | bytes 393224 | tf_op jit(solution)/shard_map/ppermute | solution.py:202
  60.0 6.2 %collective-permute-start.14 = (bf16[512,128]{1,0:T(8,128)(2,1)S(1)}, bf16[512,128]{1,0:T(8,128)(2,1)}, u32[]{:S(2)}, u32[]{:S(2)}) collective-permute-start(bf16[512,128]{1,0:T(8,128)(2,1)S(1)} %collective-permute-done.13.refs_5_), channel_id=1, source_target_pairs={{0,224},{32,0},{64,32},{96,64},{128,96},{160,128},{192,160},{224,1... | collective-permute-start | bytes 393224 | tf_op jit(solution)/shard_map/ppermute | solution.py:202
  66.3 11.4 %collective-permute-start.18 = (bf16[8,528,128]{2,1,0:T(8,128)(2,1)}, bf16[8,528,128]{2,1,0:T(8,128)(2,1)S(1)}, u32[]{:S(2)}, u32[]{:S(2)}) collective-permute-start(bf16[8,528,128]{2,1,0:T(8,128)(2,1)} %bitcast.48), channel_id=1, source_target_pairs={{0,1},{1,0},{2,3},{3,2},{4,5},{5,4},{6,7},{7,6},{8,9},{9,8},{10,11... | collective-permute-start | bytes 3244040 | tf_op jit(solution)/shard_map/ppermute | solution.py:215
  69.1 8.6 %collective-permute-start.19 = (bf16[512,128]{1,0:T(8,128)(2,1)}, bf16[512,128]{1,0:T(8,128)(2,1)S(1)}, u32[]{:S(2)}, u32[]{:S(2)}) collective-permute-start(bf16[512,128]{1,0:T(8,128)(2,1)} %copy-done.16), channel_id=1, source_target_pairs={{0,32},{32,64},{64,96},{96,128},{128,160},{160,192},{192,224},{224... | collective-permute-start | bytes 393224 | tf_op jit(solution)/shard_map/ppermute | solution.py:202
  71.3 6.5 %collective-permute-start.20 = (bf16[512,128]{1,0:T(8,128)(2,1)}, bf16[512,128]{1,0:T(8,128)(2,1)S(1)}, u32[]{:S(2)}, u32[]{:S(2)}) collective-permute-start(bf16[512,128]{1,0:T(8,128)(2,1)} %collective-permute-done.14.refs_7_), channel_id=1, source_target_pairs={{0,224},{32,0},{64,32},{96,64},{128,96},{160,128},{192,160},{224,1... | collective-permute-start | bytes 393224 | tf_op jit(solution)/shard_map/ppermute | solution.py:202
  73.0 7.1 %collective-permute-start.21 = (bf16[256,128]{1,0:T(8,128)(2,1)S(1)}, bf16[256,128]{1,0:T(8,128)(2,1)S(1)}, u32[]{:S(2)}, u32[]{:S(2)}) collective-permute-start(bf16[256,128]{1,0:T(8,128)(2,1)S(1)} %add_convert_fusion.13), channel_id=1, source_target_pairs={{0,0},{1,16},{2,32},{3,48},{4,64},{5,80},{6,96},{7,112},{8,128},{9... | collective-permute-start | bytes 196616 | tf_op jit(solution)/shard_map/ppermute | solution.py:242
  103.8 8.3 %collective-permute-start.22 = (bf16[256,128]{1,0:T(8,128)(2,1)S(1)}, bf16[256,128]{1,0:T(8,128)(2,1)S(1)}, u32[]{:S(2)}, u32[]{:S(2)}) collective-permute-start(bf16[256,128]{1,0:T(8,128)(2,1)S(1)} %convert_element_type.180), channel_id=1, source_target_pairs={{0,32},{32,0},{64,96},{96,64},{128,160},{160,128},{192,224},{224,1... | collective-permute-start | bytes 196616 | tf_op jit(solution)/shard_map/ppermute | solution.py:215
  112.0 18.1 %collective-permute-start.23 = (bf16[256,128]{1,0:T(8,128)(2,1)S(1)}, bf16[256,128]{1,0:T(8,128)(2,1)S(1)}, u32[]{:S(2)}, u32[]{:S(2)}) collective-permute-start(bf16[256,128]{1,0:T(8,128)(2,1)S(1)} %fusion.3), channel_id=1, source_target_pairs={{0,64},{32,96},{64,0},{96,32},{128,192},{160,224},{192,128},{224,1... | collective-permute-start | bytes 196616 | tf_op jit(solution)/shard_map/ppermute | solution.py:215
  121.0 11.4 %collective-permute-start.27 = (bf16[512,128]{1,0:T(8,128)(2,1)S(1)}, bf16[512,128]{1,0:T(8,128)(2,1)S(1)}, u32[]{:S(2)}, u32[]{:S(2)}) collective-permute-start(bf16[512,128]{1,0:T(8,128)(2,1)S(1)} %get-tuple-element.63), channel_id=1, source_target_pairs={{0,32},{32,64},{64,96},{96,128},{128,160},{160,192},{192,224},{224... | collective-permute-start | bytes 393224 | tf_op jit(solution)/shard_map/ppermute | solution.py:202
  121.4 11.6 %collective-permute-start.31 = (bf16[512,128]{1,0:T(8,128)(2,1)S(1)}, bf16[512,128]{1,0:T(8,128)(2,1)S(1)}, u32[]{:S(2)}, u32[]{:S(2)}) collective-permute-start(bf16[512,128]{1,0:T(8,128)(2,1)S(1)} %get-tuple-element.67), channel_id=1, source_target_pairs={{0,224},{32,0},{64,32},{96,64},{128,96},{160,128},{192,160},{224,1... | collective-permute-start | bytes 393224 | tf_op jit(solution)/shard_map/ppermute | solution.py:202
  123.7 9.7 %collective-permute-start.34 = (bf16[512,128]{1,0:T(8,128)(2,1)S(1)}, bf16[512,128]{1,0:T(8,128)(2,1)S(1)}, u32[]{:S(2)}, u32[]{:S(2)}) collective-permute-start(bf16[512,128]{1,0:T(8,128)(2,1)S(1)} %get-tuple-element.71), channel_id=1, source_target_pairs={{0,32},{32,64},{64,96},{96,128},{128,160},{160,192},{192,224},{224... | collective-permute-start | bytes 393224 | tf_op jit(solution)/shard_map/ppermute | solution.py:202
  123.7 16.4 %collective-permute-start.37 = (bf16[512,128]{1,0:T(8,128)(2,1)S(1)}, bf16[512,128]{1,0:T(8,128)(2,1)S(1)}, u32[]{:S(2)}, u32[]{:S(2)}) collective-permute-start(bf16[512,128]{1,0:T(8,128)(2,1)S(1)} %get-tuple-element.75), channel_id=1, source_target_pairs={{0,224},{32,0},{64,32},{96,64},{128,96},{160,128},{192,160},{224,1... | collective-permute-start | bytes 393224 | tf_op jit(solution)/shard_map/ppermute | solution.py:202
  130.2 17.5 %collective-permute-start.26 = (bf16[8,768,128]{2,1,0:T(8,128)(2,1)S(1)}, bf16[8,768,128]{2,1,0:T(8,128)(2,1)S(1)}, u32[]{:S(2)}, u32[]{:S(2)}) collective-permute-start(bf16[8,768,128]{2,1,0:T(8,128)(2,1)S(1)} %shard_map.103), channel_id=1, source_target_pairs={{0,1},{1,0},{2,3},{3,2},{4,5},{5,4},{6,7},{7,6},{8,9},{9,8},{10,11... | collective-permute-start | bytes 4718600 | tf_op jit(solution)/shard_map/ppermute | solution.py:215
  132.4 7.7 %collective-permute-start.24 = (bf16[256,128]{1,0:T(8,128)(2,1)S(1)}, bf16[256,128]{1,0:T(8,128)(2,1)S(1)}, u32[]{:S(2)}, u32[]{:S(2)}) collective-permute-start(bf16[256,128]{1,0:T(8,128)(2,1)S(1)} %fusion.5), channel_id=1, source_target_pairs={{0,128},{32,160},{64,192},{96,224},{128,0},{160,32},{192,64},{224,... | collective-permute-start | bytes 196616 | tf_op jit(solution)/shard_map/ppermute | solution.py:215
  133.0 14.6 %collective-permute-start.28 = (bf16[512,128]{1,0:T(8,128)(2,1)S(1)}, bf16[512,128]{1,0:T(8,128)(2,1)S(1)}, u32[]{:S(2)}, u32[]{:S(2)}) collective-permute-start(bf16[512,128]{1,0:T(8,128)(2,1)S(1)} %add_convert_fusion.11), channel_id=1, source_target_pairs={{0,32},{32,64},{64,96},{96,128},{128,160},{160,192},{192,224},{224... | collective-permute-start | bytes 393224 | tf_op jit(solution)/shard_map/ppermute | solution.py:202
  133.4 30.7 %collective-permute-start.32 = (bf16[512,128]{1,0:T(8,128)(2,1)S(1)}, bf16[512,128]{1,0:T(8,128)(2,1)S(1)}, u32[]{:S(2)}, u32[]{:S(2)}) collective-permute-start(bf16[512,128]{1,0:T(8,128)(2,1)S(1)} %add_convert_fusion.8), channel_id=1, source_target_pairs={{0,224},{32,0},{64,32},{96,64},{128,96},{160,128},{192,160},{224,1... | collective-permute-start | bytes 393224 | tf_op jit(solution)/shard_map/ppermute | solution.py:202
  140.1 18.8 %collective-permute-start.35 = (bf16[512,128]{1,0:T(8,128)(2,1)}, bf16[512,128]{1,0:T(8,128)(2,1)}, u32[]{:S(2)}, u32[]{:S(2)}) collective-permute-start(bf16[512,128]{1,0:T(8,128)(2,1)} %add_convert_fusion.6), channel_id=1, source_target_pairs={{0,32},{32,64},{64,96},{96,128},{128,160},{160,192},{192,224},{224... | collective-permute-start | bytes 393224 | tf_op jit(solution)/shard_map/ppermute | solution.py:202
  140.2 4.7 %collective-permute-start.25 = (bf16[256,128]{1,0:T(8,128)(2,1)S(1)}, bf16[256,128]{1,0:T(8,128)(2,1)S(1)}, u32[]{:S(2)}, u32[]{:S(2)}) collective-permute-start(bf16[256,128]{1,0:T(8,128)(2,1)S(1)} %fusion.4), channel_id=1, source_target_pairs={{0,16},{16,0},{1,17},{17,1},{2,18},{18,2},{3,19},{19,3},{4,20},{20... | collective-permute-start | bytes 196616 | tf_op jit(solution)/shard_map/ppermute | solution.py:215
  144.9 13.0 %collective-permute-start.38 = (bf16[512,128]{1,0:T(8,128)(2,1)}, bf16[512,128]{1,0:T(8,128)(2,1)}, u32[]{:S(2)}, u32[]{:S(2)}) collective-permute-start(bf16[512,128]{1,0:T(8,128)(2,1)} %add_convert_fusion.4), channel_id=1, source_target_pairs={{0,224},{32,0},{64,32},{96,64},{128,96},{160,128},{192,160},{224,1... | collective-permute-start | bytes 393224 | tf_op jit(solution)/shard_map/ppermute | solution.py:202
  154.3 36.7 %all-to-all-start = ((bf16[8,896,128]{2,1,0:T(8,128)(2,1)}), bf16[8,896,128]{2,1,0:T(8,128)(2,1)S(1)}, u32[]{:S(2)}, u32[]{:S(2)}) async-start(bf16[8,896,128]{2,1,0:T(8,128)(2,1)} %shard_map.104), calls=%async_computation | async-start | bytes 3670016 | tf_op jit(solution)/shard_map/all_to_all | solution.py:308
  158.8 3.9 %collective-permute-start.39 = (bf16[512,128]{1,0:T(8,128)(2,1)S(1)}, bf16[512,128]{1,0:T(8,128)(2,1)S(1)}, u32[]{:S(2)}, u32[]{:S(2)}) collective-permute-start(bf16[512,128]{1,0:T(8,128)(2,1)S(1)} %add_convert_fusion.3), channel_id=1, source_target_pairs={{0,224},{32,0},{64,32},{96,64},{128,96},{160,128},{192,160},{224,1... | collective-permute-start | bytes 393224 | tf_op jit(solution)/shard_map/ppermute | solution.py:202
  159.9 5.8 %collective-permute-start.36 = (bf16[512,128]{1,0:T(8,128)(2,1)S(1)}, bf16[512,128]{1,0:T(8,128)(2,1)S(1)}, u32[]{:S(2)}, u32[]{:S(2)}) collective-permute-start(bf16[512,128]{1,0:T(8,128)(2,1)S(1)} %add_convert_fusion.5), channel_id=1, source_target_pairs={{0,32},{32,64},{64,96},{96,128},{128,160},{160,192},{192,224},{224... | collective-permute-start | bytes 393224 | tf_op jit(solution)/shard_map/ppermute | solution.py:202
  162.8 5.2 %collective-permute-start.40 = (bf16[512,128]{1,0:T(8,128)(2,1)S(1)}, bf16[512,128]{1,0:T(8,128)(2,1)S(1)}, u32[]{:S(2)}, u32[]{:S(2)}) collective-permute-start(bf16[512,128]{1,0:T(8,128)(2,1)S(1)} %add_convert_fusion.2), channel_id=1, source_target_pairs={{0,224},{32,0},{64,32},{96,64},{128,96},{160,128},{192,160},{224,1... | collective-permute-start | bytes 393224 | tf_op jit(solution)/shard_map/ppermute | solution.py:202
  164.1 17.0 %collective-permute-start.33 = (bf16[512,128]{1,0:T(8,128)(2,1)S(1)}, bf16[512,128]{1,0:T(8,128)(2,1)S(1)}, u32[]{:S(2)}, u32[]{:S(2)}) collective-permute-start(bf16[512,128]{1,0:T(8,128)(2,1)S(1)} %add_convert_fusion.7), channel_id=1, source_target_pairs={{0,224},{32,0},{64,32},{96,64},{128,96},{160,128},{192,160},{224,1... | collective-permute-start | bytes 393224 | tf_op jit(solution)/shard_map/ppermute | solution.py:202
  164.2 6.5 %collective-permute-start.29 = (bf16[512,128]{1,0:T(8,128)(2,1)S(1)}, bf16[512,128]{1,0:T(8,128)(2,1)S(1)}, u32[]{:S(2)}, u32[]{:S(2)}) collective-permute-start(bf16[512,128]{1,0:T(8,128)(2,1)S(1)} %add_convert_fusion.10), channel_id=1, source_target_pairs={{0,32},{32,64},{64,96},{96,128},{128,160},{160,192},{192,224},{224... | collective-permute-start | bytes 393224 | tf_op jit(solution)/shard_map/ppermute | solution.py:202
  168.0 13.3 %collective-permute-start.41 = (bf16[512,128]{1,0:T(8,128)(2,1)S(1)}, bf16[512,128]{1,0:T(8,128)(2,1)S(1)}, u32[]{:S(2)}, u32[]{:S(2)}) collective-permute-start(bf16[512,128]{1,0:T(8,128)(2,1)S(1)} %add_convert_fusion.1), channel_id=1, source_target_pairs={{0,16},{16,0},{1,17},{17,1},{2,18},{18,2},{3,19},{19,3},{4,20},{20... | collective-permute-start | bytes 393224 | tf_op jit(solution)/shard_map/ppermute | solution.py:215
  170.7 10.6 %collective-permute-start.30 = (bf16[512,128]{1,0:T(8,128)(2,1)S(1)}, bf16[512,128]{1,0:T(8,128)(2,1)S(1)}, u32[]{:S(2)}, u32[]{:S(2)}) collective-permute-start(bf16[512,128]{1,0:T(8,128)(2,1)S(1)} %add_convert_fusion.9), channel_id=1, source_target_pairs={{0,32},{32,64},{64,96},{96,128},{128,160},{160,192},{192,224},{224... | collective-permute-start | bytes 393224 | tf_op jit(solution)/shard_map/ppermute | solution.py:202
  170.9 20.5 %collective-permute-start.43 = (bf16[256,128]{1,0:T(8,128)(2,1)S(1)}, bf16[256,128]{1,0:T(8,128)(2,1)S(1)}, u32[]{:S(2)}, u32[]{:S(2)}) collective-permute-start(bf16[256,128]{1,0:T(8,128)(2,1)S(1)} %add_convert_fusion.12), channel_id=1, source_target_pairs={{0,0},{1,16},{2,32},{3,48},{4,64},{5,80},{6,96},{7,112},{8,128},{9... | collective-permute-start | bytes 196616 | tf_op jit(solution)/shard_map/ppermute | solution.py:310
  181.4 20.1 %collective-permute-start.42 = (bf16[512,128]{1,0:T(8,128)(2,1)S(1)}, bf16[512,128]{1,0:T(8,128)(2,1)S(1)}, u32[]{:S(2)}, u32[]{:S(2)}) collective-permute-start(bf16[512,128]{1,0:T(8,128)(2,1)S(1)} %add_convert_fusion), channel_id=1, source_target_pairs={{0,0},{1,16},{2,32},{3,48},{4,64},{5,80},{6,96},{7,112},{8,128},{9... | collective-permute-start | bytes 393224 | tf_op jit(solution)/shard_map/ppermute | solution.py:307
  191.3 13.4 %collective-permute-start.44 = (f32[64,128]{1,0:T(8,128)S(1)}, f32[64,128]{1,0:T(8,128)S(1)}, u32[]{:S(2)}, u32[]{:S(2)}) collective-permute-start(f32[64,128]{1,0:T(8,128)S(1)} %slice.44), channel_id=1, source_target_pairs={{0,1},{1,0},{2,3},{3,2},{4,5},{5,4},{6,7},{7,6},{8,9},{9,8},{10,11... | collective-permute-start | bytes 98312 | tf_op jit(solution)/shard_map/ppermute | solution.py:215
  (21 other events, 135.4 us)
Sparse Core Ops, SparseCore 0:
  11.5 44.4 all-gather.2

commit v2 on v1

v2 whole, which is shorter than its diff:
```python
import functools

import jax
import jax.numpy as jnp
from jax import lax
from jax.experimental import pallas as pl
from jax.experimental.pallas import tpu as pltpu
from jax.sharding import Mesh, PartitionSpec as P

BS = 64
NB = 16
SH = 16
NZ = 8
NK = 8
FEAT = 512
WIDTH = 2048
TOK = 128
RANK = 256
RS = RANK // SH
ROWS = FEAT + RS
WROWS = FEAT + 16
VROWS = WIDTH // TOK * RS
UROWS = FEAT // TOK * RS
BCOLS = WIDTH // BS

ROW = ("z", "xh")
COL = ("xl", "y", "core")
ALL = ROW + COL

NN = (((1,), (0,)), ((), ()))
NT = (((1,), (1,)), ((), ()))
F32 = jnp.float32
BF16 = jnp.bfloat16


def dot(a, b, dims):
    return lax.dot_general(a, b, dims, preferred_element_type=F32)


def gelu_pair(z):
    half = 0.5 * (1.0 + lax.erf(z * 0.7071067811865476))
    slope = half + z * jnp.exp(-0.5 * z * z) * 0.3989422804014327
    return z * half, slope


def block_start(position):
    return pl.multiple_of(position * BS, BS)


def x_slot(place, s):
    return (((s >> 1) - place[0]) & (NZ - 1)) * 2 + ((s & 1) ^ place[1])


def x_shard(place, slot):
    return (((slot >> 1) + place[0]) & (NZ - 1)) * 2 + ((slot & 1) ^ place[1])


def first_kernel(x, u, x_t, p):
    x_t[...] = x[...].T
    p[...] = dot(u[...].T, x_t[...], NN).reshape(SH, RS, TOK)


def forward_kernel(place, index, *refs):
    x_parts = refs[:NZ]
    w, v, cot, hidden, dz_t, q_t, x, z_t, sems = refs[NZ:]
    copies = [
        pltpu.make_async_copy(x_parts[rel], x.at[2 * rel : 2 * rel + 2], sems.at[rel])
        for rel in range(NZ)
    ]
    for copy in copies:
        copy.start()
    z_t[...] = jnp.zeros_like(z_t)
    for copy in copies:
        copy.wait()

    def shard(slot, carry):
        s = x_shard(place, slot)
        sums = []
        for pair in range(NB // 2):
            both = w[s, pair * BS : (pair + 1) * BS, :].T
            for side in range(2):
                b = index[s, 2 * pair + side]
                x_block = x[slot, pl.ds(block_start(b // BCOLS), BS), :]
                sums.append((b % BCOLS, dot(both[side * BS : (side + 1) * BS], x_block, NN)))
        for where, value in sums:
            z_t[pl.ds(block_start(where), BS), :] += value
        return carry

    lax.fori_loop(0, SH, shard, 0)
    p = jnp.concatenate([x[x_slot(place, s), FEAT:, :] for s in range(SH)], axis=0).T
    for j in range(WIDTH // TOK):
        part = slice(j * TOK, (j + 1) * TOK)
        z = z_t[part, :].T + dot(p, v[:, part], NN)
        value, slope = gelu_pair(z)
        hidden[:, part] = value.astype(BF16)
        dz = cot[:, part].astype(F32) * slope
        dz_t[part, :] = dz.T.astype(BF16)
    q_t[...] = dot(v[...], dz_t[...], NN)


def back_kernel(slots, place, index, w, dz_t, *refs):
    outs = refs[: len(slots) // 2]
    total, done = refs[len(slots) // 2 :]

    def shard(i, carry):
        slot = (i + slots[0]) & (2 * NZ - 1)
        s = x_shard(place, slot)
        total[...] = jnp.zeros_like(total)
        sums = []
        for pair in range(NB // 2):
            both = w[s, pair * BS : (pair + 1) * BS, :]
            for side in range(2):
                b = index[s, 2 * pair + side]
                dz_block = dz_t[pl.ds(block_start(b % BCOLS), BS), :]
                sums.append((b // BCOLS, dot(both[:, side * BS : (side + 1) * BS], dz_block, NN)))
        for where, value in sums:
            total[pl.ds(block_start(where), BS), :] += value
        done[i] = total[...].astype(BF16)
        return carry

    lax.fori_loop(0, len(slots), shard, 0)
    for i in range(len(slots) // 2):
        outs[i][...] = done[2 * i : 2 * i + 2]


def grad_rows(place, index, x, dz_t, out, half, other):
    core = place[2] ^ half

    def plus(value, k, first):
        if other is not None:
            value += other[k, first : first + value.shape[0], :].astype(F32)
        return value.astype(BF16)

    def shard(k, carry):
        s = 2 * k + core
        slot = x_slot(place, s)
        for pair in range(NB // 2):
            halves = []
            for side in range(2):
                b = index[s, 2 * pair + side]
                x_block = x[slot, pl.ds(block_start(b // BCOLS), BS), :]
                dz_block = dz_t[pl.ds(block_start(b % BCOLS), BS), :]
                halves.append(dot(x_block, dz_block, NT))
            both = jnp.concatenate(halves, axis=1)
            out[k, pair * BS : (pair + 1) * BS, :] = plus(both, k, pair * BS)
        return carry

    lax.fori_loop(0, NK, shard, 0)
    p = jnp.concatenate([x[x_slot(place, 2 * k + core), FEAT:, :] for k in range(NK)], axis=0)
    for j in range(WIDTH // TOK):
        part = dot(p, dz_t[j * TOK : (j + 1) * TOK, :], NT)
        first = FEAT + j * RS
        for k in range(NK):
            out[k, first : first + RS, :] = plus(part[k * RS : (k + 1) * RS], k, first)


def grad_other_kernel(place, index, x, dz_t, out):
    grad_rows(place, index, x, dz_t, out, 1, None)


def grad_own_kernel(place, index, x, dz_t, q_t, other, out):
    grad_rows(place, index, x, dz_t, out, 0, other)
    q = q_t[place[3]]

    def shard(k, carry):
        for half in range(2):
            slot = x_slot(place, 2 * k + (place[2] ^ half))
            u = dot(q, x[slot, :FEAT, :], NT).astype(BF16)
            for j in range(FEAT // TOK):
                first = FEAT + VROWS + half * UROWS + j * RS
                out[k, first : first + RS, :] = u[:, j * TOK : (j + 1) * TOK]
        return carry

    lax.fori_loop(0, NK, shard, 0)


def call(kernel, out_shape, flops, bytes_accessed, operands, scratch=(), free=0, scalars=2):
    vmem = pl.BlockSpec(memory_space=pltpu.VMEM)
    smem = pl.BlockSpec(memory_space=pltpu.SMEM)
    anywhere = pl.BlockSpec(memory_space=pl.ANY)
    many = isinstance(out_shape, tuple)
    return pl.pallas_call(
        kernel,
        out_shape=out_shape,
        in_specs=[smem] * scalars + [anywhere] * free + [vmem] * (len(operands) - scalars - free),
        out_specs=(vmem,) * len(out_shape) if many else vmem,
        scratch_shapes=list(scratch),
        compiler_params=pltpu.CompilerParams(vmem_limit_bytes=10 << 20),
        cost_estimate=pl.CostEstimate(
            flops=flops, bytes_accessed=bytes_accessed, transcendentals=0
        ),
    )(*operands)


def shape(*dims, kind=BF16):
    return jax.ShapeDtypeStruct(dims, kind)


def add(*terms):
    return sum(t.astype(F32) for t in terms).astype(BF16)


def shift(x, by):
    return lax.ppermute(x, "z", [(i, (i + by) % NZ) for i in range(NZ)])


def gather_ring(own):
    held = {0: own, -1: shift(own, 1), 1: shift(own, -1)}
    for step in (1, 2):
        held[-step - 1] = shift(held[-step], 1)
        held[step + 1] = shift(held[step], -1)
    held[4] = shift(held[-3], 1)
    return [held[rel if rel <= 4 else rel - NZ] for rel in range(NZ)]


def meet(x, axis, flip):
    count = {"z": 8, "xh": 2, "xl": 2, "y": 4, "core": 2}[axis]
    return lax.ppermute(x, axis, [(i, i ^ flip) for i in range(count)])


def on_device(inputs, cotangent, sparse_blocks, block_index, u_factor, v_factor):
    turn = [(r * SH + c, c * SH + r) for r in range(SH) for c in range(SH)]
    turn_pair = [(r * SH + c, (c ^ 1) * SH + r) for r in range(SH) for c in range(SH)]
    place = jnp.stack(
        [lax.axis_index("z"), lax.axis_index("xh"), lax.axis_index("core"), lax.axis_index(ROW)]
    ).astype(jnp.int32)

    w_pairs = sparse_blocks.reshape(NB // 2, 2, BS, BS).transpose(0, 2, 1, 3).reshape(FEAT, 2 * BS)
    index_row = jnp.zeros((16, TOK), BF16).at[0, :NB].set(block_index.reshape(NB).astype(BF16))
    w_mine = jnp.concatenate([w_pairs, index_row])
    w_mine, inputs = lax.optimization_barrier((w_mine, inputs))
    w_all = lax.all_gather(w_mine, COL, axis=0)
    index = w_all[:, FEAT, :NB].astype(jnp.int32)

    mine, p = call(
        first_kernel,
        (shape(FEAT, TOK), shape(SH, RS, TOK, kind=F32)),
        40_000_000,
        1 << 19,
        (inputs, u_factor),
        scalars=0,
    )
    turned = lax.ppermute(mine, ALL, turn)
    p_in = lax.all_to_all(p, COL, 0, 0)
    turned, p_in = lax.optimization_barrier((turned, p_in))
    p = jnp.sum(p_in, axis=0).astype(BF16)
    parts = [
        turned,
        lax.ppermute(p, ALL, turn),
        meet(turned, "xh", 1),
        lax.ppermute(p, ALL, turn_pair),
    ]
    x_parts = gather_ring(jnp.concatenate(parts).reshape(2, ROWS, TOK))

    hidden, dz_t, q, x_all = call(
        forward_kernel,
        (
            shape(TOK, WIDTH),
            shape(WIDTH, TOK),
            shape(RANK, TOK, kind=F32),
            shape(SH, ROWS, TOK),
        ),
        800_000_000,
        10 << 20,
        (place, index, *x_parts, w_all, v_factor, cotangent),
        [pltpu.VMEM((WIDTH, TOK), F32), pltpu.SemaphoreType.DMA((NZ,))],
        free=NZ,
    )

    back = {}
    dz_back = dz_t
    for slots in (range(6, 12), range(12, 22)):
        outs = call(
            functools.partial(back_kernel, slots),
            (shape(2, FEAT, TOK),) * (len(slots) // 2),
            20_000_000 * len(slots),
            len(slots) << 19,
            (place, index, w_all, dz_back),
            [pltpu.VMEM((FEAT, TOK), F32), pltpu.VMEM((len(slots), FEAT, TOK), BF16)],
        )
        back.update({slot // 2 % NZ: part for slot, part in zip(slots[::2], outs)})
        dz_back, back[3] = lax.optimization_barrier((dz_back, back[3]))

    up, down = shift(back[4], 1), shift(back[5], -1)
    q, up, down, back[0] = lax.optimization_barrier((q, up, down, back[0]))
    up = add(back[3], up)
    for axis, flip in (("z", 1), ("z", 2), ("z", 4), ("xh", 1)):
        q = q + meet(q.astype(BF16), axis, flip).astype(F32)
    q_t = q.astype(BF16)

    grads = call(
        grad_other_kernel,
        shape(NK, FEAT + VROWS, TOK),
        200_000_000,
        4 << 20,
        (place, index, x_all, dz_t),
    )
    grads = call(
        grad_own_kernel,
        shape(NK, FEAT + VROWS + 2 * UROWS, TOK),
        300_000_000,
        6 << 20,
        (place, index, x_all, dz_t, q_t.reshape(SH, RS, TOK), meet(grads, "core", 1)),
    )

    down = add(back[6], down)
    up = add(back[2], shift(up, 1))
    down = add(back[7], shift(down, -1))
    up = add(back[1], shift(up, 1))
    up, down = shift(up, 1), shift(down, -1)
    grads, up, down = lax.optimization_barrier((grads, up, down))
    other = add(back[0][1], up[1], down[1])
    total = add(back[0][0], up[0], down[0], meet(other, "xh", 1))
    x_grad_t = lax.ppermute(total, ALL, turn)
    grads_in = lax.all_to_all(grads, ("xl", "y"), 0, 0)
    q_turned = lax.ppermute(q_t, ALL, turn)

    grads_sum = jnp.sum(grads_in.astype(F32), axis=0)
    blocks_grad = (
        grads_sum[:FEAT]
        .astype(BF16)
        .reshape(NB // 2, BS, 2, BS)
        .transpose(0, 2, 1, 3)
        .reshape(sparse_blocks.shape)
    )
    v_grad = (
        grads_sum[FEAT : FEAT + VROWS]
        .reshape(WIDTH // TOK, RS, TOK)
        .transpose(1, 0, 2)
        .reshape(RS, WIDTH)
    )
    u_own = grads_sum[FEAT + VROWS : FEAT + VROWS + UROWS]
    u_other = grads_sum[FEAT + VROWS + UROWS :]
    u_grad = (
        (u_own + meet(u_other, "core", 1))
        .reshape(FEAT // TOK, RS, TOK)
        .transpose(0, 2, 1)
        .reshape(FEAT, RS)
    )
    x_low = lax.dot_general(
        q_turned, u_factor, (((0,), (1,)), ((), ())), preferred_element_type=F32
    )
    x_grad_t, x_low, blocks_grad, v_grad, u_grad = lax.optimization_barrier(
        (x_grad_t, x_low, blocks_grad, v_grad, u_grad)
    )
    input_grad = add(x_grad_t.T, x_low)
    return hidden, input_grad, blocks_grad, u_grad, v_grad


def solution(mesh):
    fine = Mesh(mesh.devices.reshape(8, 2, 2, 4, 2), ALL)
    in_specs = (
        P(ROW, COL),
        P(COL, ROW),
        P(COL, ROW, None, None),
        P(COL, ROW, None),
        P(COL, None),
        P(None, ROW),
    )
    out_specs = (
        P(COL, ROW),
        P(ROW, COL),
        P(COL, ROW, None, None),
        P(COL, ROW),
        P(COL, ROW),
    )
    return jax.shard_map(
        on_device, mesh=fine, in_specs=in_specs, out_specs=out_specs, check_vma=False
    )
```

time: 215 us -> 208 us (0.967); the launches traced: 212 us -> 207 us
  starting transfers between devices: 114 us -> 63.7 us
  waiting for transfers between devices: 31.5 us -> 76.6 us
  blocking collectives: 0 us -> 16.1 us
  local copies, waits for them, and re-layouts: 19.1 us -> 8.67 us
  other arithmetic: 5.52 us -> 2.38 us
    ppermute x28 -> x14, starting transfers between devices: 49.4 us -> 23.7 us  [shift(): return lax.ppermute(x, 'z', [(i, (i + by) % NZ) for i in range(NZ)])]
    ppermute x13 -> x8, starting transfers between devices: 33.6 us -> 9.27 us  [meet(): return lax.ppermute(x, axis, [(i, i ^ flip) for i in range(count)])]
    ppermute x1, waiting for transfers between devices: 0.01 us -> 23.6 us  [on_device(): q_turned = lax.ppermute(q_t, ALL, turn)]
    ppermute x28 -> x14, waiting for transfers between devices: 6.59 us -> 25.8 us  [shift(): return lax.ppermute(x, 'z', [(i, (i + by) % NZ) for i in range(NZ)])]
    ppermute x13 -> x8, waiting for transfers between devices: 6.36 us -> 22.9 us  [meet(): return lax.ppermute(x, axis, [(i, i ^ flip) for i in range(count)])]
    all_to_all x0 -> x1, blocking collectives: none -> 16.1 us  [on_device(): p_in = lax.all_to_all(p, COL, 0, 0)]
    unnamed x48 -> x13, local copies, waits for them, and re-layouts: 13.9 us -> 2.4 us
    ppermute x1, waiting for transfers between devices: 10.1 us -> 0.42 us  [on_device(): x_grad_t = lax.ppermute(total, ALL, turn)]
  transfers between devices with their start and end apart: 47 -> 29, of which waited for: 12 -> 14; matrix products, arithmetic and copies ran while one was open for 4% -> 3% of each run, Pallas kernels for 6% -> 7%
where the time goes in v2:
time: 208 us; the launch traced here: 207 us
  waiting for transfers between devices  76.6 us (37%)
  starting transfers between devices  63.7 us (31%)
  Pallas kernels  25.3 us (12%)
  blocking collectives  16.1 us (8%)
  between operations  14.4 us (7%)
  local copies, waits for them, and re-layouts  8.67 us (4%)
  other arithmetic  2.38 us (1%)
    ppermute x14, waiting for transfers between devices, shift(): return lax.ppermute(x, 'z', [(i, (i + by) % NZ) for i in range(NZ)])  25.8 us
    pallas_call x6, Pallas kernels, call(): pl.pallas_call(kernel, out_shape=out_shape, in_specs=[smem] * scalars + [...  25.3 us
    ppermute x14, starting transfers between devices, shift(): return lax.ppermute(x, 'z', [(i, (i + by) % NZ) for i in range(NZ)])  23.7 us
    ppermute x1, waiting for transfers between devices, on_device(): q_turned = lax.ppermute(q_t, ALL, turn)  23.6 us
    ppermute x8, waiting for transfers between devices, meet(): return lax.ppermute(x, axis, [(i, i ^ flip) for i in range(count)])  22.9 us
    all_to_all x1, blocking collectives, on_device(): p_in = lax.all_to_all(p, COL, 0, 0)  16.1 us
    ppermute x1, starting transfers between devices, on_device(): q_turned = lax.ppermute(q_t, ALL, turn)  9.81 us
    ppermute x8, starting transfers between devices, meet(): return lax.ppermute(x, axis, [(i, i ^ flip) for i in range(count)])  9.27 us
  transfers between devices with their start and end apart: 29, of which 14 were waited for; matrix products, arithmetic and copies ran while one was open for 3% of the time, Pallas kernels for 7%

profile of v2, /device:TPU:1, one launch (start us, length us, event | category | flops | bytes accessed | tf_op | source)
XLA Modules:
  0.0 207.4 jit_solution(15764826841333110209)
XLA Ops:
  7.3 1.3 reshape.90
  9.0 0.7 convert_bitcast_fusion
  9.8 0.8 copy.35
  10.9 6.0 %collective-permute-start = (bf16[512,128]{1,0:T(8,128)(2,1)S(1)}, bf16[512,128]{1,0:T(8,128)(2,1)S(1)}, u32[]{:S(2)}, u32[]{:S(2)}) collective-permute-start(bf16[512,128]{1,0:T(8,128)(2,1)S(1)} %get-tuple-element.52), channel_id=1, source_target_pairs={{0,0},{1,16},{2,32},{3,48},{4,64},{5,80},{6,96},{7,112},{8,128},{9... | collective-permute-start | bytes 393224 | tf_op jit(solution)/shard_map/ppermute | solution.py:243
  17.0 16.1 %all_to_all.10 = f32[16,16,128]{2,1,0:T(8,128)S(1)} all-to-all(f32[16,16,128]{2,1,0:T(8,128)S(1)} %get-tuple-element.53), channel_id=1, replica_groups=mesh['z'=8,'xh'=2,'xl'=2,'y'=4,'core'=2] {'xl','y','core'}, dimensions={0} | all-to-all | bytes 262144 | tf_op jit(solution)/shard_map/all_to_all | solution.py:244
  33.1 0.8 collective-permute-start.2
  33.9 5.3 %collective-permute-start.1 = (bf16[16,128]{1,0:T(8,128)(2,1)S(1)}, bf16[16,128]{1,0:T(8,128)(2,1)S(1)}, u32[]{:S(2)}, u32[]{:S(2)}) collective-permute-start(bf16[16,128]{1,0:T(8,128)(2,1)S(1)} %reduce_sum.18), channel_id=1, source_target_pairs={{0,0},{1,16},{2,32},{3,48},{4,64},{5,80},{6,96},{7,112},{8,128},{9... | collective-permute-start | bytes 12296 | tf_op jit(solution)/shard_map/ppermute | solution.py:249
  39.3 2.4 %collective-permute-done.1 = bf16[16,128]{1,0:T(8,128)(2,1)S(1)} collective-permute-done((bf16[16,128]{1,0:T(8,128)(2,1)S(1)}, bf16[16,128]{1,0:T(8,128)(2,1)S(1)}, u32[]{:S(2)}, u32[]{:S(2)}) %collective-permute-start.1) | collective-permute-done | bytes 4128 | tf_op jit(solution)/shard_map/ppermute | solution.py:249
  41.7 1.5 collective-permute-done.3
  43.3 2.0 collective-permute-start.7
  45.3 7.7 %collective-permute-start.4 = (bf16[2,528,128]{2,1,0:T(8,128)(2,1)S(1)}, bf16[2,528,128]{2,1,0:T(8,128)(2,1)S(1)}, u32[]{:S(2)}, u32[]{:S(2)}) collective-permute-start(bf16[2,528,128]{2,1,0:T(8,128)(2,1)S(1)} %bitcast.57), channel_id=1, source_target_pairs={{0,224},{32,0},{64,32},{96,64},{128,96},{160,128},{192,160},{224,1... | collective-permute-start | bytes 811016 | tf_op jit(solution)/shard_map/ppermute | solution.py:204
  52.9 6.3 %collective-permute-done.7.refs_7_ = bf16[2,528,128]{2,1,0:T(8,128)(2,1)S(1)} collective-permute-done((bf16[2,528,128]{2,1,0:T(8,128)(2,1)S(1)}, bf16[2,528,128]{2,1,0:T(8,128)(2,1)S(1)}, u32[]{:S(2)}, u32[]{:S(2)}) %collective-permute-start.7) | collective-permute-done | bytes 270368 | tf_op jit(solution)/shard_map/ppermute | solution.py:204
  59.2 2.7 %collective-permute-start.5 = (bf16[2,528,128]{2,1,0:T(8,128)(2,1)S(1)}, bf16[2,528,128]{2,1,0:T(8,128)(2,1)S(1)}, u32[]{:S(2)}, u32[]{:S(2)}) collective-permute-start(bf16[2,528,128]{2,1,0:T(8,128)(2,1)S(1)} %collective-permute-done.4.refs_1_), channel_id=1, source_target_pairs={{0,224},{32,0},{64,32},{96,64},{128,96},{160,128},{192,160},{224,1... | collective-permute-start | bytes 811016 | tf_op jit(solution)/shard_map/ppermute | solution.py:204
  61.9 5.5 %collective-permute-done.8.refs_6_ = bf16[2,528,128]{2,1,0:T(8,128)(2,1)S(1)} collective-permute-done((bf16[2,528,128]{2,1,0:T(8,128)(2,1)S(1)}, bf16[2,528,128]{2,1,0:T(8,128)(2,1)S(1)}, u32[]{:S(2)}, u32[]{:S(2)}) %collective-permute-start.8) | collective-permute-done | bytes 270368 | tf_op jit(solution)/shard_map/ppermute | solution.py:204
  67.4 2.7 %collective-permute-start.6 = (bf16[2,528,128]{2,1,0:T(8,128)(2,1)S(1)}, bf16[2,528,128]{2,1,0:T(8,128)(2,1)}, u32[]{:S(2)}, u32[]{:S(2)}) collective-permute-start(bf16[2,528,128]{2,1,0:T(8,128)(2,1)S(1)} %collective-permute-done.5.refs_2_), channel_id=1, source_target_pairs={{0,224},{32,0},{64,32},{96,64},{128,96},{160,128},{192,160},{224,1... | collective-permute-start | bytes 811016 | tf_op jit(solution)/shard_map/ppermute | solution.py:204
  70.1 4.5 %collective-permute-done.9.refs_5_ = bf16[2,528,128]{2,1,0:T(8,128)(2,1)S(1)} collective-permute-done((bf16[2,528,128]{2,1,0:T(8,128)(2,1)S(1)}, bf16[2,528,128]{2,1,0:T(8,128)(2,1)S(1)}, u32[]{:S(2)}, u32[]{:S(2)}) %collective-permute-start.9) | collective-permute-done | bytes 270368 | tf_op jit(solution)/shard_map/ppermute | solution.py:204
  74.7 0.8 slice.61
  75.5 5.8 %collective-permute-done.10.refs_4_ = bf16[2,528,128]{2,1,0:T(8,128)(2,1)} collective-permute-done((bf16[2,528,128]{2,1,0:T(8,128)(2,1)S(1)}, bf16[2,528,128]{2,1,0:T(8,128)(2,1)}, u32[]{:S(2)}, u32[]{:S(2)}) %collective-permute-start.10) | collective-permute-done | bytes 270368 | tf_op jit(solution)/shard_map/ppermute | solution.py:204
  81.2 1.6 copy-done
  82.9 8.6 %shard_map.102 = (bf16[128,2048]{1,0:T(8,128)(2,1)}, bf16[2048,128]{1,0:T(8,128)(2,1)S(1)}, f32[256,128]{1,0:T(8,128)S(1)}, bf16[16,528,128]{2,1,0:T(8,128)(2,1)S(1)}) custom-call(s32[4]{0:T(128)S(1)} %pad_add_fusion.place, s32[16,16]{1,0:T(8,128)S(1)} %fusion.7.index, bf16[2,528,128]{2,1,0:T(8,128)(2,1)S(1)} %bitcast.58, ...), custom_call_target="tpu_custom_call" | custom-call | flops 800000000 | bytes 10485760 | tf_op jit(solution)/shard_map/pallas_call | solution.py:182
  91.5 2.4 %shard_map.103 = (bf16[2,512,128]{2,1,0:T(8,128)(2,1)S(1)}, bf16[2,512,128]{2,1,0:T(8,128)(2,1)S(1)}, bf16[2,512,128]{2,1,0:T(8,128)(2,1)S(1)}) custom-call(s32[4]{0:T(128)S(1)} %pad_add_fusion.place, s32[16,16]{1,0:T(8,128)S(1)} %fusion.7.index, bf16[16,528,128]{2,1,0:T(8,128)(2,1)S(1)} %bitcast.54, bf16[2048,128]{1,0:T(8,128)(2,1)S(1)} %get-tuple-element.62.dz_t), custom_call_target="tpu_custom_call" | custom-call | flops 120000000 | bytes 3145728 | tf_op jit(solution)/shard_map/pallas_call | solution.py:182
  94.0 3.6 %collective-permute-start.12 = (bf16[2,512,128]{2,1,0:T(8,128)(2,1)S(1)}, bf16[2,512,128]{2,1,0:T(8,128)(2,1)S(1)}, u32[]{:S(2)}, u32[]{:S(2)}) collective-permute-start(bf16[2,512,128]{2,1,0:T(8,128)(2,1)S(1)} %get-tuple-element.60), channel_id=1, source_target_pairs={{0,224},{32,0},{64,32},{96,64},{128,96},{160,128},{192,160},{224,1... | collective-permute-start | bytes 786440 | tf_op jit(solution)/shard_map/ppermute | solution.py:204
  97.6 3.8 %shard_map.105 = bf16[8,768,128]{2,1,0:T(8,128)(2,1)S(1)} custom-call(s32[4]{0:T(128)S(1)} %pad_add_fusion.place, s32[16,16]{1,0:T(8,128)S(1)} %fusion.7.index, bf16[16,528,128]{2,1,0:T(8,128)(2,1)S(1)} %get-tuple-element.65.x, bf16[2048,128]{1,0:T(8,128)(2,1)S(1)} %get-tuple-element.62.dz_t), custom_call_target="tpu_custom_call" | custom-call | flops 200000000 | bytes 4194304 | tf_op jit(solution)/shard_map/pallas_call | solution.py:182
  101.4 3.8 %collective-permute-start.17 = (bf16[8,768,128]{2,1,0:T(8,128)(2,1)S(1)}, bf16[8,768,128]{2,1,0:T(8,128)(2,1)S(1)}, u32[]{:S(2)}, u32[]{:S(2)}) collective-permute-start(bf16[8,768,128]{2,1,0:T(8,128)(2,1)S(1)} %shard_map.105), channel_id=1, source_target_pairs={{0,1},{1,0},{2,3},{3,2},{4,5},{5,4},{6,7},{7,6},{8,9},{9,8},{10,11... | collective-permute-start | bytes 4718600 | tf_op jit(solution)/shard_map/ppermute | solution.py:218
  105.1 3.6 %shard_map.104 = (bf16[2,512,128]{2,1,0:T(8,128)(2,1)S(1)}, bf16[2,512,128]{2,1,0:T(8,128)(2,1)S(1)}, bf16[2,512,128]{2,1,0:T(8,128)(2,1)S(1)}, bf16[2,512,128]{2,1,0:T(8,128)(2,1)S(1)}, bf16[2,512,128]{2,1,0:T(8,128)(2,1)S(1)}) custom-call(s32[4]{0:T(128)S(1)} %pad_add_fusion.place, s32[16,16]{1,0:T(8,128)S(1)} %fusion.7.index, ...), custom_call_target="tpu_custom_call" | custom-call | flops 200000000 | bytes 5242880 | tf_op jit(solution)/shard_map/pallas_call | solution.py:182
  108.9 1.5 collective-permute-start.18
  110.4 2.1 %collective-permute-done.13 = bf16[256,128]{1,0:T(8,128)(2,1)S(1)} collective-permute-done((bf16[256,128]{1,0:T(8,128)(2,1)S(1)}, bf16[256,128]{1,0:T(8,128)(2,1)S(1)}, u32[]{:S(2)}, u32[]{:S(2)}) %collective-permute-start.13) | collective-permute-done | bytes 65568 | tf_op jit(solution)/shard_map/ppermute | solution.py:218
  112.7 1.5 collective-permute-start.21
  114.2 4.3 %collective-permute-done.14 = bf16[256,128]{1,0:T(8,128)(2,1)S(1)} collective-permute-done((bf16[256,128]{1,0:T(8,128)(2,1)S(1)}, bf16[256,128]{1,0:T(8,128)(2,1)S(1)}, u32[]{:S(2)}, u32[]{:S(2)}) %collective-permute-start.14) | collective-permute-done | bytes 65568 | tf_op jit(solution)/shard_map/ppermute | solution.py:218
  118.6 2.2 %collective-permute-start.15 = (bf16[256,128]{1,0:T(8,128)(2,1)S(1)}, bf16[256,128]{1,0:T(8,128)(2,1)S(1)}, u32[]{:S(2)}, u32[]{:S(2)}) collective-permute-start(bf16[256,128]{1,0:T(8,128)(2,1)S(1)} %fusion.8), channel_id=1, source_target_pairs={{0,128},{32,160},{64,192},{96,224},{128,0},{160,32},{192,64},{224,... | collective-permute-start | bytes 196616 | tf_op jit(solution)/shard_map/ppermute | solution.py:218
  121.0 4.9 %collective-permute-done.15 = bf16[256,128]{1,0:T(8,128)(2,1)S(1)} collective-permute-done((bf16[256,128]{1,0:T(8,128)(2,1)S(1)}, bf16[256,128]{1,0:T(8,128)(2,1)S(1)}, u32[]{:S(2)}, u32[]{:S(2)}) %collective-permute-start.15) | collective-permute-done | bytes 65568 | tf_op jit(solution)/shard_map/ppermute | solution.py:218
  126.0 2.0 collective-permute-start.16
  128.0 1.8 collective-permute-start.22
  129.8 2.5 %collective-permute-done.19 = bf16[2,512,128]{2,1,0:T(8,128)(2,1)S(1)} collective-permute-done((bf16[2,512,128]{2,1,0:T(8,128)(2,1)S(1)}, bf16[2,512,128]{2,1,0:T(8,128)(2,1)S(1)}, u32[]{:S(2)}, u32[]{:S(2)}) %collective-permute-start.19) | collective-permute-done | bytes 262176 | tf_op jit(solution)/shard_map/ppermute | solution.py:204
  132.6 6.6 %shard_map.106 = bf16[8,896,128]{2,1,0:T(8,128)(2,1)} custom-call(s32[4]{0:T(128)S(1)} %pad_add_fusion.place, s32[16,16]{1,0:T(8,128)S(1)} %fusion.7.index, bf16[16,528,128]{2,1,0:T(8,128)(2,1)S(1)} %get-tuple-element.65.x, bf16[2048,128]{1,0:T(8,128)(2,1)S(1)} %get-tuple-element.62.dz_t, bf16[16,16,128]{2,1,0:T(8,128)(2,1)S(1)} %bitcast.59, ...), custom_call_target="tpu_custom_call" | custom-call | flops 300000000 | bytes 6291456 | tf_op jit(solution)/shard_map/pallas_call | solution.py:182
  139.2 1.2 collective-permute-done.20
  140.4 4.9 %all-to-all-start.1 = ((bf16[8,896,128]{2,1,0:T(8,128)(2,1)}), bf16[8,896,128]{2,1,0:T(8,128)(2,1)S(1)}, u32[]{:S(2)}, u32[]{:S(2)}) async-start(bf16[8,896,128]{2,1,0:T(8,128)(2,1)} %shard_map.106), calls=%async_computation.1 | async-start | bytes 3670016 | tf_op jit(solution)/shard_map/all_to_all | solution.py:315
  145.3 9.8 %collective-permute-start.25 = (bf16[256,128]{1,0:T(8,128)(2,1)S(1)}, bf16[256,128]{1,0:T(8,128)(2,1)S(1)}, u32[]{:S(2)}, u32[]{:S(2)}) collective-permute-start(bf16[256,128]{1,0:T(8,128)(2,1)S(1)} %add_convert_fusion.6), channel_id=1, source_target_pairs={{0,0},{1,16},{2,32},{3,48},{4,64},{5,80},{6,96},{7,112},{8,128},{9... | collective-permute-start | bytes 196616 | tf_op jit(solution)/shard_map/ppermute | solution.py:316
  155.1 23.6 %collective-permute-done.25 = bf16[256,128]{1,0:T(8,128)(2,1)S(1)} collective-permute-done((bf16[256,128]{1,0:T(8,128)(2,1)S(1)}, bf16[256,128]{1,0:T(8,128)(2,1)S(1)}, u32[]{:S(2)}, u32[]{:S(2)}) %collective-permute-start.25) | collective-permute-done | bytes 65568 | tf_op jit(solution)/shard_map/ppermute | solution.py:316
  178.9 0.7 fusion.4
  179.9 0.3 collective-permute-start.26
  180.2 11.5 %collective-permute-done.23 = bf16[512,128]{1,0:T(8,128)(2,1)S(1)} collective-permute-done((bf16[512,128]{1,0:T(8,128)(2,1)}, bf16[512,128]{1,0:T(8,128)(2,1)S(1)}, u32[]{:S(2)}, u32[]{:S(2)}) %collective-permute-start.23) | collective-permute-done | bytes 131104 | tf_op jit(solution)/shard_map/ppermute | solution.py:218
  191.8 4.5 %collective-permute-start.24 = (bf16[512,128]{1,0:T(8,128)(2,1)S(1)}, bf16[512,128]{1,0:T(8,128)(2,1)S(1)}, u32[]{:S(2)}, u32[]{:S(2)}) collective-permute-start(bf16[512,128]{1,0:T(8,128)(2,1)S(1)} %fusion.2), channel_id=1, source_target_pairs={{0,0},{1,16},{2,32},{3,48},{4,64},{5,80},{6,96},{7,112},{8,128},{9... | collective-permute-start | bytes 393224 | tf_op jit(solution)/shard_map/ppermute | solution.py:314
  197.0 0.9 reshape.95
  197.9 0.7 copy.51
  198.6 0.6 copy.52
  199.2 0.4 collective-permute-done.24
  199.8 0.8 copy.42
  (69 shorter events, 3.4 us)
Async XLA Ops:
  7.2 3.4 %copy-start.5 = (bf16[128,512]{1,0:T(8,128)(2,1)S(1)}, bf16[128,512]{1,0:T(8,128)(2,1)}, u32[]{:S(2)}) copy-start(bf16[128,512]{1,0:T(8,128)(2,1)} %x.2) | copy-start | bytes 393220
  7.2 3.4 %copy-start.2 = (bf16[512,256]{1,0:T(8,128)(2,1)S(1)}, bf16[512,256]{1,0:T(8,128)(2,1)}, u32[]{:S(2)}) copy-start(bf16[512,256]{1,0:T(8,128)(2,1)} %u.1) | copy-start | bytes 786436
  7.2 74.1 %copy-start.3 = (bf16[256,2048]{1,0:T(8,128)(2,1)S(1)}, bf16[256,2048]{1,0:T(8,128)(2,1)}, u32[]{:S(2)}) copy-start(bf16[256,2048]{1,0:T(8,128)(2,1)} %refs_9_.1) | copy-start | bytes 3145732
  7.2 74.0 %copy-start.4 = (bf16[128,2048]{1,0:T(8,128)(2,1)S(1)}, bf16[128,2048]{1,0:T(8,128)(2,1)}, u32[]{:S(2)}) copy-start(bf16[128,2048]{1,0:T(8,128)(2,1)} %refs_10_.1) | copy-start | bytes 1572868
  7.2 67.5 %all-gather.3.cloned.1.call-start = ((), (), s32[]{:S(2)}) async-start(), calls=%async_computation.2 | async-start | bytes 2297856 | tf_op jit(solution)/shard_map/all_gather | solution.py:232
  10.9 22.2 %collective-permute-start = (bf16[512,128]{1,0:T(8,128)(2,1)S(1)}, bf16[512,128]{1,0:T(8,128)(2,1)S(1)}, u32[]{:S(2)}, u32[]{:S(2)}) collective-permute-start(bf16[512,128]{1,0:T(8,128)(2,1)S(1)} %get-tuple-element.52), channel_id=1, source_target_pairs={{0,0},{1,16},{2,32},{3,48},{4,64},{5,80},{6,96},{7,112},{8,128},{9... | collective-permute-start | bytes 393224 | tf_op jit(solution)/shard_map/ppermute | solution.py:243
  33.1 10.2 %collective-permute-start.2 = (bf16[512,128]{1,0:T(8,128)(2,1)S(1)}, bf16[512,128]{1,0:T(8,128)(2,1)S(1)}, u32[]{:S(2)}, u32[]{:S(2)}) collective-permute-start(bf16[512,128]{1,0:T(8,128)(2,1)S(1)} %collective-permute-done), channel_id=1, source_target_pairs={{0,16},{16,0},{1,17},{17,1},{2,18},{18,2},{3,19},{19,3},{4,20},{20... | collective-permute-start | bytes 393224 | tf_op jit(solution)/shard_map/ppermute | solution.py:218
  33.9 7.8 %collective-permute-start.1 = (bf16[16,128]{1,0:T(8,128)(2,1)S(1)}, bf16[16,128]{1,0:T(8,128)(2,1)S(1)}, u32[]{:S(2)}, u32[]{:S(2)}) collective-permute-start(bf16[16,128]{1,0:T(8,128)(2,1)S(1)} %reduce_sum.18), channel_id=1, source_target_pairs={{0,0},{1,16},{2,32},{3,48},{4,64},{5,80},{6,96},{7,112},{8,128},{9... | collective-permute-start | bytes 12296 | tf_op jit(solution)/shard_map/ppermute | solution.py:249
  39.2 4.0 %collective-permute-start.3 = (bf16[16,128]{1,0:T(8,128)(2,1)S(1)}, bf16[16,128]{1,0:T(8,128)(2,1)S(1)}, u32[]{:S(2)}, u32[]{:S(2)}) collective-permute-start(bf16[16,128]{1,0:T(8,128)(2,1)S(1)} %reduce_sum.18), channel_id=1, source_target_pairs={{0,16},{1,0},{2,48},{3,32},{4,80},{5,64},{6,112},{7,96},{8,144},{9... | collective-permute-start | bytes 12296 | tf_op jit(solution)/shard_map/ppermute | solution.py:251
  43.3 15.9 %collective-permute-start.7 = (bf16[2,528,128]{2,1,0:T(8,128)(2,1)S(1)}, bf16[2,528,128]{2,1,0:T(8,128)(2,1)S(1)}, u32[]{:S(2)}, u32[]{:S(2)}) collective-permute-start(bf16[2,528,128]{2,1,0:T(8,128)(2,1)S(1)} %bitcast.56), channel_id=1, source_target_pairs={{0,32},{32,64},{64,96},{96,128},{128,160},{160,192},{192,224},{224... | collective-permute-start | bytes 811016 | tf_op jit(solution)/shard_map/ppermute | solution.py:204
  45.3 14.0 %collective-permute-start.4 = (bf16[2,528,128]{2,1,0:T(8,128)(2,1)S(1)}, bf16[2,528,128]{2,1,0:T(8,128)(2,1)S(1)}, u32[]{:S(2)}, u32[]{:S(2)}) collective-permute-start(bf16[2,528,128]{2,1,0:T(8,128)(2,1)S(1)} %bitcast.57), channel_id=1, source_target_pairs={{0,224},{32,0},{64,32},{96,64},{128,96},{160,128},{192,160},{224,1... | collective-permute-start | bytes 811016 | tf_op jit(solution)/shard_map/ppermute | solution.py:204
  59.2 8.2 %collective-permute-start.8 = (bf16[2,528,128]{2,1,0:T(8,128)(2,1)S(1)}, bf16[2,528,128]{2,1,0:T(8,128)(2,1)S(1)}, u32[]{:S(2)}, u32[]{:S(2)}) collective-permute-start(bf16[2,528,128]{2,1,0:T(8,128)(2,1)S(1)} %collective-permute-done.7.refs_7_), channel_id=1, source_target_pairs={{0,32},{32,64},{64,96},{96,128},{128,160},{160,192},{192,224},{224... | collective-permute-start | bytes 811016 | tf_op jit(solution)/shard_map/ppermute | solution.py:204
  59.2 8.2 %collective-permute-start.5 = (bf16[2,528,128]{2,1,0:T(8,128)(2,1)S(1)}, bf16[2,528,128]{2,1,0:T(8,128)(2,1)S(1)}, u32[]{:S(2)}, u32[]{:S(2)}) collective-permute-start(bf16[2,528,128]{2,1,0:T(8,128)(2,1)S(1)} %collective-permute-done.4.refs_1_), channel_id=1, source_target_pairs={{0,224},{32,0},{64,32},{96,64},{128,96},{160,128},{192,160},{224,1... | collective-permute-start | bytes 811016 | tf_op jit(solution)/shard_map/ppermute | solution.py:204
  67.4 7.2 %collective-permute-start.9 = (bf16[2,528,128]{2,1,0:T(8,128)(2,1)S(1)}, bf16[2,528,128]{2,1,0:T(8,128)(2,1)S(1)}, u32[]{:S(2)}, u32[]{:S(2)}) collective-permute-start(bf16[2,528,128]{2,1,0:T(8,128)(2,1)S(1)} %collective-permute-done.8.refs_6_), channel_id=1, source_target_pairs={{0,32},{32,64},{64,96},{96,128},{128,160},{160,192},{192,224},{224... | collective-permute-start | bytes 811016 | tf_op jit(solution)/shard_map/ppermute | solution.py:204
  67.4 8.1 %collective-permute-start.6 = (bf16[2,528,128]{2,1,0:T(8,128)(2,1)S(1)}, bf16[2,528,128]{2,1,0:T(8,128)(2,1)}, u32[]{:S(2)}, u32[]{:S(2)}) collective-permute-start(bf16[2,528,128]{2,1,0:T(8,128)(2,1)S(1)} %collective-permute-done.5.refs_2_), channel_id=1, source_target_pairs={{0,224},{32,0},{64,32},{96,64},{128,96},{160,128},{192,160},{224,1... | collective-permute-start | bytes 811016 | tf_op jit(solution)/shard_map/ppermute | solution.py:204
  74.6 6.6 %collective-permute-start.10 = (bf16[2,528,128]{2,1,0:T(8,128)(2,1)S(1)}, bf16[2,528,128]{2,1,0:T(8,128)(2,1)}, u32[]{:S(2)}, u32[]{:S(2)}) collective-permute-start(bf16[2,528,128]{2,1,0:T(8,128)(2,1)S(1)} %collective-permute-done.9.refs_5_), channel_id=1, source_target_pairs={{0,32},{32,64},{64,96},{96,128},{128,160},{160,192},{192,224},{224... | collective-permute-start | bytes 811016 | tf_op jit(solution)/shard_map/ppermute | solution.py:204
  81.2 1.6 copy-start
  82.9 8.6 %copy-start.1 = (bf16[8448,128]{1,0:T(8,128)(2,1)S(1)}, bf16[8448,128]{1,0:T(8,128)(2,1)}, u32[]{:S(2)}) copy-start(bf16[8448,128]{1,0:T(8,128)(2,1)} %all-gather.3.cloned.1.call-done) | copy-start | bytes 6488068
  93.9 14.8 %collective-permute-start.11 = (bf16[2,512,128]{2,1,0:T(8,128)(2,1)S(1)}, bf16[2,512,128]{2,1,0:T(8,128)(2,1)S(1)}, u32[]{:S(2)}, u32[]{:S(2)}) collective-permute-start(bf16[2,512,128]{2,1,0:T(8,128)(2,1)S(1)} %get-tuple-element.59), channel_id=1, source_target_pairs={{0,32},{32,64},{64,96},{96,128},{128,160},{160,192},{192,224},{224... | collective-permute-start | bytes 786440 | tf_op jit(solution)/shard_map/ppermute | solution.py:204
  94.0 14.7 %collective-permute-start.12 = (bf16[2,512,128]{2,1,0:T(8,128)(2,1)S(1)}, bf16[2,512,128]{2,1,0:T(8,128)(2,1)S(1)}, u32[]{:S(2)}, u32[]{:S(2)}) collective-permute-start(bf16[2,512,128]{2,1,0:T(8,128)(2,1)S(1)} %get-tuple-element.60), channel_id=1, source_target_pairs={{0,224},{32,0},{64,32},{96,64},{128,96},{160,128},{192,160},{224,1... | collective-permute-start | bytes 786440 | tf_op jit(solution)/shard_map/ppermute | solution.py:204
  101.4 31.3 %collective-permute-start.17 = (bf16[8,768,128]{2,1,0:T(8,128)(2,1)S(1)}, bf16[8,768,128]{2,1,0:T(8,128)(2,1)S(1)}, u32[]{:S(2)}, u32[]{:S(2)}) collective-permute-start(bf16[8,768,128]{2,1,0:T(8,128)(2,1)S(1)} %shard_map.105), channel_id=1, source_target_pairs={{0,1},{1,0},{2,3},{3,2},{4,5},{5,4},{6,7},{7,6},{8,9},{9,8},{10,11... | collective-permute-start | bytes 4718600 | tf_op jit(solution)/shard_map/ppermute | solution.py:218
  108.7 3.8 %collective-permute-start.13 = (bf16[256,128]{1,0:T(8,128)(2,1)S(1)}, bf16[256,128]{1,0:T(8,128)(2,1)S(1)}, u32[]{:S(2)}, u32[]{:S(2)}) collective-permute-start(bf16[256,128]{1,0:T(8,128)(2,1)S(1)} %convert_element_type.146), channel_id=1, source_target_pairs={{0,32},{32,0},{64,96},{96,64},{128,160},{160,128},{192,224},{224,1... | collective-permute-start | bytes 196616 | tf_op jit(solution)/shard_map/ppermute | solution.py:218
  108.9 11.9 %collective-permute-start.18 = (bf16[2,512,128]{2,1,0:T(8,128)(2,1)S(1)}, bf16[2,512,128]{2,1,0:T(8,128)(2,1)S(1)}, u32[]{:S(2)}, u32[]{:S(2)}) collective-permute-start(bf16[2,512,128]{2,1,0:T(8,128)(2,1)S(1)} %add_convert_fusion.4), channel_id=1, source_target_pairs={{0,32},{32,64},{64,96},{96,128},{128,160},{160,192},{192,224},{224... | collective-permute-start | bytes 786440 | tf_op jit(solution)/shard_map/ppermute | solution.py:204
  112.5 6.0 %collective-permute-start.14 = (bf16[256,128]{1,0:T(8,128)(2,1)S(1)}, bf16[256,128]{1,0:T(8,128)(2,1)S(1)}, u32[]{:S(2)}, u32[]{:S(2)}) collective-permute-start(bf16[256,128]{1,0:T(8,128)(2,1)S(1)} %fusion.5), channel_id=1, source_target_pairs={{0,64},{32,96},{64,0},{96,32},{128,192},{160,224},{192,128},{224,1... | collective-permute-start | bytes 196616 | tf_op jit(solution)/shard_map/ppermute | solution.py:218
  112.7 15.2 %collective-permute-start.21 = (bf16[2,512,128]{2,1,0:T(8,128)(2,1)S(1)}, bf16[2,512,128]{2,1,0:T(8,128)(2,1)S(1)}, u32[]{:S(2)}, u32[]{:S(2)}) collective-permute-start(bf16[2,512,128]{2,1,0:T(8,128)(2,1)S(1)} %add_convert_fusion.1), channel_id=1, source_target_pairs={{0,224},{32,0},{64,32},{96,64},{128,96},{160,128},{192,160},{224,1... | collective-permute-start | bytes 786440 | tf_op jit(solution)/shard_map/ppermute | solution.py:204
  118.6 7.3 %collective-permute-start.15 = (bf16[256,128]{1,0:T(8,128)(2,1)S(1)}, bf16[256,128]{1,0:T(8,128)(2,1)S(1)}, u32[]{:S(2)}, u32[]{:S(2)}) collective-permute-start(bf16[256,128]{1,0:T(8,128)(2,1)S(1)} %fusion.8), channel_id=1, source_target_pairs={{0,128},{32,160},{64,192},{96,224},{128,0},{160,32},{192,64},{224,... | collective-permute-start | bytes 196616 | tf_op jit(solution)/shard_map/ppermute | solution.py:218
  120.9 11.4 %collective-permute-start.19 = (bf16[2,512,128]{2,1,0:T(8,128)(2,1)S(1)}, bf16[2,512,128]{2,1,0:T(8,128)(2,1)S(1)}, u32[]{:S(2)}, u32[]{:S(2)}) collective-permute-start(bf16[2,512,128]{2,1,0:T(8,128)(2,1)S(1)} %add_convert_fusion.3), channel_id=1, source_target_pairs={{0,32},{32,64},{64,96},{96,128},{128,160},{160,192},{192,224},{224... | collective-permute-start | bytes 786440 | tf_op jit(solution)/shard_map/ppermute | solution.py:204
  126.0 6.6 %collective-permute-start.16 = (bf16[256,128]{1,0:T(8,128)(2,1)S(1)}, bf16[256,128]{1,0:T(8,128)(2,1)S(1)}, u32[]{:S(2)}, u32[]{:S(2)}) collective-permute-start(bf16[256,128]{1,0:T(8,128)(2,1)S(1)} %fusion.6), channel_id=1, source_target_pairs={{0,16},{16,0},{1,17},{17,1},{2,18},{18,2},{3,19},{19,3},{4,20},{20... | collective-permute-start | bytes 196616 | tf_op jit(solution)/shard_map/ppermute | solution.py:218
  128.0 11.2 %collective-permute-start.22 = (bf16[2,512,128]{2,1,0:T(8,128)(2,1)S(1)}, bf16[2,512,128]{2,1,0:T(8,128)(2,1)S(1)}, u32[]{:S(2)}, u32[]{:S(2)}) collective-permute-start(bf16[2,512,128]{2,1,0:T(8,128)(2,1)S(1)} %add_convert_fusion), channel_id=1, source_target_pairs={{0,224},{32,0},{64,32},{96,64},{128,96},{160,128},{192,160},{224,1... | collective-permute-start | bytes 786440 | tf_op jit(solution)/shard_map/ppermute | solution.py:204
  132.5 7.9 %collective-permute-start.20 = (bf16[2,512,128]{2,1,0:T(8,128)(2,1)S(1)}, bf16[2,512,128]{2,1,0:T(8,128)(2,1)S(1)}, u32[]{:S(2)}, u32[]{:S(2)}) collective-permute-start(bf16[2,512,128]{2,1,0:T(8,128)(2,1)S(1)} %add_convert_fusion.2), channel_id=1, source_target_pairs={{0,32},{32,64},{64,96},{96,128},{128,160},{160,192},{192,224},{224... | collective-permute-start | bytes 786440 | tf_op jit(solution)/shard_map/ppermute | solution.py:204
  140.4 39.2 %all-to-all-start.1 = ((bf16[8,896,128]{2,1,0:T(8,128)(2,1)}), bf16[8,896,128]{2,1,0:T(8,128)(2,1)S(1)}, u32[]{:S(2)}, u32[]{:S(2)}) async-start(bf16[8,896,128]{2,1,0:T(8,128)(2,1)} %shard_map.106), calls=%async_computation.1 | async-start | bytes 3670016 | tf_op jit(solution)/shard_map/all_to_all | solution.py:315
  145.3 33.4 %collective-permute-start.25 = (bf16[256,128]{1,0:T(8,128)(2,1)S(1)}, bf16[256,128]{1,0:T(8,128)(2,1)S(1)}, u32[]{:S(2)}, u32[]{:S(2)}) collective-permute-start(bf16[256,128]{1,0:T(8,128)(2,1)S(1)} %add_convert_fusion.6), channel_id=1, source_target_pairs={{0,0},{1,16},{2,32},{3,48},{4,64},{5,80},{6,96},{7,112},{8,128},{9... | collective-permute-start | bytes 196616 | tf_op jit(solution)/shard_map/ppermute | solution.py:316
  179.6 12.2 %collective-permute-start.23 = (bf16[512,128]{1,0:T(8,128)(2,1)}, bf16[512,128]{1,0:T(8,128)(2,1)S(1)}, u32[]{:S(2)}, u32[]{:S(2)}) collective-permute-start(bf16[512,128]{1,0:T(8,128)(2,1)} %fusion.4), channel_id=1, source_target_pairs={{0,16},{16,0},{1,17},{17,1},{2,18},{18,2},{3,19},{19,3},{4,20},{20... | collective-permute-start | bytes 393224 | tf_op jit(solution)/shard_map/ppermute | solution.py:218
  179.9 18.7 %collective-permute-start.26 = (f32[64,128]{1,0:T(8,128)S(1)}, f32[64,128]{1,0:T(8,128)S(1)}, u32[]{:S(2)}, u32[]{:S(2)}) collective-permute-start(f32[64,128]{1,0:T(8,128)S(1)} %slice.65), channel_id=1, source_target_pairs={{0,1},{1,0},{2,3},{3,2},{4,5},{5,4},{6,7},{7,6},{8,9},{9,8},{10,11... | collective-permute-start | bytes 98312 | tf_op jit(solution)/shard_map/ppermute | solution.py:218
  191.8 7.8 %collective-permute-start.24 = (bf16[512,128]{1,0:T(8,128)(2,1)S(1)}, bf16[512,128]{1,0:T(8,128)(2,1)S(1)}, u32[]{:S(2)}, u32[]{:S(2)}) collective-permute-start(bf16[512,128]{1,0:T(8,128)(2,1)S(1)} %fusion.2), channel_id=1, source_target_pairs={{0,0},{1,16},{2,32},{3,48},{4,64},{5,80},{6,96},{7,112},{8,128},{9... | collective-permute-start | bytes 393224 | tf_op jit(solution)/shard_map/ppermute | solution.py:314
Sparse Core Ops, SparseCore 0:
  10.7 45.3 all-gather.2

commit v3 on v2

--- a/solution.py
+++ b/solution.py
@@ -17,7 +17,6 @@
 TOK = 128
 RANK = 256
 RS = RANK // SH
-ROWS = FEAT + RS
 WROWS = FEAT + 16
 VROWS = WIDTH // TOK * RS
 UROWS = FEAT // TOK * RS
@@ -57,12 +56,12 @@
 
 def first_kernel(x, u, x_t, p):
     x_t[...] = x[...].T
-    p[...] = dot(u[...].T, x_t[...], NN).reshape(SH, RS, TOK)
+    p[...] = dot(u[...].T, x_t[...], NN)
 
 
 def forward_kernel(place, index, *refs):
     x_parts = refs[:NZ]
-    w, v, cot, hidden, dz_t, q_t, x, z_t, sems = refs[NZ:]
+    w, p_t, v, cot, hidden, dz_t, q_t, x, z_t, sems = refs[NZ:]
     copies = [
         pltpu.make_async_copy(x_parts[rel], x.at[2 * rel : 2 * rel + 2], sems.at[rel])
         for rel in range(NZ)
@@ -87,7 +86,7 @@
         return carry
 
     lax.fori_loop(0, SH, shard, 0)
-    p = jnp.concatenate([x[x_slot(place, s), FEAT:, :] for s in range(SH)], axis=0).T
+    p = p_t[...].T
     for j in range(WIDTH // TOK):
         part = slice(j * TOK, (j + 1) * TOK)
         z = z_t[part, :].T + dot(p, v[:, part], NN)
@@ -123,7 +122,7 @@
         outs[i][...] = done[2 * i : 2 * i + 2]
 
 
-def grad_rows(place, index, x, dz_t, out, half, other):
+def grad_rows(place, index, x, dz_t, p_t, out, half, other):
     core = place[2] ^ half
 
     def plus(value, k, first):
@@ -146,7 +145,7 @@
         return carry
 
     lax.fori_loop(0, NK, shard, 0)
-    p = jnp.concatenate([x[x_slot(place, 2 * k + core), FEAT:, :] for k in range(NK)], axis=0)
+    p = jnp.concatenate([p_t[2 * k + core] for k in range(NK)], axis=0)
     for j in range(WIDTH // TOK):
         part = dot(p, dz_t[j * TOK : (j + 1) * TOK, :], NT)
         first = FEAT + j * RS
@@ -154,24 +153,25 @@
             out[k, first : first + RS, :] = plus(part[k * RS : (k + 1) * RS], k, first)
 
 
-def grad_other_kernel(place, index, x, dz_t, out):
-    grad_rows(place, index, x, dz_t, out, 1, None)
-
-
-def grad_own_kernel(place, index, x, dz_t, q_t, other, out):
-    grad_rows(place, index, x, dz_t, out, 0, other)
+def grad_other_kernel(place, index, x, dz_t, p_t, out):
+    grad_rows(place, index, x, dz_t, p_t, out, 1, None)
+
+
+def grad_own_kernel(place, index, x, dz_t, p_t, other, out):
+    grad_rows(place, index, x, dz_t, p_t, out, 0, other)
+
+
+def u_kernel(place, x, q_t, out):
     q = q_t[place[3]]
 
-    def shard(k, carry):
-        for half in range(2):
-            slot = x_slot(place, 2 * k + (place[2] ^ half))
-            u = dot(q, x[slot, :FEAT, :], NT).astype(BF16)
-            for j in range(FEAT // TOK):
-                first = FEAT + VROWS + half * UROWS + j * RS
-                out[k, first : first + RS, :] = u[:, j * TOK : (j + 1) * TOK]
+    def shard(slot, carry):
+        u = dot(q, x[slot], NT).astype(BF16)
+        s = x_shard(place, slot)
+        for j in range(FEAT // TOK):
+            out[s, j * RS : (j + 1) * RS, :] = u[:, j * TOK : (j + 1) * TOK]
         return carry
 
-    lax.fori_loop(0, NK, shard, 0)
+    lax.fori_loop(0, SH, shard, 0)
 
 
 def call(kernel, out_shape, flops, bytes_accessed, operands, scratch=(), free=0, scalars=2):
@@ -204,15 +204,6 @@
     return lax.ppermute(x, "z", [(i, (i + by) % NZ) for i in range(NZ)])
 
 
-def gather_ring(own):
-    held = {0: own, -1: shift(own, 1), 1: shift(own, -1)}
-    for step in (1, 2):
-        held[-step - 1] = shift(held[-step], 1)
-        held[step + 1] = shift(held[step], -1)
-    held[4] = shift(held[-3], 1)
-    return [held[rel if rel <= 4 else rel - NZ] for rel in range(NZ)]
-
-
 def meet(x, axis, flip):
     count = {"z": 8, "xh": 2, "xl": 2, "y": 4, "core": 2}[axis]
     return lax.ppermute(x, axis, [(i, i ^ flip) for i in range(count)])
@@ -220,7 +211,6 @@
 
 def on_device(inputs, cotangent, sparse_blocks, block_index, u_factor, v_factor):
     turn = [(r * SH + c, c * SH + r) for r in range(SH) for c in range(SH)]
-    turn_pair = [(r * SH + c, (c ^ 1) * SH + r) for r in range(SH) for c in range(SH)]
     place = jnp.stack(
         [lax.axis_index("z"), lax.axis_index("xh"), lax.axis_index("core"), lax.axis_index(ROW)]
     ).astype(jnp.int32)
@@ -234,23 +224,26 @@
 
     mine, p = call(
         first_kernel,
-        (shape(FEAT, TOK), shape(SH, RS, TOK, kind=F32)),
+        (shape(FEAT, TOK), shape(RANK, TOK, kind=F32)),
         40_000_000,
         1 << 19,
         (inputs, u_factor),
         scalars=0,
     )
     turned = lax.ppermute(mine, ALL, turn)
-    p_in = lax.all_to_all(p, COL, 0, 0)
-    turned, p_in = lax.optimization_barrier((turned, p_in))
-    p = jnp.sum(p_in, axis=0).astype(BF16)
-    parts = [
-        turned,
-        lax.ppermute(p, ALL, turn),
-        meet(turned, "xh", 1),
-        lax.ppermute(p, ALL, turn_pair),
-    ]
-    x_parts = gather_ring(jnp.concatenate(parts).reshape(2, ROWS, TOK))
+    p = p + meet(p, "core", 1)
+    turned, p = lax.optimization_barrier((turned, p))
+    other, p_in = lax.optimization_barrier((meet(turned, "xh", 1), meet(p, "xl", 1)))
+    p = p + p_in
+    own = jnp.stack([turned, other])
+    held = {0: own}
+    for step, flip in ((1, 1), (2, 2), (3, 0)):
+        before, after = shift(held[1 - step], 1), shift(held[step - 1], -1)
+        p_in = meet(p, "y", flip) if flip else lax.ppermute(p.astype(BF16), ALL, turn)
+        held[-step], held[step], p_in = lax.optimization_barrier((before, after, p_in))
+        p = p + p_in if flip else p_in
+    held[4] = shift(held[-3], 1)
+    x_parts = [held[rel if rel <= 4 else rel - NZ] for rel in range(NZ)]
 
     hidden, dz_t, q, x_all = call(
         forward_kernel,
@@ -258,18 +251,16 @@
             shape(TOK, WIDTH),
             shape(WIDTH, TOK),
             shape(RANK, TOK, kind=F32),
-            shape(SH, ROWS, TOK),
+            shape(SH, FEAT, TOK),
         ),
         800_000_000,
         10 << 20,
-        (place, index, *x_parts, w_all, v_factor, cotangent),
+        (place, index, *x_parts, w_all, p, v_factor, cotangent),
         [pltpu.VMEM((WIDTH, TOK), F32), pltpu.SemaphoreType.DMA((NZ,))],
         free=NZ,
     )
 
-    back = {}
-    dz_back = dz_t
-    for slots in (range(6, 12), range(12, 22)):
+    def back_call(slots, dz_back):
         outs = call(
             functools.partial(back_kernel, slots),
             (shape(2, FEAT, TOK),) * (len(slots) // 2),
@@ -278,42 +269,62 @@
             (place, index, w_all, dz_back),
             [pltpu.VMEM((FEAT, TOK), F32), pltpu.VMEM((len(slots), FEAT, TOK), BF16)],
         )
-        back.update({slot // 2 % NZ: part for slot, part in zip(slots[::2], outs)})
-        dz_back, back[3] = lax.optimization_barrier((dz_back, back[3]))
-
+        return {slot // 2 % NZ: part for slot, part in zip(slots[::2], outs)}
+
+    back = back_call(range(6, 12), dz_t)
+    dz_t, q, back[3] = lax.optimization_barrier((dz_t, q, back[3]))
     up, down = shift(back[4], 1), shift(back[5], -1)
-    q, up, down, back[0] = lax.optimization_barrier((q, up, down, back[0]))
-    up = add(back[3], up)
-    for axis, flip in (("z", 1), ("z", 2), ("z", 4), ("xh", 1)):
-        q = q + meet(q.astype(BF16), axis, flip).astype(F32)
-    q_t = q.astype(BF16)
-
+    q_in = meet(q.astype(BF16), "z", 1)
+    back.update(back_call(range(12, 22), dz_t))
+    dz_t, q_in, back[0] = lax.optimization_barrier((dz_t, q_in, back[0]))
+
+    q = q + q_in.astype(F32)
+    q_in = meet(q.astype(BF16), "z", 2)
+    p_slices = p.reshape(SH, RS, TOK)
     grads = call(
         grad_other_kernel,
         shape(NK, FEAT + VROWS, TOK),
         200_000_000,
         4 << 20,
-        (place, index, x_all, dz_t),
-    )
+        (place, index, x_all, dz_t, p_slices),
+    )
+    up, down, q_in, grads = lax.optimization_barrier((up, down, q_in, grads))
+
+    grads_in = meet(grads, "core", 1)
+    up, down = shift(add(back[3], up), 1), shift(add(back[6], down), -1)
+    q = q + q_in.astype(F32)
+    q_in = meet(q.astype(BF16), "z", 4)
     grads = call(
         grad_own_kernel,
-        shape(NK, FEAT + VROWS + 2 * UROWS, TOK),
-        300_000_000,
+        shape(NK, FEAT + VROWS, TOK),
+        200_000_000,
         6 << 20,
-        (place, index, x_all, dz_t, q_t.reshape(SH, RS, TOK), meet(grads, "core", 1)),
-    )
-
-    down = add(back[6], down)
-    up = add(back[2], shift(up, 1))
-    down = add(back[7], shift(down, -1))
-    up = add(back[1], shift(up, 1))
-    up, down = shift(up, 1), shift(down, -1)
-    grads, up, down = lax.optimization_barrier((grads, up, down))
+        (place, index, x_all, dz_t, p_slices, grads_in),
+    )
+    up, down, q_in, grads = lax.optimization_barrier((up, down, q_in, grads))
+
+    grads_in = lax.all_to_all(grads, ("xl", "y"), 0, 0)
+    up, down = shift(add(back[2], up), 1), shift(add(back[7], down), -1)
+    q = q + q_in.astype(F32)
+    q_in = meet(q.astype(BF16), "xh", 1)
+    up, down, q_in = lax.optimization_barrier((up, down, q_in))
+
+    up = shift(add(back[1], up), 1)
+    q_t = (q + q_in.astype(F32)).astype(BF16)
+    u_part = call(
+        u_kernel,
+        shape(SH, UROWS, TOK),
+        70_000_000,
+        3 << 20,
+        (place, x_all, q_t.reshape(SH, RS, TOK)),
+        scalars=1,
+    )
+    up, u_part = lax.optimization_barrier((up, u_part))
     other = add(back[0][1], up[1], down[1])
     total = add(back[0][0], up[0], down[0], meet(other, "xh", 1))
     x_grad_t = lax.ppermute(total, ALL, turn)
-    grads_in = lax.all_to_all(grads, ("xl", "y"), 0, 0)
     q_turned = lax.ppermute(q_t, ALL, turn)
+    u_in = lax.all_to_all(u_part, COL, 0, 0)
 
     grads_sum = jnp.sum(grads_in.astype(F32), axis=0)
     blocks_grad = (
@@ -324,24 +335,22 @@
         .reshape(sparse_blocks.shape)
     )
     v_grad = (
-        grads_sum[FEAT : FEAT + VROWS]
+        grads_sum[FEAT:]
         .reshape(WIDTH // TOK, RS, TOK)
         .transpose(1, 0, 2)
         .reshape(RS, WIDTH)
     )
-    u_own = grads_sum[FEAT + VROWS : FEAT + VROWS + UROWS]
-    u_other = grads_sum[FEAT + VROWS + UROWS :]
     u_grad = (
-        (u_own + meet(u_other, "core", 1))
+        jnp.sum(u_in.astype(F32), axis=0)
         .reshape(FEAT // TOK, RS, TOK)
         .transpose(0, 2, 1)
         .reshape(FEAT, RS)
     )
+    x_grad_t, q_turned, blocks_grad, v_grad, u_grad = lax.optimization_barrier(
+        (x_grad_t, q_turned, blocks_grad, v_grad, u_grad)
+    )
     x_low = lax.dot_general(
         q_turned, u_factor, (((0,), (1,)), ((), ())), preferred_element_type=F32
-    )
-    x_grad_t, x_low, blocks_grad, v_grad, u_grad = lax.optimization_barrier(
-        (x_grad_t, x_low, blocks_grad, v_grad, u_grad)
     )
     input_grad = add(x_grad_t.T, x_low)
     return hidden, input_grad, blocks_grad, u_grad, v_grad

time: 208 us -> 215 us (1.034)
  waiting for transfers between devices: 76.6 us -> 81.8 us
    ppermute x8 -> x11, waiting for transfers between devices: 22.9 us -> 48.1 us  [meet(): return lax.ppermute(x, axis, [(i, i ^ flip) for i in range(count)])]
    ppermute x1, waiting for transfers between devices: 23.6 us -> 0.01 us  [on_device(): q_turned = lax.ppermute(q_t, ALL, turn)]
    ppermute x8 -> x11, starting transfers between devices: 9.27 us -> 15.6 us  [meet(): return lax.ppermute(x, axis, [(i, i ^ flip) for i in range(count)])]
    ppermute x1, waiting for transfers between devices: 0.01 us -> 6.13 us  [on_device(): turned = lax.ppermute(mine, ALL, turn)]
    ppermute x14, waiting for transfers between devices: 25.8 us -> 20 us  [shift(): return lax.ppermute(x, 'z', [(i, (i + by) % NZ) for i in range(NZ)])]
    ppermute x1, waiting for transfers between devices: 0.42 us -> 5.66 us  [on_device(): x_grad_t = lax.ppermute(total, ALL, turn)]
    ppermute x1, starting transfers between devices: 9.81 us -> 5.9 us  [on_device(): q_turned = lax.ppermute(q_t, ALL, turn)]
    ppermute x1, starting transfers between devices: 6.04 us -> 2.82 us  [on_device(): turned = lax.ppermute(mine, ALL, turn)]
  transfers between devices with their start and end apart: 29 -> 31, of which waited for: 14 -> 19; matrix products, arithmetic and copies ran while one was open for 3% -> 2% of each run, Pallas kernels for 7% -> 7%
where the time goes in v3:
time: 215 us; the launch traced here: 214 us
  waiting for transfers between devices  81.8 us (38%)
  starting transfers between devices  64.3 us (30%)
  Pallas kernels  26.5 us (12%)
  blocking collectives  17 us (8%)
  between operations  14.4 us (7%)
  local copies, waits for them, and re-layouts  8.41 us (4%)
    ppermute x11, waiting for transfers between devices, meet(): return lax.ppermute(x, axis, [(i, i ^ flip) for i in range(count)])  48.1 us
    pallas_call x7, Pallas kernels, call(): pl.pallas_call(kernel, out_shape=out_shape, in_specs=[smem] * scalars + [...  26.5 us
    ppermute x14, starting transfers between devices, shift(): return lax.ppermute(x, 'z', [(i, (i + by) % NZ) for i in range(NZ)])  21.3 us
    ppermute x14, waiting for transfers between devices, shift(): return lax.ppermute(x, 'z', [(i, (i + by) % NZ) for i in range(NZ)])  20 us
    all_to_all x1, blocking collectives, on_device(): u_in = lax.all_to_all(u_part, COL, 0, 0)  17 us
    ppermute x11, starting transfers between devices, meet(): return lax.ppermute(x, axis, [(i, i ^ flip) for i in range(count)])  15.6 us
    ppermute x1, starting transfers between devices, on_device(): lax.ppermute(p.astype(BF16), ALL, turn)  8.43 us
    ppermute x1, starting transfers between devices, on_device(): x_grad_t = lax.ppermute(total, ALL, turn)  6.69 us
  transfers between devices with their start and end apart: 31, of which 19 were waited for; matrix products, arithmetic and copies ran while one was open for 2% of the time, Pallas kernels for 7%

profile of v3, /device:TPU:1, one launch (start us, length us, event | category | flops | bytes accessed | tf_op | source)
XLA Modules:
  0.0 214.4 jit_solution(229477641494997266)
XLA Ops:
  7.2 0.7 convert_bitcast_fusion
  8.0 1.2 reshape.90
  9.7 0.8 copy.35
  10.8 3.3 %collective-permute-start.1 = (f32[256,128]{1,0:T(8,128)S(1)}, f32[256,128]{1,0:T(8,128)S(1)}, u32[]{:S(2)}, u32[]{:S(2)}) collective-permute-start(f32[256,128]{1,0:T(8,128)S(1)} %get-tuple-element.73), channel_id=1, source_target_pairs={{0,1},{1,0},{2,3},{3,2},{4,5},{5,4},{6,7},{7,6},{8,9},{9,8},{10,11... | collective-permute-start | bytes 393224 | tf_op jit(solution)/shard_map/ppermute | solution.py:209
  14.2 2.8 %collective-permute-start = (bf16[512,128]{1,0:T(8,128)(2,1)S(1)}, bf16[512,128]{1,0:T(8,128)(2,1)S(1)}, u32[]{:S(2)}, u32[]{:S(2)}) collective-permute-start(bf16[512,128]{1,0:T(8,128)(2,1)S(1)} %get-tuple-element.72), channel_id=1, source_target_pairs={{0,0},{1,16},{2,32},{3,48},{4,64},{5,80},{6,96},{7,112},{8,128},{9... | collective-permute-start | bytes 393224 | tf_op jit(solution)/shard_map/ppermute | solution.py:233
  17.0 6.1 %collective-permute-done = bf16[512,128]{1,0:T(8,128)(2,1)S(1)} collective-permute-done((bf16[512,128]{1,0:T(8,128)(2,1)S(1)}, bf16[512,128]{1,0:T(8,128)(2,1)S(1)}, u32[]{:S(2)}, u32[]{:S(2)}) %collective-permute-start) | collective-permute-done | bytes 131104 | tf_op jit(solution)/shard_map/ppermute | solution.py:233
  23.2 5.8 %collective-permute-start.3 = (f32[256,128]{1,0:T(8,128)S(1)}, f32[256,128]{1,0:T(8,128)S(1)}, u32[]{:S(2)}, u32[]{:S(2)}) collective-permute-start(f32[256,128]{1,0:T(8,128)S(1)} %add.71), channel_id=1, source_target_pairs={{0,8},{8,0},{1,9},{9,1},{2,10},{10,2},{3,11},{11,3},{4,12},{12,4},... | collective-permute-start | bytes 393224 | tf_op jit(solution)/shard_map/ppermute | solution.py:209
  28.9 9.0 %collective-permute-done.2 = bf16[512,128]{1,0:T(8,128)(2,1)S(1)} collective-permute-done((bf16[512,128]{1,0:T(8,128)(2,1)S(1)}, bf16[512,128]{1,0:T(8,128)(2,1)S(1)}, u32[]{:S(2)}, u32[]{:S(2)}) %collective-permute-start.2) | collective-permute-done | bytes 131104 | tf_op jit(solution)/shard_map/ppermute | solution.py:209
  37.9 3.2 %collective-permute-done.3 = f32[256,128]{1,0:T(8,128)S(1)} collective-permute-done((f32[256,128]{1,0:T(8,128)S(1)}, f32[256,128]{1,0:T(8,128)S(1)}, u32[]{:S(2)}, u32[]{:S(2)}) %collective-permute-start.3) | collective-permute-done | bytes 131104 | tf_op jit(solution)/shard_map/ppermute | solution.py:209
  41.2 6.4 %collective-permute-start.5 = (bf16[2,512,128]{2,1,0:T(8,128)(2,1)S(1)}, bf16[2,512,128]{2,1,0:T(8,128)(2,1)S(1)}, u32[]{:S(2)}, u32[]{:S(2)}) collective-permute-start(bf16[2,512,128]{2,1,0:T(8,128)(2,1)S(1)} %pad_maximum_fusion.refs_0_), channel_id=1, source_target_pairs={{0,224},{32,0},{64,32},{96,64},{128,96},{160,128},{192,160},{224,1... | collective-permute-start | bytes 786440 | tf_op jit(solution)/shard_map/ppermute | solution.py:204
  47.7 4.1 %collective-permute-done.6 = f32[256,128]{1,0:T(8,128)S(1)} collective-permute-done((f32[256,128]{1,0:T(8,128)S(1)}, f32[256,128]{1,0:T(8,128)S(1)}, u32[]{:S(2)}, u32[]{:S(2)}) %collective-permute-start.6) | collective-permute-done | bytes 131104 | tf_op jit(solution)/shard_map/ppermute | solution.py:209
  52.4 3.1 %collective-permute-done.4.refs_7_ = bf16[2,512,128]{2,1,0:T(8,128)(2,1)S(1)} collective-permute-done((bf16[2,512,128]{2,1,0:T(8,128)(2,1)S(1)}, bf16[2,512,128]{2,1,0:T(8,128)(2,1)S(1)}, u32[]{:S(2)}, u32[]{:S(2)}) %collective-permute-start.4) | collective-permute-done | bytes 262176 | tf_op jit(solution)/shard_map/ppermute | solution.py:204
  55.5 1.3 collective-permute-start.8
  57.0 5.3 %collective-permute-done.9 = f32[256,128]{1,0:T(8,128)S(1)} collective-permute-done((f32[256,128]{1,0:T(8,128)S(1)}, f32[256,128]{1,0:T(8,128)S(1)}, u32[]{:S(2)}, u32[]{:S(2)}) %collective-permute-start.9) | collective-permute-done | bytes 131104 | tf_op jit(solution)/shard_map/ppermute | solution.py:209
  62.4 1.8 collective-permute-done.7.refs_6_
  64.1 0.7 collective-permute-start.11
  64.8 0.8 collective-permute-start.10
  65.6 8.4 %collective-permute-start.12 = (bf16[256,128]{1,0:T(8,128)(2,1)S(1)}, bf16[256,128]{1,0:T(8,128)(2,1)S(1)}, u32[]{:S(2)}, u32[]{:S(2)}) collective-permute-start(bf16[256,128]{1,0:T(8,128)(2,1)S(1)} %add_convert_fusion.7), channel_id=1, source_target_pairs={{0,0},{1,16},{2,32},{3,48},{4,64},{5,80},{6,96},{7,112},{8,128},{9... | collective-permute-start | bytes 196616 | tf_op jit(solution)/shard_map/ppermute | solution.py:242
  74.1 1.9 collective-permute-done.12.refs_9_
  76.0 5.4 %collective-permute-start.13 = (bf16[2,512,128]{2,1,0:T(8,128)(2,1)}, bf16[2,512,128]{2,1,0:T(8,128)(2,1)}, u32[]{:S(2)}, u32[]{:S(2)}) collective-permute-start(bf16[2,512,128]{2,1,0:T(8,128)(2,1)} %collective-permute-done.10.refs_5_), channel_id=1, source_target_pairs={{0,32},{32,64},{64,96},{96,128},{128,160},{160,192},{192,224},{224... | collective-permute-start | bytes 786440 | tf_op jit(solution)/shard_map/ppermute | solution.py:204
  81.4 0.8 slice.53
  82.2 8.4 %collective-permute-done.13.refs_4_ = bf16[2,512,128]{2,1,0:T(8,128)(2,1)} collective-permute-done((bf16[2,512,128]{2,1,0:T(8,128)(2,1)}, bf16[2,512,128]{2,1,0:T(8,128)(2,1)}, u32[]{:S(2)}, u32[]{:S(2)}) %collective-permute-start.13) | collective-permute-done | bytes 262176 | tf_op jit(solution)/shard_map/ppermute | solution.py:204
  90.7 1.6 copy-done
  92.3 8.4 %shard_map.102 = (bf16[128,2048]{1,0:T(8,128)(2,1)}, bf16[2048,128]{1,0:T(8,128)(2,1)S(1)}, f32[256,128]{1,0:T(8,128)S(1)}, bf16[16,512,128]{2,1,0:T(8,128)(2,1)S(1)}) custom-call(s32[4]{0:T(128)S(1)} %pad_add_fusion.place, s32[16,16]{1,0:T(8,128)S(1)} %fusion.7.index, bf16[2,512,128]{2,1,0:T(8,128)(2,1)S(1)} %pad_maximum_fusion.refs_0_, ...), custom_call_target="tpu_custom_call" | custom-call | flops 800000000 | bytes 10485760 | tf_op jit(solution)/shard_map/pallas_call | solution.py:182
  100.7 2.4 %shard_map.103 = (bf16[2,512,128]{2,1,0:T(8,128)(2,1)S(1)}, bf16[2,512,128]{2,1,0:T(8,128)(2,1)S(1)}, bf16[2,512,128]{2,1,0:T(8,128)(2,1)S(1)}) custom-call(s32[4]{0:T(128)S(1)} %pad_add_fusion.place, s32[16,16]{1,0:T(8,128)S(1)} %fusion.7.index, bf16[16,528,128]{2,1,0:T(8,128)(2,1)S(1)} %bitcast.56, bf16[2048,128]{1,0:T(8,128)(2,1)S(1)} %get-tuple-element.102.dz_t), custom_call_target="tpu_custom_call" | custom-call | flops 120000000 | bytes 3145728 | tf_op jit(solution)/shard_map/pallas_call | solution.py:182
  103.3 1.5 collective-permute-start.15
  104.7 1.5 collective-permute-start.16
  106.2 3.6 %shard_map.104 = (bf16[2,512,128]{2,1,0:T(8,128)(2,1)S(1)}, bf16[2,512,128]{2,1,0:T(8,128)(2,1)S(1)}, bf16[2,512,128]{2,1,0:T(8,128)(2,1)S(1)}, bf16[2,512,128]{2,1,0:T(8,128)(2,1)S(1)}, bf16[2,512,128]{2,1,0:T(8,128)(2,1)S(1)}) custom-call(s32[4]{0:T(128)S(1)} %pad_add_fusion.place, s32[16,16]{1,0:T(8,128)S(1)} %fusion.7.index, ...), custom_call_target="tpu_custom_call" | custom-call | flops 200000000 | bytes 5242880 | tf_op jit(solution)/shard_map/pallas_call | solution.py:182
  109.9 3.8 %shard_map.105 = bf16[8,768,128]{2,1,0:T(8,128)(2,1)S(1)} custom-call(s32[4]{0:T(128)S(1)} %pad_add_fusion.place, s32[16,16]{1,0:T(8,128)S(1)} %fusion.7.index, bf16[16,512,128]{2,1,0:T(8,128)(2,1)S(1)} %get-tuple-element.101.x, bf16[2048,128]{1,0:T(8,128)(2,1)S(1)} %get-tuple-element.102.dz_t, bf16[16,16,128]{2,1,0:T(8,128)(2,1)S(1)} %bitcast.58), custom_call_target="tpu_custom_call" | custom-call | flops 200000000 | bytes 4194304 | tf_op jit(solution)/shard_map/pallas_call | solution.py:182
  114.4 3.9 %collective-permute-start.21 = (bf16[8,768,128]{2,1,0:T(8,128)(2,1)S(1)}, bf16[8,768,128]{2,1,0:T(8,128)(2,1)S(1)}, u32[]{:S(2)}, u32[]{:S(2)}) collective-permute-start(bf16[8,768,128]{2,1,0:T(8,128)(2,1)S(1)} %shard_map.105), channel_id=1, source_target_pairs={{0,1},{1,0},{2,3},{3,2},{4,5},{5,4},{6,7},{7,6},{8,9},{9,8},{10,11... | collective-permute-start | bytes 4718600 | tf_op jit(solution)/shard_map/ppermute | solution.py:209
  118.5 1.5 collective-permute-start.18
  120.1 1.9 collective-permute-start.20
  122.0 5.0 %shard_map.106 = bf16[8,768,128]{2,1,0:T(8,128)(2,1)} custom-call(s32[4]{0:T(128)S(1)} %pad_add_fusion.place, s32[16,16]{1,0:T(8,128)S(1)} %fusion.7.index, bf16[16,512,128]{2,1,0:T(8,128)(2,1)S(1)} %get-tuple-element.101.x, bf16[2048,128]{1,0:T(8,128)(2,1)S(1)} %get-tuple-element.102.dz_t, bf16[16,16,128]{2,1,0:T(8,128)(2,1)S(1)} %bitcast.59, ...), custom_call_target="tpu_custom_call" | custom-call | flops 200000000 | bytes 6291456 | tf_op jit(solution)/shard_map/pallas_call | solution.py:182
  127.0 2.1 collective-permute-done.20
  129.1 1.4 collective-permute-done.18
  130.9 1.3 collective-permute-start.22
  132.4 4.6 %collective-permute-done.24 = bf16[256,128]{1,0:T(8,128)(2,1)S(1)} collective-permute-done((bf16[256,128]{1,0:T(8,128)(2,1)S(1)}, bf16[256,128]{1,0:T(8,128)(2,1)S(1)}, u32[]{:S(2)}, u32[]{:S(2)}) %collective-permute-start.24) | collective-permute-done | bytes 65568 | tf_op jit(solution)/shard_map/ppermute | solution.py:209
  137.7 1.0 collective-permute-done.22
  139.2 3.0 %shard_map.107 = bf16[16,64,128]{2,1,0:T(8,128)(2,1)S(1)} custom-call(s32[4]{0:T(128)S(1)} %pad_add_fusion.place, bf16[16,512,128]{2,1,0:T(8,128)(2,1)S(1)} %get-tuple-element.101.x, bf16[16,16,128]{2,1,0:T(8,128)(2,1)S(1)} %bitcast.60), custom_call_target="tpu_custom_call" | custom-call | flops 70000000 | bytes 3145728 | tf_op jit(solution)/shard_map/pallas_call | solution.py:182
  142.2 3.1 %collective-permute-done.25 = bf16[2,512,128]{2,1,0:T(8,128)(2,1)S(1)} collective-permute-done((bf16[2,512,128]{2,1,0:T(8,128)(2,1)S(1)}, bf16[2,512,128]{2,1,0:T(8,128)(2,1)S(1)}, u32[]{:S(2)}, u32[]{:S(2)}) %collective-permute-start.25) | collective-permute-done | bytes 262176 | tf_op jit(solution)/shard_map/ppermute | solution.py:204
  145.3 17.0 %all_to_all.10 = bf16[16,64,128]{2,1,0:T(8,128)(2,1)S(1)} all-to-all(bf16[16,64,128]{2,1,0:T(8,128)(2,1)S(1)} %shard_map.107), channel_id=1, replica_groups=mesh['z'=8,'xh'=2,'xl'=2,'y'=4,'core'=2] {'xl','y','core'}, dimensions={0} | all-to-all | bytes 524288 | tf_op jit(solution)/shard_map/all_to_all | solution.py:327
  162.2 3.6 %all-to-all-start = ((bf16[8,768,128]{2,1,0:T(8,128)(2,1)}), bf16[8,768,128]{2,1,0:T(8,128)(2,1)S(1)}, u32[]{:S(2)}, u32[]{:S(2)}) async-start(bf16[8,768,128]{2,1,0:T(8,128)(2,1)} %shard_map.106), calls=%async_computation | async-start | bytes 3145728 | tf_op jit(solution)/shard_map/all_to_all | solution.py:306
  166.1 5.9 %collective-permute-start.28 = (bf16[256,128]{1,0:T(8,128)(2,1)S(1)}, bf16[256,128]{1,0:T(8,128)(2,1)S(1)}, u32[]{:S(2)}, u32[]{:S(2)}) collective-permute-start(bf16[256,128]{1,0:T(8,128)(2,1)S(1)} %add_convert_fusion.6), channel_id=1, source_target_pairs={{0,0},{1,16},{2,32},{3,48},{4,64},{5,80},{6,96},{7,112},{8,128},{9... | collective-permute-start | bytes 196616 | tf_op jit(solution)/shard_map/ppermute | solution.py:326
  172.0 19.1 %collective-permute-done.26 = bf16[512,128]{1,0:T(8,128)(2,1)S(1)} collective-permute-done((bf16[512,128]{1,0:T(8,128)(2,1)S(1)}, bf16[512,128]{1,0:T(8,128)(2,1)S(1)}, u32[]{:S(2)}, u32[]{:S(2)}) %collective-permute-start.26) | collective-permute-done | bytes 131104 | tf_op jit(solution)/shard_map/ppermute | solution.py:209
  191.1 6.7 %collective-permute-start.27 = (bf16[512,128]{1,0:T(8,128)(2,1)S(1)}, bf16[512,128]{1,0:T(8,128)(2,1)S(1)}, u32[]{:S(2)}, u32[]{:S(2)}) collective-permute-start(bf16[512,128]{1,0:T(8,128)(2,1)S(1)} %fusion.2), channel_id=1, source_target_pairs={{0,0},{1,16},{2,32},{3,48},{4,64},{5,80},{6,96},{7,112},{8,128},{9... | collective-permute-start | bytes 393224 | tf_op jit(solution)/shard_map/ppermute | solution.py:325
  200.0 0.9 reshape.95
  200.9 5.7 %collective-permute-done.27 = bf16[512,128]{1,0:T(8,128)(2,1)S(1)} collective-permute-done((bf16[512,128]{1,0:T(8,128)(2,1)S(1)}, bf16[512,128]{1,0:T(8,128)(2,1)S(1)}, u32[]{:S(2)}, u32[]{:S(2)}) %collective-permute-start.27) | collective-permute-done | bytes 131104 | tf_op jit(solution)/shard_map/ppermute | solution.py:325
  206.8 0.8 copy.42
  (74 shorter events, 7.6 us)
Async XLA Ops:
  7.2 3.3 %copy-start.5 = (bf16[128,512]{1,0:T(8,128)(2,1)S(1)}, bf16[128,512]{1,0:T(8,128)(2,1)}, u32[]{:S(2)}) copy-start(bf16[128,512]{1,0:T(8,128)(2,1)} %x.2) | copy-start | bytes 393220
  7.2 3.3 %copy-start.2 = (bf16[512,256]{1,0:T(8,128)(2,1)S(1)}, bf16[512,256]{1,0:T(8,128)(2,1)}, u32[]{:S(2)}) copy-start(bf16[512,256]{1,0:T(8,128)(2,1)} %u.1) | copy-start | bytes 786436
  7.2 74.2 %all-gather.3.cloned.1.call-start = ((), (), s32[]{:S(2)}) async-start(), calls=%async_computation.2 | async-start | bytes 2297856 | tf_op jit(solution)/shard_map/all_gather | solution.py:222
  9.6 81.0 %copy-start.3 = (bf16[256,2048]{1,0:T(8,128)(2,1)S(1)}, bf16[256,2048]{1,0:T(8,128)(2,1)}, u32[]{:S(2)}) copy-start(bf16[256,2048]{1,0:T(8,128)(2,1)} %refs_10_.1) | copy-start | bytes 3145732
  9.7 81.0 %copy-start.4 = (bf16[128,2048]{1,0:T(8,128)(2,1)S(1)}, bf16[128,2048]{1,0:T(8,128)(2,1)}, u32[]{:S(2)}) copy-start(bf16[128,2048]{1,0:T(8,128)(2,1)} %refs_11_.1) | copy-start | bytes 1572868
  10.8 6.2 %collective-permute-start.1 = (f32[256,128]{1,0:T(8,128)S(1)}, f32[256,128]{1,0:T(8,128)S(1)}, u32[]{:S(2)}, u32[]{:S(2)}) collective-permute-start(f32[256,128]{1,0:T(8,128)S(1)} %get-tuple-element.73), channel_id=1, source_target_pairs={{0,1},{1,0},{2,3},{3,2},{4,5},{5,4},{6,7},{7,6},{8,9},{9,8},{10,11... | collective-permute-start | bytes 393224 | tf_op jit(solution)/shard_map/ppermute | solution.py:209
  14.2 9.0 %collective-permute-start = (bf16[512,128]{1,0:T(8,128)(2,1)S(1)}, bf16[512,128]{1,0:T(8,128)(2,1)S(1)}, u32[]{:S(2)}, u32[]{:S(2)}) collective-permute-start(bf16[512,128]{1,0:T(8,128)(2,1)S(1)} %get-tuple-element.72), channel_id=1, source_target_pairs={{0,0},{1,16},{2,32},{3,48},{4,64},{5,80},{6,96},{7,112},{8,128},{9... | collective-permute-start | bytes 393224 | tf_op jit(solution)/shard_map/ppermute | solution.py:233
  23.1 14.8 %collective-permute-start.2 = (bf16[512,128]{1,0:T(8,128)(2,1)S(1)}, bf16[512,128]{1,0:T(8,128)(2,1)S(1)}, u32[]{:S(2)}, u32[]{:S(2)}) collective-permute-start(bf16[512,128]{1,0:T(8,128)(2,1)S(1)} %collective-permute-done), channel_id=1, source_target_pairs={{0,16},{16,0},{1,17},{17,1},{2,18},{18,2},{3,19},{19,3},{4,20},{20... | collective-permute-start | bytes 393224 | tf_op jit(solution)/shard_map/ppermute | solution.py:209
  23.2 18.0 %collective-permute-start.3 = (f32[256,128]{1,0:T(8,128)S(1)}, f32[256,128]{1,0:T(8,128)S(1)}, u32[]{:S(2)}, u32[]{:S(2)}) collective-permute-start(f32[256,128]{1,0:T(8,128)S(1)} %add.71), channel_id=1, source_target_pairs={{0,8},{8,0},{1,9},{9,1},{2,10},{10,2},{3,11},{11,3},{4,12},{12,4},... | collective-permute-start | bytes 393224 | tf_op jit(solution)/shard_map/ppermute | solution.py:209
  41.2 11.2 %collective-permute-start.5 = (bf16[2,512,128]{2,1,0:T(8,128)(2,1)S(1)}, bf16[2,512,128]{2,1,0:T(8,128)(2,1)S(1)}, u32[]{:S(2)}, u32[]{:S(2)}) collective-permute-start(bf16[2,512,128]{2,1,0:T(8,128)(2,1)S(1)} %pad_maximum_fusion.refs_0_), channel_id=1, source_target_pairs={{0,224},{32,0},{64,32},{96,64},{128,96},{160,128},{192,160},{224,1... | collective-permute-start | bytes 786440 | tf_op jit(solution)/shard_map/ppermute | solution.py:204
  47.6 7.9 %collective-permute-start.4 = (bf16[2,512,128]{2,1,0:T(8,128)(2,1)S(1)}, bf16[2,512,128]{2,1,0:T(8,128)(2,1)S(1)}, u32[]{:S(2)}, u32[]{:S(2)}) collective-permute-start(bf16[2,512,128]{2,1,0:T(8,128)(2,1)S(1)} %pad_maximum_fusion.refs_0_), channel_id=1, source_target_pairs={{0,32},{32,64},{64,96},{96,128},{128,160},{160,192},{192,224},{224... | collective-permute-start | bytes 786440 | tf_op jit(solution)/shard_map/ppermute | solution.py:204
  47.6 4.2 %collective-permute-start.6 = (f32[256,128]{1,0:T(8,128)S(1)}, f32[256,128]{1,0:T(8,128)S(1)}, u32[]{:S(2)}, u32[]{:S(2)}) collective-permute-start(f32[256,128]{1,0:T(8,128)S(1)} %add.72), channel_id=1, source_target_pairs={{0,2},{2,0},{4,6},{6,4},{1,3},{3,1},{5,7},{7,5},{8,10},{10,8},{12,... | collective-permute-start | bytes 393224 | tf_op jit(solution)/shard_map/ppermute | solution.py:209
  55.5 6.9 %collective-permute-start.8 = (bf16[2,512,128]{2,1,0:T(8,128)(2,1)S(1)}, bf16[2,512,128]{2,1,0:T(8,128)(2,1)S(1)}, u32[]{:S(2)}, u32[]{:S(2)}) collective-permute-start(bf16[2,512,128]{2,1,0:T(8,128)(2,1)S(1)} %collective-permute-done.5.refs_1_), channel_id=1, source_target_pairs={{0,224},{32,0},{64,32},{96,64},{128,96},{160,128},{192,160},{224,1... | collective-permute-start | bytes 786440 | tf_op jit(solution)/shard_map/ppermute | solution.py:204
  56.7 7.4 %collective-permute-start.7 = (bf16[2,512,128]{2,1,0:T(8,128)(2,1)S(1)}, bf16[2,512,128]{2,1,0:T(8,128)(2,1)S(1)}, u32[]{:S(2)}, u32[]{:S(2)}) collective-permute-start(bf16[2,512,128]{2,1,0:T(8,128)(2,1)S(1)} %collective-permute-done.4.refs_7_), channel_id=1, source_target_pairs={{0,32},{32,64},{64,96},{96,128},{128,160},{160,192},{192,224},{224... | collective-permute-start | bytes 786440 | tf_op jit(solution)/shard_map/ppermute | solution.py:204
  56.9 5.4 %collective-permute-start.9 = (f32[256,128]{1,0:T(8,128)S(1)}, f32[256,128]{1,0:T(8,128)S(1)}, u32[]{:S(2)}, u32[]{:S(2)}) collective-permute-start(f32[256,128]{1,0:T(8,128)S(1)} %add.73), channel_id=1, source_target_pairs={{0,4},{2,6},{4,0},{6,2},{1,5},{3,7},{5,1},{7,3},{8,12},{10,14},{12... | collective-permute-start | bytes 393224 | tf_op jit(solution)/shard_map/ppermute | solution.py:209
  64.1 11.9 %collective-permute-start.11 = (bf16[2,512,128]{2,1,0:T(8,128)(2,1)S(1)}, bf16[2,512,128]{2,1,0:T(8,128)(2,1)S(1)}, u32[]{:S(2)}, u32[]{:S(2)}) collective-permute-start(bf16[2,512,128]{2,1,0:T(8,128)(2,1)S(1)} %collective-permute-done.8.refs_2_), channel_id=1, source_target_pairs={{0,224},{32,0},{64,32},{96,64},{128,96},{160,128},{192,160},{224,1... | collective-permute-start | bytes 786440 | tf_op jit(solution)/shard_map/ppermute | solution.py:204
  64.8 11.1 %collective-permute-start.10 = (bf16[2,512,128]{2,1,0:T(8,128)(2,1)S(1)}, bf16[2,512,128]{2,1,0:T(8,128)(2,1)}, u32[]{:S(2)}, u32[]{:S(2)}) collective-permute-start(bf16[2,512,128]{2,1,0:T(8,128)(2,1)S(1)} %collective-permute-done.7.refs_6_), channel_id=1, source_target_pairs={{0,32},{32,64},{64,96},{96,128},{128,160},{160,192},{192,224},{224... | collective-permute-start | bytes 786440 | tf_op jit(solution)/shard_map/ppermute | solution.py:204
  65.6 10.4 %collective-permute-start.12 = (bf16[256,128]{1,0:T(8,128)(2,1)S(1)}, bf16[256,128]{1,0:T(8,128)(2,1)S(1)}, u32[]{:S(2)}, u32[]{:S(2)}) collective-permute-start(bf16[256,128]{1,0:T(8,128)(2,1)S(1)} %add_convert_fusion.7), channel_id=1, source_target_pairs={{0,0},{1,16},{2,32},{3,48},{4,64},{5,80},{6,96},{7,112},{8,128},{9... | collective-permute-start | bytes 196616 | tf_op jit(solution)/shard_map/ppermute | solution.py:242
  76.0 14.7 %collective-permute-start.13 = (bf16[2,512,128]{2,1,0:T(8,128)(2,1)}, bf16[2,512,128]{2,1,0:T(8,128)(2,1)}, u32[]{:S(2)}, u32[]{:S(2)}) collective-permute-start(bf16[2,512,128]{2,1,0:T(8,128)(2,1)} %collective-permute-done.10.refs_5_), channel_id=1, source_target_pairs={{0,32},{32,64},{64,96},{96,128},{128,160},{160,192},{192,224},{224... | collective-permute-start | bytes 786440 | tf_op jit(solution)/shard_map/ppermute | solution.py:204
  90.7 1.6 copy-start
  92.3 8.4 %copy-start.1 = (bf16[8448,128]{1,0:T(8,128)(2,1)S(1)}, bf16[8448,128]{1,0:T(8,128)(2,1)}, u32[]{:S(2)}) copy-start(bf16[8448,128]{1,0:T(8,128)(2,1)} %all-gather.3.cloned.1.call-done) | copy-start | bytes 6488068
  103.2 6.6 %collective-permute-start.14 = (bf16[256,128]{1,0:T(8,128)(2,1)S(1)}, bf16[256,128]{1,0:T(8,128)(2,1)S(1)}, u32[]{:S(2)}, u32[]{:S(2)}) collective-permute-start(bf16[256,128]{1,0:T(8,128)(2,1)S(1)} %convert_element_type.148), channel_id=1, source_target_pairs={{0,32},{32,0},{64,96},{96,64},{128,160},{160,128},{192,224},{224,1... | collective-permute-start | bytes 196616 | tf_op jit(solution)/shard_map/ppermute | solution.py:209
  103.3 11.1 %collective-permute-start.15 = (bf16[2,512,128]{2,1,0:T(8,128)(2,1)S(1)}, bf16[2,512,128]{2,1,0:T(8,128)(2,1)S(1)}, u32[]{:S(2)}, u32[]{:S(2)}) collective-permute-start(bf16[2,512,128]{2,1,0:T(8,128)(2,1)S(1)} %get-tuple-element.98), channel_id=1, source_target_pairs={{0,32},{32,64},{64,96},{96,128},{128,160},{160,192},{192,224},{224... | collective-permute-start | bytes 786440 | tf_op jit(solution)/shard_map/ppermute | solution.py:204
  104.7 9.7 %collective-permute-start.16 = (bf16[2,512,128]{2,1,0:T(8,128)(2,1)S(1)}, bf16[2,512,128]{2,1,0:T(8,128)(2,1)S(1)}, u32[]{:S(2)}, u32[]{:S(2)}) collective-permute-start(bf16[2,512,128]{2,1,0:T(8,128)(2,1)S(1)} %get-tuple-element.99), channel_id=1, source_target_pairs={{0,224},{32,0},{64,32},{96,64},{128,96},{160,128},{192,160},{224,1... | collective-permute-start | bytes 786440 | tf_op jit(solution)/shard_map/ppermute | solution.py:204
  109.8 4.5 %collective-permute-start.17 = (bf16[256,128]{1,0:T(8,128)(2,1)S(1)}, bf16[256,128]{1,0:T(8,128)(2,1)S(1)}, u32[]{:S(2)}, u32[]{:S(2)}) collective-permute-start(bf16[256,128]{1,0:T(8,128)(2,1)S(1)} %fusion.5), channel_id=1, source_target_pairs={{0,64},{32,96},{64,0},{96,32},{128,192},{160,224},{192,128},{224,1... | collective-permute-start | bytes 196616 | tf_op jit(solution)/shard_map/ppermute | solution.py:209
  114.4 7.6 %collective-permute-start.21 = (bf16[8,768,128]{2,1,0:T(8,128)(2,1)S(1)}, bf16[8,768,128]{2,1,0:T(8,128)(2,1)S(1)}, u32[]{:S(2)}, u32[]{:S(2)}) collective-permute-start(bf16[8,768,128]{2,1,0:T(8,128)(2,1)S(1)} %shard_map.105), channel_id=1, source_target_pairs={{0,1},{1,0},{2,3},{3,2},{4,5},{5,4},{6,7},{7,6},{8,9},{9,8},{10,11... | collective-permute-start | bytes 4718600 | tf_op jit(solution)/shard_map/ppermute | solution.py:209
  118.3 10.8 %collective-permute-start.19 = (bf16[2,512,128]{2,1,0:T(8,128)(2,1)S(1)}, bf16[2,512,128]{2,1,0:T(8,128)(2,1)S(1)}, u32[]{:S(2)}, u32[]{:S(2)}) collective-permute-start(bf16[2,512,128]{2,1,0:T(8,128)(2,1)S(1)} %add_convert_fusion.3), channel_id=1, source_target_pairs={{0,224},{32,0},{64,32},{96,64},{128,96},{160,128},{192,160},{224,1... | collective-permute-start | bytes 786440 | tf_op jit(solution)/shard_map/ppermute | solution.py:204
  118.5 12.0 %collective-permute-start.18 = (bf16[2,512,128]{2,1,0:T(8,128)(2,1)S(1)}, bf16[2,512,128]{2,1,0:T(8,128)(2,1)S(1)}, u32[]{:S(2)}, u32[]{:S(2)}) collective-permute-start(bf16[2,512,128]{2,1,0:T(8,128)(2,1)S(1)} %add_convert_fusion.4), channel_id=1, source_target_pairs={{0,32},{32,64},{64,96},{96,128},{128,160},{160,192},{192,224},{224... | collective-permute-start | bytes 786440 | tf_op jit(solution)/shard_map/ppermute | solution.py:204
  120.1 9.1 %collective-permute-start.20 = (bf16[256,128]{1,0:T(8,128)(2,1)S(1)}, bf16[256,128]{1,0:T(8,128)(2,1)S(1)}, u32[]{:S(2)}, u32[]{:S(2)}) collective-permute-start(bf16[256,128]{1,0:T(8,128)(2,1)S(1)} %fusion.8), channel_id=1, source_target_pairs={{0,128},{32,160},{64,192},{96,224},{128,0},{160,32},{192,64},{224,... | collective-permute-start | bytes 196616 | tf_op jit(solution)/shard_map/ppermute | solution.py:209
  130.6 7.1 %collective-permute-start.23 = (bf16[2,512,128]{2,1,0:T(8,128)(2,1)S(1)}, bf16[2,512,128]{2,1,0:T(8,128)(2,1)S(1)}, u32[]{:S(2)}, u32[]{:S(2)}) collective-permute-start(bf16[2,512,128]{2,1,0:T(8,128)(2,1)S(1)} %add_convert_fusion.1), channel_id=1, source_target_pairs={{0,224},{32,0},{64,32},{96,64},{128,96},{160,128},{192,160},{224,1... | collective-permute-start | bytes 786440 | tf_op jit(solution)/shard_map/ppermute | solution.py:204
  130.9 7.7 %collective-permute-start.22 = (bf16[2,512,128]{2,1,0:T(8,128)(2,1)S(1)}, bf16[2,512,128]{2,1,0:T(8,128)(2,1)S(1)}, u32[]{:S(2)}, u32[]{:S(2)}) collective-permute-start(bf16[2,512,128]{2,1,0:T(8,128)(2,1)S(1)} %add_convert_fusion.2), channel_id=1, source_target_pairs={{0,32},{32,64},{64,96},{96,128},{128,160},{160,192},{192,224},{224... | collective-permute-start | bytes 786440 | tf_op jit(solution)/shard_map/ppermute | solution.py:204
  132.3 4.7 %collective-permute-start.24 = (bf16[256,128]{1,0:T(8,128)(2,1)S(1)}, bf16[256,128]{1,0:T(8,128)(2,1)S(1)}, u32[]{:S(2)}, u32[]{:S(2)}) collective-permute-start(bf16[256,128]{1,0:T(8,128)(2,1)S(1)} %fusion.6), channel_id=1, source_target_pairs={{0,16},{16,0},{1,17},{17,1},{2,18},{18,2},{3,19},{19,3},{4,20},{20... | collective-permute-start | bytes 196616 | tf_op jit(solution)/shard_map/ppermute | solution.py:209
  138.7 6.5 %collective-permute-start.25 = (bf16[2,512,128]{2,1,0:T(8,128)(2,1)S(1)}, bf16[2,512,128]{2,1,0:T(8,128)(2,1)S(1)}, u32[]{:S(2)}, u32[]{:S(2)}) collective-permute-start(bf16[2,512,128]{2,1,0:T(8,128)(2,1)S(1)} %add_convert_fusion), channel_id=1, source_target_pairs={{0,32},{32,64},{64,96},{96,128},{128,160},{160,192},{192,224},{224... | collective-permute-start | bytes 786440 | tf_op jit(solution)/shard_map/ppermute | solution.py:204
  162.2 36.3 %all-to-all-start = ((bf16[8,768,128]{2,1,0:T(8,128)(2,1)}), bf16[8,768,128]{2,1,0:T(8,128)(2,1)S(1)}, u32[]{:S(2)}, u32[]{:S(2)}) async-start(bf16[8,768,128]{2,1,0:T(8,128)(2,1)} %shard_map.106), calls=%async_computation | async-start | bytes 3145728 | tf_op jit(solution)/shard_map/all_to_all | solution.py:306
  165.9 25.2 %collective-permute-start.26 = (bf16[512,128]{1,0:T(8,128)(2,1)S(1)}, bf16[512,128]{1,0:T(8,128)(2,1)S(1)}, u32[]{:S(2)}, u32[]{:S(2)}) collective-permute-start(bf16[512,128]{1,0:T(8,128)(2,1)S(1)} %fusion.4), channel_id=1, source_target_pairs={{0,16},{16,0},{1,17},{17,1},{2,18},{18,2},{3,19},{19,3},{4,20},{20... | collective-permute-start | bytes 393224 | tf_op jit(solution)/shard_map/ppermute | solution.py:209
  166.1 34.8 %collective-permute-start.28 = (bf16[256,128]{1,0:T(8,128)(2,1)S(1)}, bf16[256,128]{1,0:T(8,128)(2,1)S(1)}, u32[]{:S(2)}, u32[]{:S(2)}) collective-permute-start(bf16[256,128]{1,0:T(8,128)(2,1)S(1)} %add_convert_fusion.6), channel_id=1, source_target_pairs={{0,0},{1,16},{2,32},{3,48},{4,64},{5,80},{6,96},{7,112},{8,128},{9... | collective-permute-start | bytes 196616 | tf_op jit(solution)/shard_map/ppermute | solution.py:326
  191.1 15.5 %collective-permute-start.27 = (bf16[512,128]{1,0:T(8,128)(2,1)S(1)}, bf16[512,128]{1,0:T(8,128)(2,1)S(1)}, u32[]{:S(2)}, u32[]{:S(2)}) collective-permute-start(bf16[512,128]{1,0:T(8,128)(2,1)S(1)} %fusion.2), channel_id=1, source_target_pairs={{0,0},{1,16},{2,32},{3,48},{4,64},{5,80},{6,96},{7,112},{8,128},{9... | collective-permute-start | bytes 393224 | tf_op jit(solution)/shard_map/ppermute | solution.py:325
Sparse Core Ops, SparseCore 0:
  10.6 44.9 all-gather.2

commit v4 on v2

--- a/solution.py
+++ b/solution.py
@@ -204,15 +204,6 @@
     return lax.ppermute(x, "z", [(i, (i + by) % NZ) for i in range(NZ)])
 
 
-def gather_ring(own):
-    held = {0: own, -1: shift(own, 1), 1: shift(own, -1)}
-    for step in (1, 2):
-        held[-step - 1] = shift(held[-step], 1)
-        held[step + 1] = shift(held[step], -1)
-    held[4] = shift(held[-3], 1)
-    return [held[rel if rel <= 4 else rel - NZ] for rel in range(NZ)]
-
-
 def meet(x, axis, flip):
     count = {"z": 8, "xh": 2, "xl": 2, "y": 4, "core": 2}[axis]
     return lax.ppermute(x, axis, [(i, i ^ flip) for i in range(count)])
@@ -230,7 +221,6 @@
     w_mine = jnp.concatenate([w_pairs, index_row])
     w_mine, inputs = lax.optimization_barrier((w_mine, inputs))
     w_all = lax.all_gather(w_mine, COL, axis=0)
-    index = w_all[:, FEAT, :NB].astype(jnp.int32)
 
     mine, p = call(
         first_kernel,
@@ -250,7 +240,14 @@
         meet(turned, "xh", 1),
         lax.ppermute(p, ALL, turn_pair),
     ]
-    x_parts = gather_ring(jnp.concatenate(parts).reshape(2, ROWS, TOK))
+    held = {0: jnp.concatenate(parts).reshape(2, ROWS, TOK)}
+    for step in (1, 2, 3):
+        held[-step], held[step] = shift(held[1 - step], 1), shift(held[step - 1], -1)
+        if step == 2:
+            w_all, held[-2], held[2] = lax.optimization_barrier((w_all, held[-2], held[2]))
+    held[4] = shift(held[-3], 1)
+    x_parts = [held[rel if rel <= 4 else rel - NZ] for rel in range(NZ)]
+    index = w_all[:, FEAT, :NB].astype(jnp.int32)
 
     hidden, dz_t, q, x_all = call(
         forward_kernel,
@@ -267,9 +264,7 @@
         free=NZ,
     )
 
-    back = {}
-    dz_back = dz_t
-    for slots in (range(6, 12), range(12, 22)):
+    def back_call(slots, dz_back):
         outs = call(
             functools.partial(back_kernel, slots),
             (shape(2, FEAT, TOK),) * (len(slots) // 2),
@@ -278,16 +273,20 @@
             (place, index, w_all, dz_back),
             [pltpu.VMEM((FEAT, TOK), F32), pltpu.VMEM((len(slots), FEAT, TOK), BF16)],
         )
-        back.update({slot // 2 % NZ: part for slot, part in zip(slots[::2], outs)})
-        dz_back, back[3] = lax.optimization_barrier((dz_back, back[3]))
+        return {slot // 2 % NZ: part for slot, part in zip(slots[::2], outs)}
+
+    q_in = meet(q.astype(BF16), "z", 1)
+    back = back_call(range(6, 12), dz_t)
+    dz_t, q_in, back[3] = lax.optimization_barrier((dz_t, q_in, back[3]))
 
     up, down = shift(back[4], 1), shift(back[5], -1)
-    q, up, down, back[0] = lax.optimization_barrier((q, up, down, back[0]))
-    up = add(back[3], up)
-    for axis, flip in (("z", 1), ("z", 2), ("z", 4), ("xh", 1)):
-        q = q + meet(q.astype(BF16), axis, flip).astype(F32)
-    q_t = q.astype(BF16)
-
+    q = q + q_in.astype(F32)
+    q_in = meet(q.astype(BF16), "z", 2)
+    back.update(back_call(range(12, 22), dz_t))
+    dz_t, q_in, back[0] = lax.optimization_barrier((dz_t, q_in, back[0]))
+
+    q = q + q_in.astype(F32)
+    q_in = meet(q.astype(BF16), "z", 4)
     grads = call(
         grad_other_kernel,
         shape(NK, FEAT + VROWS, TOK),
@@ -295,20 +294,26 @@
         4 << 20,
         (place, index, x_all, dz_t),
     )
+    up, down, q_in, grads = lax.optimization_barrier((up, down, q_in, grads))
+
+    grads_in = meet(grads, "core", 1)
+    up, down = shift(add(back[3], up), 1), shift(add(back[6], down), -1)
+    q = q + q_in.astype(F32)
+    q_in = meet(q.astype(BF16), "xh", 1)
+    up, down, q_in, grads_in = lax.optimization_barrier((up, down, q_in, grads_in))
+
+    up, down = shift(add(back[2], up), 1), shift(add(back[7], down), -1)
+    q_t = (q + q_in.astype(F32)).astype(BF16)
     grads = call(
         grad_own_kernel,
         shape(NK, FEAT + VROWS + 2 * UROWS, TOK),
         300_000_000,
         6 << 20,
-        (place, index, x_all, dz_t, q_t.reshape(SH, RS, TOK), meet(grads, "core", 1)),
-    )
-
-    down = add(back[6], down)
-    up = add(back[2], shift(up, 1))
-    down = add(back[7], shift(down, -1))
-    up = add(back[1], shift(up, 1))
-    up, down = shift(up, 1), shift(down, -1)
-    grads, up, down = lax.optimization_barrier((grads, up, down))
+        (place, index, x_all, dz_t, q_t.reshape(SH, RS, TOK), grads_in),
+    )
+    up, down, grads = lax.optimization_barrier((up, down, grads))
+
+    up = shift(add(back[1], up), 1)
     other = add(back[0][1], up[1], down[1])
     total = add(back[0][0], up[0], down[0], meet(other, "xh", 1))
     x_grad_t = lax.ppermute(total, ALL, turn)
@@ -337,11 +342,11 @@
         .transpose(0, 2, 1)
         .reshape(FEAT, RS)
     )
+    x_grad_t, q_turned, blocks_grad, v_grad, u_grad = lax.optimization_barrier(
+        (x_grad_t, q_turned, blocks_grad, v_grad, u_grad)
+    )
     x_low = lax.dot_general(
         q_turned, u_factor, (((0,), (1,)), ((), ())), preferred_element_type=F32
-    )
-    x_grad_t, x_low, blocks_grad, v_grad, u_grad = lax.optimization_barrier(
-        (x_grad_t, x_low, blocks_grad, v_grad, u_grad)
     )
     input_grad = add(x_grad_t.T, x_low)
     return hidden, input_grad, blocks_grad, u_grad, v_grad

time: 208 us -> 196 us (0.942)
  waiting for transfers between devices: 76.6 us -> 52.5 us
  starting transfers between devices: 63.7 us -> 75.9 us
    ppermute x1, waiting for transfers between devices: 23.6 us -> 0.01 us  [on_device(): q_turned = lax.ppermute(q_t, ALL, turn)]
    ppermute x8, waiting for transfers between devices: 22.9 us -> 8.41 us  [meet(): return lax.ppermute(x, axis, [(i, i ^ flip) for i in range(count)])]
    ppermute x8, starting transfers between devices: 9.27 us -> 23 us  [meet(): return lax.ppermute(x, axis, [(i, i ^ flip) for i in range(count)])]
    all_to_all x1, waiting for transfers between devices: 0.01 us -> 10.5 us  [on_device(): grads_in = lax.all_to_all(grads, ('xl', 'y'), 0, 0)]
    ppermute x1, waiting for transfers between devices: 0.42 us -> 5.82 us  [on_device(): x_grad_t = lax.ppermute(total, ALL, turn)]
    optimization_barrier x1, local copies, waits for them, and re-layouts: 0.12 us -> 2.32 us  [on_device(): lax.optimization_barrier((w_all, held[-2], held[2]))]
  transfers between devices with their start and end apart: 29 -> 29, of which waited for: 14 -> 15; matrix products, arithmetic and copies ran while one was open for 3% -> 3% of each run, Pallas kernels for 7% -> 9%
where the time goes in v4:
time: 196 us; the launch traced here: 195 us
  starting transfers between devices  75.9 us (39%)
  waiting for transfers between devices  52.5 us (27%)
  Pallas kernels  24.5 us (12%)
  blocking collectives  16.1 us (8%)
  between operations  14.4 us (7%)
  local copies, waits for them, and re-layouts  9.97 us (5%)
    pallas_call x6, Pallas kernels, call(): pl.pallas_call(kernel, out_shape=out_shape, in_specs=[smem] * scalars + [...  24.5 us
    ppermute x14, waiting for transfers between devices, shift(): return lax.ppermute(x, 'z', [(i, (i + by) % NZ) for i in range(NZ)])  23.9 us
    ppermute x8, starting transfers between devices, meet(): return lax.ppermute(x, axis, [(i, i ^ flip) for i in range(count)])  23 us
    ppermute x14, starting transfers between devices, shift(): return lax.ppermute(x, 'z', [(i, (i + by) % NZ) for i in range(NZ)])  22 us
    all_to_all x1, blocking collectives, on_device(): p_in = lax.all_to_all(p, COL, 0, 0)  16.1 us
    all_to_all x1, waiting for transfers between devices, on_device(): grads_in = lax.all_to_all(grads, ('xl', 'y'), 0, 0)  10.5 us
    ppermute x1, starting transfers between devices, on_device(): q_turned = lax.ppermute(q_t, ALL, turn)  9.41 us
    ppermute x8, waiting for transfers between devices, meet(): return lax.ppermute(x, axis, [(i, i ^ flip) for i in range(count)])  8.41 us
  transfers between devices with their start and end apart: 29, of which 15 were waited for; matrix products, arithmetic and copies ran while one was open for 3% of the time, Pallas kernels for 9%

profile of v4, /device:TPU:1, one launch (start us, length us, event | category | flops | bytes accessed | tf_op | source)
XLA Modules:
  0.0 195.4 jit_solution(11704235105727267461)
XLA Ops:
  7.2 0.7 convert_bitcast_fusion
  8.0 1.2 reshape.90
  9.6 0.8 copy.35
  10.5 0.9 copy-done.4
  11.7 6.0 %collective-permute-start = (bf16[512,128]{1,0:T(8,128)(2,1)S(1)}, bf16[512,128]{1,0:T(8,128)(2,1)S(1)}, u32[]{:S(2)}, u32[]{:S(2)}) collective-permute-start(bf16[512,128]{1,0:T(8,128)(2,1)S(1)} %get-tuple-element.62), channel_id=1, source_target_pairs={{0,0},{1,16},{2,32},{3,48},{4,64},{5,80},{6,96},{7,112},{8,128},{9... | collective-permute-start | bytes 393224 | tf_op jit(solution)/shard_map/ppermute | solution.py:233
  17.7 16.1 %all_to_all.10 = f32[16,16,128]{2,1,0:T(8,128)S(1)} all-to-all(f32[16,16,128]{2,1,0:T(8,128)S(1)} %get-tuple-element.63), channel_id=1, replica_groups=mesh['z'=8,'xh'=2,'xl'=2,'y'=4,'core'=2] {'xl','y','core'}, dimensions={0} | all-to-all | bytes 262144 | tf_op jit(solution)/shard_map/all_to_all | solution.py:234
  33.9 1.9 collective-permute-start.2
  35.7 4.0 %collective-permute-start.1 = (bf16[16,128]{1,0:T(8,128)(2,1)S(1)}, bf16[16,128]{1,0:T(8,128)(2,1)S(1)}, u32[]{:S(2)}, u32[]{:S(2)}) collective-permute-start(bf16[16,128]{1,0:T(8,128)(2,1)S(1)} %reduce_sum.18), channel_id=1, source_target_pairs={{0,0},{1,16},{2,32},{3,48},{4,64},{5,80},{6,96},{7,112},{8,128},{9... | collective-permute-start | bytes 12296 | tf_op jit(solution)/shard_map/ppermute | solution.py:239
  39.9 2.3 %collective-permute-done.1 = bf16[16,128]{1,0:T(8,128)(2,1)S(1)} collective-permute-done((bf16[16,128]{1,0:T(8,128)(2,1)S(1)}, bf16[16,128]{1,0:T(8,128)(2,1)S(1)}, u32[]{:S(2)}, u32[]{:S(2)}) %collective-permute-start.1) | collective-permute-done | bytes 4128 | tf_op jit(solution)/shard_map/ppermute | solution.py:239
  42.2 1.7 collective-permute-done.3
  43.9 9.8 %collective-permute-start.6 = (bf16[2,528,128]{2,1,0:T(8,128)(2,1)S(1)}, bf16[2,528,128]{2,1,0:T(8,128)(2,1)S(1)}, u32[]{:S(2)}, u32[]{:S(2)}) collective-permute-start(bf16[2,528,128]{2,1,0:T(8,128)(2,1)S(1)} %bitcast.56), channel_id=1, source_target_pairs={{0,224},{32,0},{64,32},{96,64},{128,96},{160,128},{192,160},{224,1... | collective-permute-start | bytes 811016 | tf_op jit(solution)/shard_map/ppermute | solution.py:204
  53.6 5.3 %collective-permute-done.6.refs_1_ = bf16[2,528,128]{2,1,0:T(8,128)(2,1)S(1)} collective-permute-done((bf16[2,528,128]{2,1,0:T(8,128)(2,1)S(1)}, bf16[2,528,128]{2,1,0:T(8,128)(2,1)S(1)}, u32[]{:S(2)}, u32[]{:S(2)}) %collective-permute-start.6) | collective-permute-done | bytes 270368 | tf_op jit(solution)/shard_map/ppermute | solution.py:204
  59.0 3.4 %collective-permute-start.7 = (bf16[2,528,128]{2,1,0:T(8,128)(2,1)S(1)}, bf16[2,528,128]{2,1,0:T(8,128)(2,1)S(1)}, u32[]{:S(2)}, u32[]{:S(2)}) collective-permute-start(bf16[2,528,128]{2,1,0:T(8,128)(2,1)S(1)} %collective-permute-done.6.refs_1_), channel_id=1, source_target_pairs={{0,224},{32,0},{64,32},{96,64},{128,96},{160,128},{192,160},{224,1... | collective-permute-start | bytes 811016 | tf_op jit(solution)/shard_map/ppermute | solution.py:204
  62.4 4.4 %collective-permute-done.7.refs_2_ = bf16[2,528,128]{2,1,0:T(8,128)(2,1)S(1)} collective-permute-done((bf16[2,528,128]{2,1,0:T(8,128)(2,1)S(1)}, bf16[2,528,128]{2,1,0:T(8,128)(2,1)S(1)}, u32[]{:S(2)}, u32[]{:S(2)}) %collective-permute-start.7) | collective-permute-done | bytes 270368 | tf_op jit(solution)/shard_map/ppermute | solution.py:204
  66.8 3.1 %collective-permute-done.5.refs_6_ = bf16[2,528,128]{2,1,0:T(8,128)(2,1)S(1)} collective-permute-done((bf16[2,528,128]{2,1,0:T(8,128)(2,1)S(1)}, bf16[2,528,128]{2,1,0:T(8,128)(2,1)S(1)}, u32[]{:S(2)}, u32[]{:S(2)}) %collective-permute-start.5) | collective-permute-done | bytes 270368 | tf_op jit(solution)/shard_map/ppermute | solution.py:204
  70.0 2.7 %collective-permute-start.8 = (bf16[2,528,128]{2,1,0:T(8,128)(2,1)S(1)}, bf16[2,528,128]{2,1,0:T(8,128)(2,1)S(1)}, u32[]{:S(2)}, u32[]{:S(2)}) collective-permute-start(bf16[2,528,128]{2,1,0:T(8,128)(2,1)S(1)} %collective-permute-done.7.refs_2_), channel_id=1, source_target_pairs={{0,224},{32,0},{64,32},{96,64},{128,96},{160,128},{192,160},{224,1... | collective-permute-start | bytes 811016 | tf_op jit(solution)/shard_map/ppermute | solution.py:204
  72.6 3.8 %collective-permute-done.9.refs_5_ = bf16[2,528,128]{2,1,0:T(8,128)(2,1)S(1)} collective-permute-done((bf16[2,528,128]{2,1,0:T(8,128)(2,1)S(1)}, bf16[2,528,128]{2,1,0:T(8,128)(2,1)S(1)}, u32[]{:S(2)}, u32[]{:S(2)}) %collective-permute-start.9) | collective-permute-done | bytes 270368 | tf_op jit(solution)/shard_map/ppermute | solution.py:204
  76.6 2.3 %copy.36 = bf16[16,528,128]{2,0,1:T(8,128)(2,1)S(1)} copy(bf16[16,528,128]{2,1,0:T(8,128)(2,1)} %bitcast.52) | data formatting | bytes 4325376 | tf_op jit(solution)/shard_map/optimization_barrier | solution.py:247
  78.9 4.1 %collective-permute-done.10.refs_4_ = bf16[2,528,128]{2,1,0:T(8,128)(2,1)S(1)} collective-permute-done((bf16[2,528,128]{2,1,0:T(8,128)(2,1)S(1)}, bf16[2,528,128]{2,1,0:T(8,128)(2,1)S(1)}, u32[]{:S(2)}, u32[]{:S(2)}) %collective-permute-start.10) | collective-permute-done | bytes 270368 | tf_op jit(solution)/shard_map/ppermute | solution.py:204
  83.0 7.8 %shard_map.102 = (bf16[128,2048]{1,0:T(8,128)(2,1)}, bf16[2048,128]{1,0:T(8,128)(2,1)S(1)}, f32[256,128]{1,0:T(8,128)S(1)}, bf16[16,528,128]{2,1,0:T(8,128)(2,1)S(1)}) custom-call(s32[4]{0:T(128)S(1)} %pad_add_fusion.place, s32[16,16]{1,0:T(8,128)S(1)} %fusion.7.index, bf16[2,528,128]{2,1,0:T(8,128)(2,1)S(1)} %bitcast.58, ...), custom_call_target="tpu_custom_call" | custom-call | flops 800000000 | bytes 10485760 | tf_op jit(solution)/shard_map/pallas_call | solution.py:182
  91.0 2.4 %shard_map.103 = (bf16[2,512,128]{2,1,0:T(8,128)(2,1)S(1)}, bf16[2,512,128]{2,1,0:T(8,128)(2,1)S(1)}, bf16[2,512,128]{2,1,0:T(8,128)(2,1)S(1)}) custom-call(s32[4]{0:T(128)S(1)} %pad_add_fusion.place, s32[16,16]{1,0:T(8,128)S(1)} %fusion.7.index, bf16[16,528,128]{2,1,0:T(8,128)(2,1)S(1)} %bitcast.54, bf16[2048,128]{1,0:T(8,128)(2,1)S(1)} %get-tuple-element.84.dz_t), custom_call_target="tpu_custom_call" | custom-call | flops 120000000 | bytes 3145728 | tf_op jit(solution)/shard_map/pallas_call | solution.py:182
  93.4 0.7 collective-permute-done.11
  94.4 0.9 collective-permute-start.13
  95.2 1.9 collective-permute-start.14
  97.1 3.6 %shard_map.104 = (bf16[2,512,128]{2,1,0:T(8,128)(2,1)S(1)}, bf16[2,512,128]{2,1,0:T(8,128)(2,1)S(1)}, bf16[2,512,128]{2,1,0:T(8,128)(2,1)S(1)}, bf16[2,512,128]{2,1,0:T(8,128)(2,1)S(1)}, bf16[2,512,128]{2,1,0:T(8,128)(2,1)S(1)}) custom-call(s32[4]{0:T(128)S(1)} %pad_add_fusion.place, s32[16,16]{1,0:T(8,128)S(1)} %fusion.7.index, ...), custom_call_target="tpu_custom_call" | custom-call | flops 200000000 | bytes 5242880 | tf_op jit(solution)/shard_map/pallas_call | solution.py:182
  100.8 4.6 %collective-permute-start.15 = (bf16[256,128]{1,0:T(8,128)(2,1)S(1)}, bf16[256,128]{1,0:T(8,128)(2,1)S(1)}, u32[]{:S(2)}, u32[]{:S(2)}) collective-permute-start(bf16[256,128]{1,0:T(8,128)(2,1)S(1)} %fusion.8), channel_id=1, source_target_pairs={{0,128},{32,160},{64,192},{96,224},{128,0},{160,32},{192,64},{224,... | collective-permute-start | bytes 196616 | tf_op jit(solution)/shard_map/ppermute | solution.py:209
  105.4 3.8 %shard_map.105 = bf16[8,768,128]{2,1,0:T(8,128)(2,1)S(1)} custom-call(s32[4]{0:T(128)S(1)} %pad_add_fusion.place, s32[16,16]{1,0:T(8,128)S(1)} %fusion.7.index, bf16[16,528,128]{2,1,0:T(8,128)(2,1)S(1)} %get-tuple-element.83.x, bf16[2048,128]{1,0:T(8,128)(2,1)S(1)} %get-tuple-element.84.dz_t), custom_call_target="tpu_custom_call" | custom-call | flops 200000000 | bytes 4194304 | tf_op jit(solution)/shard_map/pallas_call | solution.py:182
  109.2 7.8 %collective-permute-start.19 = (bf16[8,768,128]{2,1,0:T(8,128)(2,1)S(1)}, bf16[8,768,128]{2,1,0:T(8,128)(2,1)S(1)}, u32[]{:S(2)}, u32[]{:S(2)}) collective-permute-start(bf16[8,768,128]{2,1,0:T(8,128)(2,1)S(1)} %shard_map.105), channel_id=1, source_target_pairs={{0,1},{1,0},{2,3},{3,2},{4,5},{5,4},{6,7},{7,6},{8,9},{9,8},{10,11... | collective-permute-start | bytes 4718600 | tf_op jit(solution)/shard_map/ppermute | solution.py:209
  117.2 1.5 collective-permute-start.16
  118.8 1.1 collective-permute-start.18
  119.9 3.6 %collective-permute-done.18 = bf16[256,128]{1,0:T(8,128)(2,1)S(1)} collective-permute-done((bf16[256,128]{1,0:T(8,128)(2,1)S(1)}, bf16[256,128]{1,0:T(8,128)(2,1)S(1)}, u32[]{:S(2)}, u32[]{:S(2)}) %collective-permute-start.18) | collective-permute-done | bytes 65568 | tf_op jit(solution)/shard_map/ppermute | solution.py:209
  123.5 1.6 collective-permute-done.17
  125.1 1.4 collective-permute-done.16
  126.7 1.5 collective-permute-start.20
  128.3 6.6 %shard_map.106 = bf16[8,896,128]{2,1,0:T(8,128)(2,1)} custom-call(s32[4]{0:T(128)S(1)} %pad_add_fusion.place, s32[16,16]{1,0:T(8,128)S(1)} %fusion.7.index, bf16[16,528,128]{2,1,0:T(8,128)(2,1)S(1)} %get-tuple-element.83.x, bf16[2048,128]{1,0:T(8,128)(2,1)S(1)} %get-tuple-element.84.dz_t, bf16[16,16,128]{2,1,0:T(8,128)(2,1)S(1)} %bitcast.59, ...), custom_call_target="tpu_custom_call" | custom-call | flops 300000000 | bytes 6291456 | tf_op jit(solution)/shard_map/pallas_call | solution.py:182
  135.0 5.0 %all-to-all-start.1 = ((bf16[8,896,128]{2,1,0:T(8,128)(2,1)}), bf16[8,896,128]{2,1,0:T(8,128)(2,1)S(1)}, u32[]{:S(2)}, u32[]{:S(2)}) async-start(bf16[8,896,128]{2,1,0:T(8,128)(2,1)} %shard_map.106), calls=%async_computation.1 | async-start | bytes 3670016 | tf_op jit(solution)/shard_map/all_to_all | solution.py:320
  140.1 9.4 %collective-permute-start.25 = (bf16[256,128]{1,0:T(8,128)(2,1)S(1)}, bf16[256,128]{1,0:T(8,128)(2,1)S(1)}, u32[]{:S(2)}, u32[]{:S(2)}) collective-permute-start(bf16[256,128]{1,0:T(8,128)(2,1)S(1)} %add_convert_fusion.6), channel_id=1, source_target_pairs={{0,0},{1,16},{2,32},{3,48},{4,64},{5,80},{6,96},{7,112},{8,128},{9... | collective-permute-start | bytes 196616 | tf_op jit(solution)/shard_map/ppermute | solution.py:321
  149.6 0.7 copy-done.7
  150.4 2.4 %collective-permute-start.23 = (bf16[512,128]{1,0:T(8,128)(2,1)S(1)}, bf16[512,128]{1,0:T(8,128)(2,1)S(1)}, u32[]{:S(2)}, u32[]{:S(2)}) collective-permute-start(bf16[512,128]{1,0:T(8,128)(2,1)S(1)} %fusion.4), channel_id=1, source_target_pairs={{0,16},{16,0},{1,17},{17,1},{2,18},{18,2},{3,19},{19,3},{4,20},{20... | collective-permute-start | bytes 393224 | tf_op jit(solution)/shard_map/ppermute | solution.py:209
  152.8 10.5 %all-to-all-done.1 = bf16[8,896,128]{2,1,0:T(8,128)(2,1)S(1)} async-done(((bf16[8,896,128]{2,1,0:T(8,128)(2,1)}), bf16[8,896,128]{2,1,0:T(8,128)(2,1)S(1)}, u32[]{:S(2)}, u32[]{:S(2)}) %all-to-all-start.1) | async-done | bytes 1835040 | tf_op jit(solution)/shard_map/all_to_all | solution.py:320
  163.5 4.8 %collective-permute-start.26 = (f32[64,128]{1,0:T(8,128)S(1)}, f32[64,128]{1,0:T(8,128)S(1)}, u32[]{:S(2)}, u32[]{:S(2)}) collective-permute-start(f32[64,128]{1,0:T(8,128)S(1)} %slice.67), channel_id=1, source_target_pairs={{0,1},{1,0},{2,3},{3,2},{4,5},{5,4},{6,7},{7,6},{8,9},{9,8},{10,11... | collective-permute-start | bytes 98312 | tf_op jit(solution)/shard_map/ppermute | solution.py:209
  168.3 4.1 %collective-permute-done.23 = bf16[512,128]{1,0:T(8,128)(2,1)S(1)} collective-permute-done((bf16[512,128]{1,0:T(8,128)(2,1)S(1)}, bf16[512,128]{1,0:T(8,128)(2,1)S(1)}, u32[]{:S(2)}, u32[]{:S(2)}) %collective-permute-start.23) | collective-permute-done | bytes 131104 | tf_op jit(solution)/shard_map/ppermute | solution.py:209
  172.6 6.3 %collective-permute-start.24 = (bf16[512,128]{1,0:T(8,128)(2,1)S(1)}, bf16[512,128]{1,0:T(8,128)(2,1)S(1)}, u32[]{:S(2)}, u32[]{:S(2)}) collective-permute-start(bf16[512,128]{1,0:T(8,128)(2,1)S(1)} %fusion.2), channel_id=1, source_target_pairs={{0,0},{1,16},{2,32},{3,48},{4,64},{5,80},{6,96},{7,112},{8,128},{9... | collective-permute-start | bytes 393224 | tf_op jit(solution)/shard_map/ppermute | solution.py:319
  179.1 0.7 copy.48
  180.2 0.9 reshape.95
  181.1 0.6 copy.49
  181.8 5.8 %collective-permute-done.24 = bf16[512,128]{1,0:T(8,128)(2,1)S(1)} collective-permute-done((bf16[512,128]{1,0:T(8,128)(2,1)S(1)}, bf16[512,128]{1,0:T(8,128)(2,1)S(1)}, u32[]{:S(2)}, u32[]{:S(2)}) %collective-permute-start.24) | collective-permute-done | bytes 131104 | tf_op jit(solution)/shard_map/ppermute | solution.py:319
  187.8 0.8 copy.42
  (73 shorter events, 3.6 us)
Async XLA Ops:
  7.2 3.3 %copy-start.1 = (bf16[512,256]{1,0:T(8,128)(2,1)S(1)}, bf16[512,256]{1,0:T(8,128)(2,1)}, u32[]{:S(2)}) copy-start(bf16[512,256]{1,0:T(8,128)(2,1)} %u.1) | copy-start | bytes 786436
  7.2 62.8 %all-gather.3.cloned.1.call-start = ((), (), s32[]{:S(2)}) async-start(), calls=%async_computation.2 | async-start | bytes 2297856 | tf_op jit(solution)/shard_map/all_gather | solution.py:223
  10.4 0.9 copy-start.4
  11.7 22.2 %collective-permute-start = (bf16[512,128]{1,0:T(8,128)(2,1)S(1)}, bf16[512,128]{1,0:T(8,128)(2,1)S(1)}, u32[]{:S(2)}, u32[]{:S(2)}) collective-permute-start(bf16[512,128]{1,0:T(8,128)(2,1)S(1)} %get-tuple-element.62), channel_id=1, source_target_pairs={{0,0},{1,16},{2,32},{3,48},{4,64},{5,80},{6,96},{7,112},{8,128},{9... | collective-permute-start | bytes 393224 | tf_op jit(solution)/shard_map/ppermute | solution.py:233
  33.9 10.0 %collective-permute-start.2 = (bf16[512,128]{1,0:T(8,128)(2,1)S(1)}, bf16[512,128]{1,0:T(8,128)(2,1)S(1)}, u32[]{:S(2)}, u32[]{:S(2)}) collective-permute-start(bf16[512,128]{1,0:T(8,128)(2,1)S(1)} %collective-permute-done), channel_id=1, source_target_pairs={{0,16},{16,0},{1,17},{17,1},{2,18},{18,2},{3,19},{19,3},{4,20},{20... | collective-permute-start | bytes 393224 | tf_op jit(solution)/shard_map/ppermute | solution.py:209
  35.7 6.4 %collective-permute-start.1 = (bf16[16,128]{1,0:T(8,128)(2,1)S(1)}, bf16[16,128]{1,0:T(8,128)(2,1)S(1)}, u32[]{:S(2)}, u32[]{:S(2)}) collective-permute-start(bf16[16,128]{1,0:T(8,128)(2,1)S(1)} %reduce_sum.18), channel_id=1, source_target_pairs={{0,0},{1,16},{2,32},{3,48},{4,64},{5,80},{6,96},{7,112},{8,128},{9... | collective-permute-start | bytes 12296 | tf_op jit(solution)/shard_map/ppermute | solution.py:239
  39.8 4.0 %collective-permute-start.3 = (bf16[16,128]{1,0:T(8,128)(2,1)S(1)}, bf16[16,128]{1,0:T(8,128)(2,1)S(1)}, u32[]{:S(2)}, u32[]{:S(2)}) collective-permute-start(bf16[16,128]{1,0:T(8,128)(2,1)S(1)} %reduce_sum.18), channel_id=1, source_target_pairs={{0,16},{1,0},{2,48},{3,32},{4,80},{5,64},{6,112},{7,96},{8,144},{9... | collective-permute-start | bytes 12296 | tf_op jit(solution)/shard_map/ppermute | solution.py:241
  43.9 15.1 %collective-permute-start.6 = (bf16[2,528,128]{2,1,0:T(8,128)(2,1)S(1)}, bf16[2,528,128]{2,1,0:T(8,128)(2,1)S(1)}, u32[]{:S(2)}, u32[]{:S(2)}) collective-permute-start(bf16[2,528,128]{2,1,0:T(8,128)(2,1)S(1)} %bitcast.56), channel_id=1, source_target_pairs={{0,224},{32,0},{64,32},{96,64},{128,96},{160,128},{192,160},{224,1... | collective-permute-start | bytes 811016 | tf_op jit(solution)/shard_map/ppermute | solution.py:204
  53.6 8.8 %collective-permute-start.4 = (bf16[2,528,128]{2,1,0:T(8,128)(2,1)S(1)}, bf16[2,528,128]{2,1,0:T(8,128)(2,1)S(1)}, u32[]{:S(2)}, u32[]{:S(2)}) collective-permute-start(bf16[2,528,128]{2,1,0:T(8,128)(2,1)S(1)} %bitcast.57), channel_id=1, source_target_pairs={{0,32},{32,64},{64,96},{96,128},{128,160},{160,192},{192,224},{224... | collective-permute-start | bytes 811016 | tf_op jit(solution)/shard_map/ppermute | solution.py:204
  59.0 7.8 %collective-permute-start.7 = (bf16[2,528,128]{2,1,0:T(8,128)(2,1)S(1)}, bf16[2,528,128]{2,1,0:T(8,128)(2,1)S(1)}, u32[]{:S(2)}, u32[]{:S(2)}) collective-permute-start(bf16[2,528,128]{2,1,0:T(8,128)(2,1)S(1)} %collective-permute-done.6.refs_1_), channel_id=1, source_target_pairs={{0,224},{32,0},{64,32},{96,64},{128,96},{160,128},{192,160},{224,1... | collective-permute-start | bytes 811016 | tf_op jit(solution)/shard_map/ppermute | solution.py:204
  62.4 7.6 %collective-permute-start.5 = (bf16[2,528,128]{2,1,0:T(8,128)(2,1)S(1)}, bf16[2,528,128]{2,1,0:T(8,128)(2,1)S(1)}, u32[]{:S(2)}, u32[]{:S(2)}) collective-permute-start(bf16[2,528,128]{2,1,0:T(8,128)(2,1)S(1)} %collective-permute-done.4.refs_7_), channel_id=1, source_target_pairs={{0,32},{32,64},{64,96},{96,128},{128,160},{160,192},{192,224},{224... | collective-permute-start | bytes 811016 | tf_op jit(solution)/shard_map/ppermute | solution.py:204
  70.0 6.5 %collective-permute-start.9 = (bf16[2,528,128]{2,1,0:T(8,128)(2,1)S(1)}, bf16[2,528,128]{2,1,0:T(8,128)(2,1)S(1)}, u32[]{:S(2)}, u32[]{:S(2)}) collective-permute-start(bf16[2,528,128]{2,1,0:T(8,128)(2,1)S(1)} %collective-permute-done.5.refs_6_), channel_id=1, source_target_pairs={{0,32},{32,64},{64,96},{96,128},{128,160},{160,192},{192,224},{224... | collective-permute-start | bytes 811016 | tf_op jit(solution)/shard_map/ppermute | solution.py:204
  70.0 8.9 %collective-permute-start.8 = (bf16[2,528,128]{2,1,0:T(8,128)(2,1)S(1)}, bf16[2,528,128]{2,1,0:T(8,128)(2,1)S(1)}, u32[]{:S(2)}, u32[]{:S(2)}) collective-permute-start(bf16[2,528,128]{2,1,0:T(8,128)(2,1)S(1)} %collective-permute-done.7.refs_2_), channel_id=1, source_target_pairs={{0,224},{32,0},{64,32},{96,64},{128,96},{160,128},{192,160},{224,1... | collective-permute-start | bytes 811016 | tf_op jit(solution)/shard_map/ppermute | solution.py:204
  76.5 6.5 %collective-permute-start.10 = (bf16[2,528,128]{2,1,0:T(8,128)(2,1)S(1)}, bf16[2,528,128]{2,1,0:T(8,128)(2,1)S(1)}, u32[]{:S(2)}, u32[]{:S(2)}) collective-permute-start(bf16[2,528,128]{2,1,0:T(8,128)(2,1)S(1)} %collective-permute-done.9.refs_5_), channel_id=1, source_target_pairs={{0,32},{32,64},{64,96},{96,128},{128,160},{160,192},{192,224},{224... | collective-permute-start | bytes 811016 | tf_op jit(solution)/shard_map/ppermute | solution.py:204
  76.6 6.4 %copy-start = (bf16[8448,128]{1,0:T(8,128)(2,1)S(1)}, bf16[8448,128]{1,0:T(8,128)(2,1)}, u32[]{:S(2)}) copy-start(bf16[8448,128]{1,0:T(8,128)(2,1)} %all-gather.3.cloned.1.call-done) | copy-start | bytes 6488068
  76.6 6.4 %copy-start.2 = (bf16[256,2048]{1,0:T(8,128)(2,1)S(1)}, bf16[256,2048]{1,0:T(8,128)(2,1)}, u32[]{:S(2)}) copy-start(bf16[256,2048]{1,0:T(8,128)(2,1)} %refs_9_.1) | copy-start | bytes 3145732
  76.6 6.4 %copy-start.3 = (bf16[128,2048]{1,0:T(8,128)(2,1)S(1)}, bf16[128,2048]{1,0:T(8,128)(2,1)}, u32[]{:S(2)}) copy-start(bf16[128,2048]{1,0:T(8,128)(2,1)} %refs_10_.1) | copy-start | bytes 1572868
  90.9 3.2 %collective-permute-start.11 = (bf16[256,128]{1,0:T(8,128)(2,1)S(1)}, bf16[256,128]{1,0:T(8,128)(2,1)S(1)}, u32[]{:S(2)}, u32[]{:S(2)}) collective-permute-start(bf16[256,128]{1,0:T(8,128)(2,1)S(1)} %convert_element_type.145), channel_id=1, source_target_pairs={{0,32},{32,0},{64,96},{96,64},{128,160},{160,128},{192,224},{224,1... | collective-permute-start | bytes 196616 | tf_op jit(solution)/shard_map/ppermute | solution.py:209
  94.1 6.6 %collective-permute-start.12 = (bf16[256,128]{1,0:T(8,128)(2,1)S(1)}, bf16[256,128]{1,0:T(8,128)(2,1)S(1)}, u32[]{:S(2)}, u32[]{:S(2)}) collective-permute-start(bf16[256,128]{1,0:T(8,128)(2,1)S(1)} %fusion.5), channel_id=1, source_target_pairs={{0,64},{32,96},{64,0},{96,32},{128,192},{160,224},{192,128},{224,1... | collective-permute-start | bytes 196616 | tf_op jit(solution)/shard_map/ppermute | solution.py:209
  94.4 14.8 %collective-permute-start.13 = (bf16[2,512,128]{2,1,0:T(8,128)(2,1)S(1)}, bf16[2,512,128]{2,1,0:T(8,128)(2,1)S(1)}, u32[]{:S(2)}, u32[]{:S(2)}) collective-permute-start(bf16[2,512,128]{2,1,0:T(8,128)(2,1)S(1)} %get-tuple-element.80), channel_id=1, source_target_pairs={{0,32},{32,64},{64,96},{96,128},{128,160},{160,192},{192,224},{224... | collective-permute-start | bytes 786440 | tf_op jit(solution)/shard_map/ppermute | solution.py:204
  95.2 13.9 %collective-permute-start.14 = (bf16[2,512,128]{2,1,0:T(8,128)(2,1)S(1)}, bf16[2,512,128]{2,1,0:T(8,128)(2,1)S(1)}, u32[]{:S(2)}, u32[]{:S(2)}) collective-permute-start(bf16[2,512,128]{2,1,0:T(8,128)(2,1)S(1)} %get-tuple-element.81), channel_id=1, source_target_pairs={{0,224},{32,0},{64,32},{96,64},{128,96},{160,128},{192,160},{224,1... | collective-permute-start | bytes 786440 | tf_op jit(solution)/shard_map/ppermute | solution.py:204
  100.8 8.4 %collective-permute-start.15 = (bf16[256,128]{1,0:T(8,128)(2,1)S(1)}, bf16[256,128]{1,0:T(8,128)(2,1)S(1)}, u32[]{:S(2)}, u32[]{:S(2)}) collective-permute-start(bf16[256,128]{1,0:T(8,128)(2,1)S(1)} %fusion.8), channel_id=1, source_target_pairs={{0,128},{32,160},{64,192},{96,224},{128,0},{160,32},{192,64},{224,... | collective-permute-start | bytes 196616 | tf_op jit(solution)/shard_map/ppermute | solution.py:209
  109.2 17.3 %collective-permute-start.19 = (bf16[8,768,128]{2,1,0:T(8,128)(2,1)S(1)}, bf16[8,768,128]{2,1,0:T(8,128)(2,1)S(1)}, u32[]{:S(2)}, u32[]{:S(2)}) collective-permute-start(bf16[8,768,128]{2,1,0:T(8,128)(2,1)S(1)} %shard_map.105), channel_id=1, source_target_pairs={{0,1},{1,0},{2,3},{3,2},{4,5},{5,4},{6,7},{7,6},{8,9},{9,8},{10,11... | collective-permute-start | bytes 4718600 | tf_op jit(solution)/shard_map/ppermute | solution.py:209
  117.1 8.0 %collective-permute-start.17 = (bf16[2,512,128]{2,1,0:T(8,128)(2,1)S(1)}, bf16[2,512,128]{2,1,0:T(8,128)(2,1)S(1)}, u32[]{:S(2)}, u32[]{:S(2)}) collective-permute-start(bf16[2,512,128]{2,1,0:T(8,128)(2,1)S(1)} %add_convert_fusion.3), channel_id=1, source_target_pairs={{0,224},{32,0},{64,32},{96,64},{128,96},{160,128},{192,160},{224,1... | collective-permute-start | bytes 786440 | tf_op jit(solution)/shard_map/ppermute | solution.py:204
  117.2 9.2 %collective-permute-start.16 = (bf16[2,512,128]{2,1,0:T(8,128)(2,1)S(1)}, bf16[2,512,128]{2,1,0:T(8,128)(2,1)S(1)}, u32[]{:S(2)}, u32[]{:S(2)}) collective-permute-start(bf16[2,512,128]{2,1,0:T(8,128)(2,1)S(1)} %add_convert_fusion.4), channel_id=1, source_target_pairs={{0,32},{32,64},{64,96},{96,128},{128,160},{160,192},{192,224},{224... | collective-permute-start | bytes 786440 | tf_op jit(solution)/shard_map/ppermute | solution.py:204
  118.8 4.7 %collective-permute-start.18 = (bf16[256,128]{1,0:T(8,128)(2,1)S(1)}, bf16[256,128]{1,0:T(8,128)(2,1)S(1)}, u32[]{:S(2)}, u32[]{:S(2)}) collective-permute-start(bf16[256,128]{1,0:T(8,128)(2,1)S(1)} %fusion.6), channel_id=1, source_target_pairs={{0,16},{16,0},{1,17},{17,1},{2,18},{18,2},{3,19},{19,3},{4,20},{20... | collective-permute-start | bytes 196616 | tf_op jit(solution)/shard_map/ppermute | solution.py:209
  126.5 8.4 %collective-permute-start.21 = (bf16[2,512,128]{2,1,0:T(8,128)(2,1)S(1)}, bf16[2,512,128]{2,1,0:T(8,128)(2,1)S(1)}, u32[]{:S(2)}, u32[]{:S(2)}) collective-permute-start(bf16[2,512,128]{2,1,0:T(8,128)(2,1)S(1)} %add_convert_fusion.1), channel_id=1, source_target_pairs={{0,224},{32,0},{64,32},{96,64},{128,96},{160,128},{192,160},{224,1... | collective-permute-start | bytes 786440 | tf_op jit(solution)/shard_map/ppermute | solution.py:204
  126.7 8.2 %collective-permute-start.20 = (bf16[2,512,128]{2,1,0:T(8,128)(2,1)S(1)}, bf16[2,512,128]{2,1,0:T(8,128)(2,1)S(1)}, u32[]{:S(2)}, u32[]{:S(2)}) collective-permute-start(bf16[2,512,128]{2,1,0:T(8,128)(2,1)S(1)} %add_convert_fusion.2), channel_id=1, source_target_pairs={{0,32},{32,64},{64,96},{96,128},{128,160},{160,192},{192,224},{224... | collective-permute-start | bytes 786440 | tf_op jit(solution)/shard_map/ppermute | solution.py:204
  134.9 14.7 %copy-start.5 = (bf16[2,512,128]{2,1,0:T(8,128)(2,1)}, bf16[2,512,128]{2,1,0:T(8,128)(2,1)S(1)}, u32[]{:S(2)}) copy-start(bf16[2,512,128]{2,1,0:T(8,128)(2,1)S(1)} %collective-permute-done.21) | copy-start | bytes 786436
  135.0 28.3 %all-to-all-start.1 = ((bf16[8,896,128]{2,1,0:T(8,128)(2,1)}), bf16[8,896,128]{2,1,0:T(8,128)(2,1)S(1)}, u32[]{:S(2)}, u32[]{:S(2)}) async-start(bf16[8,896,128]{2,1,0:T(8,128)(2,1)} %shard_map.106), calls=%async_computation.1 | async-start | bytes 3670016 | tf_op jit(solution)/shard_map/all_to_all | solution.py:320
  140.0 9.5 %collective-permute-start.22 = (bf16[2,512,128]{2,1,0:T(8,128)(2,1)S(1)}, bf16[2,512,128]{2,1,0:T(8,128)(2,1)S(1)}, u32[]{:S(2)}, u32[]{:S(2)}) collective-permute-start(bf16[2,512,128]{2,1,0:T(8,128)(2,1)S(1)} %add_convert_fusion), channel_id=1, source_target_pairs={{0,32},{32,64},{64,96},{96,128},{128,160},{160,192},{192,224},{224... | collective-permute-start | bytes 786440 | tf_op jit(solution)/shard_map/ppermute | solution.py:204
  140.1 41.6 %collective-permute-start.25 = (bf16[256,128]{1,0:T(8,128)(2,1)S(1)}, bf16[256,128]{1,0:T(8,128)(2,1)S(1)}, u32[]{:S(2)}, u32[]{:S(2)}) collective-permute-start(bf16[256,128]{1,0:T(8,128)(2,1)S(1)} %add_convert_fusion.6), channel_id=1, source_target_pairs={{0,0},{1,16},{2,32},{3,48},{4,64},{5,80},{6,96},{7,112},{8,128},{9... | collective-permute-start | bytes 196616 | tf_op jit(solution)/shard_map/ppermute | solution.py:321
  149.6 0.7 copy-start.7
  150.3 22.1 %copy-start.6 = (bf16[2,512,128]{2,1,0:T(8,128)(2,1)S(1)}, bf16[2,512,128]{2,1,0:T(8,128)(2,1)}, u32[]{:S(2)}) copy-start(bf16[2,512,128]{2,1,0:T(8,128)(2,1)} %copy-done.5) | copy-start | bytes 786436
  150.4 22.1 %collective-permute-start.23 = (bf16[512,128]{1,0:T(8,128)(2,1)S(1)}, bf16[512,128]{1,0:T(8,128)(2,1)S(1)}, u32[]{:S(2)}, u32[]{:S(2)}) collective-permute-start(bf16[512,128]{1,0:T(8,128)(2,1)S(1)} %fusion.4), channel_id=1, source_target_pairs={{0,16},{16,0},{1,17},{17,1},{2,18},{18,2},{3,19},{19,3},{4,20},{20... | collective-permute-start | bytes 393224 | tf_op jit(solution)/shard_map/ppermute | solution.py:209
  163.3 9.2 %copy-start.8 = (bf16[2,512,128]{2,1,0:T(8,128)(2,1)S(1)}, bf16[2,512,128]{2,1,0:T(8,128)(2,1)}, u32[]{:S(2)}) copy-start(bf16[2,512,128]{2,1,0:T(8,128)(2,1)} %copy-done.7) | copy-start | bytes 786436
  163.5 17.6 %collective-permute-start.26 = (f32[64,128]{1,0:T(8,128)S(1)}, f32[64,128]{1,0:T(8,128)S(1)}, u32[]{:S(2)}, u32[]{:S(2)}) collective-permute-start(f32[64,128]{1,0:T(8,128)S(1)} %slice.67), channel_id=1, source_target_pairs={{0,1},{1,0},{2,3},{3,2},{4,5},{5,4},{6,7},{7,6},{8,9},{9,8},{10,11... | collective-permute-start | bytes 98312 | tf_op jit(solution)/shard_map/ppermute | solution.py:209
  172.6 15.0 %collective-permute-start.24 = (bf16[512,128]{1,0:T(8,128)(2,1)S(1)}, bf16[512,128]{1,0:T(8,128)(2,1)S(1)}, u32[]{:S(2)}, u32[]{:S(2)}) collective-permute-start(bf16[512,128]{1,0:T(8,128)(2,1)S(1)} %fusion.2), channel_id=1, source_target_pairs={{0,0},{1,16},{2,32},{3,48},{4,64},{5,80},{6,96},{7,112},{8,128},{9... | collective-permute-start | bytes 393224 | tf_op jit(solution)/shard_map/ppermute | solution.py:319
Sparse Core Ops, SparseCore 0:
  10.6 46.0 all-gather.2

commit v5 on v4

--- a/solution.py
+++ b/solution.py
@@ -57,7 +57,10 @@
 
 def first_kernel(x, u, x_t, p):
     x_t[...] = x[...].T
-    p[...] = dot(u[...].T, x_t[...], NN).reshape(SH, RS, TOK)
+    whole = dot(u[...].T, x_t[...], NN)
+    for s in range(SH):
+        for j in range(2):
+            p[s, j] = whole[(s ^ j) * RS : (s ^ j) * RS + RS]
 
 
 def forward_kernel(place, index, *refs):
@@ -158,8 +161,11 @@
     grad_rows(place, index, x, dz_t, out, 1, None)
 
 
-def grad_own_kernel(place, index, x, dz_t, q_t, other, out):
+def grad_own_kernel(place, index, x, dz_t, other, out):
     grad_rows(place, index, x, dz_t, out, 0, other)
+
+
+def u_kernel(place, grads, x, q_t, out, rows, sem):
     q = q_t[place[3]]
 
     def shard(k, carry):
@@ -167,11 +173,31 @@
             slot = x_slot(place, 2 * k + (place[2] ^ half))
             u = dot(q, x[slot, :FEAT, :], NT).astype(BF16)
             for j in range(FEAT // TOK):
-                first = FEAT + VROWS + half * UROWS + j * RS
-                out[k, first : first + RS, :] = u[:, j * TOK : (j + 1) * TOK]
+                first = half * UROWS + j * RS
+                rows[k, first : first + RS, :] = u[:, j * TOK : (j + 1) * TOK]
         return carry
 
     lax.fori_loop(0, NK, shard, 0)
+    copy = pltpu.make_async_copy(rows, out.at[:, FEAT + VROWS :, :], sem)
+    copy.start()
+    copy.wait()
+
+
+def u_call(place, grads, x, q_t):
+    vmem = pl.BlockSpec(memory_space=pltpu.VMEM)
+    anywhere = pl.BlockSpec(memory_space=pl.ANY)
+    return pl.pallas_call(
+        u_kernel,
+        out_shape=jax.ShapeDtypeStruct(grads.shape, BF16),
+        in_specs=[pl.BlockSpec(memory_space=pltpu.SMEM), anywhere, vmem, vmem],
+        out_specs=anywhere,
+        scratch_shapes=[pltpu.VMEM((NK, 2 * UROWS, TOK), BF16), pltpu.SemaphoreType.DMA],
+        input_output_aliases={1: 0},
+        compiler_params=pltpu.CompilerParams(vmem_limit_bytes=10 << 20),
+        cost_estimate=pl.CostEstimate(
+            flops=70_000_000, bytes_accessed=3 << 20, transcendentals=0
+        ),
+    )(place, grads, x, q_t)
 
 
 def call(kernel, out_shape, flops, bytes_accessed, operands, scratch=(), free=0, scalars=2):
@@ -211,7 +237,6 @@
 
 def on_device(inputs, cotangent, sparse_blocks, block_index, u_factor, v_factor):
     turn = [(r * SH + c, c * SH + r) for r in range(SH) for c in range(SH)]
-    turn_pair = [(r * SH + c, (c ^ 1) * SH + r) for r in range(SH) for c in range(SH)]
     place = jnp.stack(
         [lax.axis_index("z"), lax.axis_index("xh"), lax.axis_index("core"), lax.axis_index(ROW)]
     ).astype(jnp.int32)
@@ -224,7 +249,7 @@
 
     mine, p = call(
         first_kernel,
-        (shape(FEAT, TOK), shape(SH, RS, TOK, kind=F32)),
+        (shape(FEAT, TOK), shape(SH, 2, RS, TOK, kind=F32)),
         40_000_000,
         1 << 19,
         (inputs, u_factor),
@@ -233,13 +258,8 @@
     turned = lax.ppermute(mine, ALL, turn)
     p_in = lax.all_to_all(p, COL, 0, 0)
     turned, p_in = lax.optimization_barrier((turned, p_in))
-    p = jnp.sum(p_in, axis=0).astype(BF16)
-    parts = [
-        turned,
-        lax.ppermute(p, ALL, turn),
-        meet(turned, "xh", 1),
-        lax.ppermute(p, ALL, turn_pair),
-    ]
+    p = lax.ppermute(jnp.sum(p_in, axis=0).astype(BF16), ALL, turn)
+    parts = [turned, p[0], meet(turned, "xh", 1), p[1]]
     held = {0: jnp.concatenate(parts).reshape(2, ROWS, TOK)}
     for step in (1, 2, 3):
         held[-step], held[step] = shift(held[1 - step], 1), shift(held[step - 1], -1)
@@ -300,18 +320,19 @@
     up, down = shift(add(back[3], up), 1), shift(add(back[6], down), -1)
     q = q + q_in.astype(F32)
     q_in = meet(q.astype(BF16), "xh", 1)
-    up, down, q_in, grads_in = lax.optimization_barrier((up, down, q_in, grads_in))
-
-    up, down = shift(add(back[2], up), 1), shift(add(back[7], down), -1)
-    q_t = (q + q_in.astype(F32)).astype(BF16)
     grads = call(
         grad_own_kernel,
         shape(NK, FEAT + VROWS + 2 * UROWS, TOK),
-        300_000_000,
+        200_000_000,
         6 << 20,
-        (place, index, x_all, dz_t, q_t.reshape(SH, RS, TOK), grads_in),
-    )
-    up, down, grads = lax.optimization_barrier((up, down, grads))
+        (place, index, x_all, dz_t, grads_in),
+    )
+    up, down, q_in, grads = lax.optimization_barrier((up, down, q_in, grads))
+
+    up, down = shift(add(back[2], up), 1), shift(add(back[7], down), -1)
+    q_t = (q + q_in.astype(F32)).astype(BF16)
+    grads = u_call(place, grads, x_all, q_t.reshape(SH, RS, TOK))
+    up, down, grads, q_t = lax.optimization_barrier((up, down, grads, q_t))
 
     up = shift(add(back[1], up), 1)
     other = add(back[0][1], up[1], down[1])

time: 196 us -> 199 us (1.015)
  waiting for transfers between devices: 52.5 us -> 73 us
  blocking collectives: 16.1 us -> 0 us
  starting transfers between devices: 75.9 us -> 73.6 us
  Pallas kernels: 24.5 us -> 26.5 us
    all_to_all x1 -> x0, blocking collectives: 16.1 us -> none  [on_device(): p_in = lax.all_to_all(p, COL, 0, 0)]
    all_to_all x0 -> x1, starting transfers between devices: none -> 6.91 us  [on_device(): p_in = lax.all_to_all(p, COL, 0, 0)]
    ppermute x8, starting transfers between devices: 23 us -> 16.2 us  [meet(): return lax.ppermute(x, axis, [(i, i ^ flip) for i in range(count)])]
    ppermute x14, waiting for transfers between devices: 23.9 us -> 30 us  [shift(): return lax.ppermute(x, 'z', [(i, (i + by) % NZ) for i in range(NZ)])]
    ppermute x8, waiting for transfers between devices: 8.41 us -> 12.1 us  [meet(): return lax.ppermute(x, axis, [(i, i ^ flip) for i in range(count)])]
    ppermute x1, waiting for transfers between devices: 0.01 us -> 3.46 us  [on_device(): turned = lax.ppermute(mine, ALL, turn)]
    all_to_all x1, waiting for transfers between devices: 10.5 us -> 13.4 us  [on_device(): grads_in = lax.all_to_all(grads, ('xl', 'y'), 0, 0)]
    ppermute x1, starting transfers between devices: 9.41 us -> 6.59 us  [on_device(): q_turned = lax.ppermute(q_t, ALL, turn)]
  transfers between devices with their start and end apart: 29 -> 29, of which waited for: 15 -> 19; matrix products, arithmetic and copies ran while one was open for 3% -> 3% of each run, Pallas kernels for 9% -> 9%
where the time goes in v5:
time: 199 us
  starting transfers between devices  73.6 us (37%)
  waiting for transfers between devices  73 us (37%)
  Pallas kernels  26.5 us (13%)
  between operations  14.4 us (7%)
  local copies, waits for them, and re-layouts  9.07 us (5%)
    ppermute x14, waiting for transfers between devices, shift(): return lax.ppermute(x, 'z', [(i, (i + by) % NZ) for i in range(NZ)])  30 us
    pallas_call x6, Pallas kernels, call(): pl.pallas_call(kernel, out_shape=out_shape, in_specs=[smem] * scalars + [...  23.7 us
    ppermute x14, starting transfers between devices, shift(): return lax.ppermute(x, 'z', [(i, (i + by) % NZ) for i in range(NZ)])  23.2 us
    ppermute x8, starting transfers between devices, meet(): return lax.ppermute(x, axis, [(i, i ^ flip) for i in range(count)])  16.2 us
    all_to_all x1, waiting for transfers between devices, on_device(): grads_in = lax.all_to_all(grads, ('xl', 'y'), 0, 0)  13.4 us
    ppermute x8, waiting for transfers between devices, meet(): return lax.ppermute(x, axis, [(i, i ^ flip) for i in range(count)])  12.1 us
    ppermute x1, waiting for transfers between devices, on_device(): x_grad_t = lax.ppermute(total, ALL, turn)  8.14 us
    all_to_all x1, starting transfers between devices, on_device(): p_in = lax.all_to_all(p, COL, 0, 0)  6.91 us
  transfers between devices with their start and end apart: 29, of which 19 were waited for; matrix products, arithmetic and copies ran while one was open for 3% of the time, Pallas kernels for 9%

profile of v5, /device:TPU:1, one launch (start us, length us, event | category | flops | bytes accessed | tf_op | source)
XLA Modules:
  0.0 198.5 jit_solution(10422528283733360412)
XLA Ops:
  7.2 0.7 convert_bitcast_fusion
  8.0 1.2 reshape.90
  9.7 0.8 copy.36
  10.5 1.0 shard_map.101
  11.5 6.9 %all-to-all-start = ((f32[16,2,16,128]{3,2,1,0:T(8,128)}), f32[16,2,16,128]{3,2,1,0:T(8,128)S(1)}, u32[]{:S(2)}, u32[]{:S(2)}) async-start(f32[16,2,16,128]{3,2,1,0:T(8,128)} %get-tuple-element.64), calls=%async_computation | async-start | bytes 524288 | tf_op jit(solution)/shard_map/all_to_all | solution.py:259
  18.4 4.3 %collective-permute-start = (bf16[512,128]{1,0:T(8,128)(2,1)S(1)}, bf16[512,128]{1,0:T(8,128)(2,1)S(1)}, u32[]{:S(2)}, u32[]{:S(2)}) collective-permute-start(bf16[512,128]{1,0:T(8,128)(2,1)S(1)} %get-tuple-element.63), channel_id=1, source_target_pairs={{0,0},{1,16},{2,32},{3,48},{4,64},{5,80},{6,96},{7,112},{8,128},{9... | collective-permute-start | bytes 393224 | tf_op jit(solution)/shard_map/ppermute | solution.py:258
  22.8 3.5 %collective-permute-done = bf16[512,128]{1,0:T(8,128)(2,1)S(1)} collective-permute-done((bf16[512,128]{1,0:T(8,128)(2,1)S(1)}, bf16[512,128]{1,0:T(8,128)(2,1)S(1)}, u32[]{:S(2)}, u32[]{:S(2)}) %collective-permute-start) | collective-permute-done | bytes 131104 | tf_op jit(solution)/shard_map/ppermute | solution.py:258
  26.3 4.6 %collective-permute-start.1 = (bf16[2,16,128]{2,1,0:T(8,128)(2,1)S(1)}, bf16[2,16,128]{2,1,0:T(8,128)(2,1)S(1)}, u32[]{:S(2)}, u32[]{:S(2)}) collective-permute-start(bf16[2,16,128]{2,1,0:T(8,128)(2,1)S(1)} %reduce_sum.18), channel_id=1, source_target_pairs={{0,0},{1,16},{2,32},{3,48},{4,64},{5,80},{6,96},{7,112},{8,128},{9... | collective-permute-start | bytes 24584 | tf_op jit(solution)/shard_map/ppermute | solution.py:261
  31.0 5.9 %collective-permute-done.1 = bf16[2,16,128]{2,1,0:T(8,128)(2,1)S(1)} collective-permute-done((bf16[2,16,128]{2,1,0:T(8,128)(2,1)S(1)}, bf16[2,16,128]{2,1,0:T(8,128)(2,1)S(1)}, u32[]{:S(2)}, u32[]{:S(2)}) %collective-permute-start.1) | collective-permute-done | bytes 8224 | tf_op jit(solution)/shard_map/ppermute | solution.py:261
  36.8 7.5 %collective-permute-done.2 = bf16[512,128]{1,0:T(8,128)(2,1)S(1)} collective-permute-done((bf16[512,128]{1,0:T(8,128)(2,1)S(1)}, bf16[512,128]{1,0:T(8,128)(2,1)S(1)}, u32[]{:S(2)}, u32[]{:S(2)}) %collective-permute-start.2) | collective-permute-done | bytes 131104 | tf_op jit(solution)/shard_map/ppermute | solution.py:235
  44.3 11.2 %collective-permute-start.5 = (bf16[2,528,128]{2,1,0:T(8,128)(2,1)S(1)}, bf16[2,528,128]{2,1,0:T(8,128)(2,1)S(1)}, u32[]{:S(2)}, u32[]{:S(2)}) collective-permute-start(bf16[2,528,128]{2,1,0:T(8,128)(2,1)S(1)} %bitcast.60), channel_id=1, source_target_pairs={{0,224},{32,0},{64,32},{96,64},{128,96},{160,128},{192,160},{224,1... | collective-permute-start | bytes 811016 | tf_op jit(solution)/shard_map/ppermute | solution.py:230
  55.6 6.2 %collective-permute-done.5.refs_1_ = bf16[2,528,128]{2,1,0:T(8,128)(2,1)S(1)} collective-permute-done((bf16[2,528,128]{2,1,0:T(8,128)(2,1)S(1)}, bf16[2,528,128]{2,1,0:T(8,128)(2,1)S(1)}, u32[]{:S(2)}, u32[]{:S(2)}) %collective-permute-start.5) | collective-permute-done | bytes 270368 | tf_op jit(solution)/shard_map/ppermute | solution.py:230
  61.7 3.2 %collective-permute-start.6 = (bf16[2,528,128]{2,1,0:T(8,128)(2,1)S(1)}, bf16[2,528,128]{2,1,0:T(8,128)(2,1)S(1)}, u32[]{:S(2)}, u32[]{:S(2)}) collective-permute-start(bf16[2,528,128]{2,1,0:T(8,128)(2,1)S(1)} %collective-permute-done.5.refs_1_), channel_id=1, source_target_pairs={{0,224},{32,0},{64,32},{96,64},{128,96},{160,128},{192,160},{224,1... | collective-permute-start | bytes 811016 | tf_op jit(solution)/shard_map/ppermute | solution.py:230
  65.1 5.3 %collective-permute-done.6.refs_2_ = bf16[2,528,128]{2,1,0:T(8,128)(2,1)S(1)} collective-permute-done((bf16[2,528,128]{2,1,0:T(8,128)(2,1)S(1)}, bf16[2,528,128]{2,1,0:T(8,128)(2,1)S(1)}, u32[]{:S(2)}, u32[]{:S(2)}) %collective-permute-start.6) | collective-permute-done | bytes 270368 | tf_op jit(solution)/shard_map/ppermute | solution.py:230
  70.4 3.5 %collective-permute-done.4.refs_6_ = bf16[2,528,128]{2,1,0:T(8,128)(2,1)S(1)} collective-permute-done((bf16[2,528,128]{2,1,0:T(8,128)(2,1)S(1)}, bf16[2,528,128]{2,1,0:T(8,128)(2,1)S(1)}, u32[]{:S(2)}, u32[]{:S(2)}) %collective-permute-start.4) | collective-permute-done | bytes 270368 | tf_op jit(solution)/shard_map/ppermute | solution.py:230
  73.9 2.7 %collective-permute-start.7 = (bf16[2,528,128]{2,1,0:T(8,128)(2,1)S(1)}, bf16[2,528,128]{2,1,0:T(8,128)(2,1)S(1)}, u32[]{:S(2)}, u32[]{:S(2)}) collective-permute-start(bf16[2,528,128]{2,1,0:T(8,128)(2,1)S(1)} %collective-permute-done.6.refs_2_), channel_id=1, source_target_pairs={{0,224},{32,0},{64,32},{96,64},{128,96},{160,128},{192,160},{224,1... | collective-permute-start | bytes 811016 | tf_op jit(solution)/shard_map/ppermute | solution.py:230
  76.6 5.1 %collective-permute-done.8.refs_5_ = bf16[2,528,128]{2,1,0:T(8,128)(2,1)S(1)} collective-permute-done((bf16[2,528,128]{2,1,0:T(8,128)(2,1)S(1)}, bf16[2,528,128]{2,1,0:T(8,128)(2,1)S(1)}, u32[]{:S(2)}, u32[]{:S(2)}) %collective-permute-start.8) | collective-permute-done | bytes 270368 | tf_op jit(solution)/shard_map/ppermute | solution.py:230
  81.8 2.3 %copy.37 = bf16[16,528,128]{2,0,1:T(8,128)(2,1)S(1)} copy(bf16[16,528,128]{2,1,0:T(8,128)(2,1)} %bitcast.56) | data formatting | bytes 4325376 | tf_op jit(solution)/shard_map/optimization_barrier | solution.py:267
  84.1 4.5 %collective-permute-done.9.refs_4_ = bf16[2,528,128]{2,1,0:T(8,128)(2,1)S(1)} collective-permute-done((bf16[2,528,128]{2,1,0:T(8,128)(2,1)S(1)}, bf16[2,528,128]{2,1,0:T(8,128)(2,1)S(1)}, u32[]{:S(2)}, u32[]{:S(2)}) %collective-permute-start.9) | collective-permute-done | bytes 270368 | tf_op jit(solution)/shard_map/ppermute | solution.py:230
  88.6 7.8 %shard_map.102 = (bf16[128,2048]{1,0:T(8,128)(2,1)}, bf16[2048,128]{1,0:T(8,128)(2,1)S(1)}, f32[256,128]{1,0:T(8,128)S(1)}, bf16[16,528,128]{2,1,0:T(8,128)(2,1)S(1)}) custom-call(s32[4]{0:T(128)S(1)} %pad_add_fusion.place, s32[16,16]{1,0:T(8,128)S(1)} %fusion.7.index, bf16[2,528,128]{2,1,0:T(8,128)(2,1)S(1)} %bitcast.62, ...), custom_call_target="tpu_custom_call" | custom-call | flops 800000000 | bytes 10485760 | tf_op jit(solution)/shard_map/pallas_call | solution.py:208
  96.5 2.4 %shard_map.103 = (bf16[2,512,128]{2,1,0:T(8,128)(2,1)S(1)}, bf16[2,512,128]{2,1,0:T(8,128)(2,1)S(1)}, bf16[2,512,128]{2,1,0:T(8,128)(2,1)S(1)}) custom-call(s32[4]{0:T(128)S(1)} %pad_add_fusion.place, s32[16,16]{1,0:T(8,128)S(1)} %fusion.7.index, bf16[16,528,128]{2,1,0:T(8,128)(2,1)S(1)} %bitcast.58, bf16[2048,128]{1,0:T(8,128)(2,1)S(1)} %get-tuple-element.85.dz_t), custom_call_target="tpu_custom_call" | custom-call | flops 120000000 | bytes 3145728 | tf_op jit(solution)/shard_map/pallas_call | solution.py:208
  99.0 0.7 collective-permute-done.10
  99.8 0.9 collective-permute-start.12
  100.6 1.9 collective-permute-start.13
  102.5 3.6 %shard_map.104 = (bf16[2,512,128]{2,1,0:T(8,128)(2,1)S(1)}, bf16[2,512,128]{2,1,0:T(8,128)(2,1)S(1)}, bf16[2,512,128]{2,1,0:T(8,128)(2,1)S(1)}, bf16[2,512,128]{2,1,0:T(8,128)(2,1)S(1)}, bf16[2,512,128]{2,1,0:T(8,128)(2,1)S(1)}) custom-call(s32[4]{0:T(128)S(1)} %pad_add_fusion.place, s32[16,16]{1,0:T(8,128)S(1)} %fusion.7.index, ...), custom_call_target="tpu_custom_call" | custom-call | flops 200000000 | bytes 5242880 | tf_op jit(solution)/shard_map/pallas_call | solution.py:208
  106.2 2.6 %collective-permute-start.14 = (bf16[256,128]{1,0:T(8,128)(2,1)S(1)}, bf16[256,128]{1,0:T(8,128)(2,1)S(1)}, u32[]{:S(2)}, u32[]{:S(2)}) collective-permute-start(bf16[256,128]{1,0:T(8,128)(2,1)S(1)} %fusion.8), channel_id=1, source_target_pairs={{0,128},{32,160},{64,192},{96,224},{128,0},{160,32},{192,64},{224,... | collective-permute-start | bytes 196616 | tf_op jit(solution)/shard_map/ppermute | solution.py:235
  108.8 3.8 %shard_map.105 = bf16[8,768,128]{2,1,0:T(8,128)(2,1)S(1)} custom-call(s32[4]{0:T(128)S(1)} %pad_add_fusion.place, s32[16,16]{1,0:T(8,128)S(1)} %fusion.7.index, bf16[16,528,128]{2,1,0:T(8,128)(2,1)S(1)} %get-tuple-element.84.x, bf16[2048,128]{1,0:T(8,128)(2,1)S(1)} %get-tuple-element.85.dz_t), custom_call_target="tpu_custom_call" | custom-call | flops 200000000 | bytes 4194304 | tf_op jit(solution)/shard_map/pallas_call | solution.py:208
  112.5 1.3 collective-permute-done.14
  113.9 6.3 %collective-permute-start.18 = (bf16[8,768,128]{2,1,0:T(8,128)(2,1)S(1)}, bf16[8,768,128]{2,1,0:T(8,128)(2,1)S(1)}, u32[]{:S(2)}, u32[]{:S(2)}) collective-permute-start(bf16[8,768,128]{2,1,0:T(8,128)(2,1)S(1)} %shard_map.105), channel_id=1, source_target_pairs={{0,1},{1,0},{2,3},{3,2},{4,5},{5,4},{6,7},{7,6},{8,9},{9,8},{10,11... | collective-permute-start | bytes 4718600 | tf_op jit(solution)/shard_map/ppermute | solution.py:235
  120.4 1.5 collective-permute-start.15
  122.1 1.1 collective-permute-done.18.other
  123.2 5.1 %shard_map.106.grads = bf16[8,896,128]{2,1,0:T(8,128)(2,1)} custom-call(s32[4]{0:T(128)S(1)} %pad_add_fusion.place, s32[16,16]{1,0:T(8,128)S(1)} %fusion.7.index, bf16[16,528,128]{2,1,0:T(8,128)(2,1)S(1)} %get-tuple-element.84.x, bf16[2048,128]{1,0:T(8,128)(2,1)S(1)} %get-tuple-element.85.dz_t, bf16[8,768,128]{2,1,0:T(8,128)(2,1)S(1)} %collective-permute-done.18.other), custom_call_target="tpu_custom_call" | custom-call | flops 200000000 | bytes 6291456 | tf_op jit(solution)/shard_map/pallas_call | solution.py:208
  128.3 1.3 collective-permute-done.15
  129.9 1.5 collective-permute-start.19
  131.4 2.8 %shard_map.107 = bf16[8,896,128]{2,1,0:T(8,128)(2,1)} custom-call(s32[4]{0:T(128)S(1)} %pad_add_fusion.place, bf16[8,896,128]{2,1,0:T(8,128)(2,1)} %shard_map.106.grads, bf16[16,528,128]{2,1,0:T(8,128)(2,1)S(1)} %get-tuple-element.84.x, bf16[16,16,128]{2,1,0:T(8,128)(2,1)S(1)} %bitcast.63), custom_call_target="tpu_custom_call", output_to_operand_aliasing={{}: (1, {})} | custom-call | flops 70000000 | bytes 3145728 | tf_op jit(solution)/shard_map/pallas_call | solution.py:189
  134.2 2.6 %collective-permute-done.20 = bf16[2,512,128]{2,1,0:T(8,128)(2,1)S(1)} collective-permute-done((bf16[2,512,128]{2,1,0:T(8,128)(2,1)S(1)}, bf16[2,512,128]{2,1,0:T(8,128)(2,1)S(1)}, u32[]{:S(2)}, u32[]{:S(2)}) %collective-permute-start.20) | collective-permute-done | bytes 262176 | tf_op jit(solution)/shard_map/ppermute | solution.py:230
  136.8 1.3 collective-permute-done.19
  138.1 6.8 %all-to-all-start.1 = ((bf16[8,896,128]{2,1,0:T(8,128)(2,1)}), bf16[8,896,128]{2,1,0:T(8,128)(2,1)S(1)}, u32[]{:S(2)}, u32[]{:S(2)}) async-start(bf16[8,896,128]{2,1,0:T(8,128)(2,1)} %shard_map.107), calls=%async_computation.1 | async-start | bytes 3670016 | tf_op jit(solution)/shard_map/all_to_all | solution.py:341
  145.0 6.6 %collective-permute-start.24 = (bf16[256,128]{1,0:T(8,128)(2,1)S(1)}, bf16[256,128]{1,0:T(8,128)(2,1)S(1)}, u32[]{:S(2)}, u32[]{:S(2)}) collective-permute-start(bf16[256,128]{1,0:T(8,128)(2,1)S(1)} %add_convert_fusion.6), channel_id=1, source_target_pairs={{0,0},{1,16},{2,32},{3,48},{4,64},{5,80},{6,96},{7,112},{8,128},{9... | collective-permute-start | bytes 196616 | tf_op jit(solution)/shard_map/ppermute | solution.py:342
  151.7 0.7 copy-done.7
  152.5 2.4 %collective-permute-start.22 = (bf16[512,128]{1,0:T(8,128)(2,1)S(1)}, bf16[512,128]{1,0:T(8,128)(2,1)S(1)}, u32[]{:S(2)}, u32[]{:S(2)}) collective-permute-start(bf16[512,128]{1,0:T(8,128)(2,1)S(1)} %fusion.4), channel_id=1, source_target_pairs={{0,16},{16,0},{1,17},{17,1},{2,18},{18,2},{3,19},{19,3},{4,20},{20... | collective-permute-start | bytes 393224 | tf_op jit(solution)/shard_map/ppermute | solution.py:235
  154.9 13.4 %all-to-all-done.1 = bf16[8,896,128]{2,1,0:T(8,128)(2,1)S(1)} async-done(((bf16[8,896,128]{2,1,0:T(8,128)(2,1)}), bf16[8,896,128]{2,1,0:T(8,128)(2,1)S(1)}, u32[]{:S(2)}, u32[]{:S(2)}) %all-to-all-start.1) | async-done | bytes 1835040 | tf_op jit(solution)/shard_map/all_to_all | solution.py:341
  168.6 4.5 %collective-permute-start.25 = (f32[64,128]{1,0:T(8,128)S(1)}, f32[64,128]{1,0:T(8,128)S(1)}, u32[]{:S(2)}, u32[]{:S(2)}) collective-permute-start(f32[64,128]{1,0:T(8,128)S(1)} %slice.77), channel_id=1, source_target_pairs={{0,1},{1,0},{2,3},{3,2},{4,5},{5,4},{6,7},{7,6},{8,9},{9,8},{10,11... | collective-permute-start | bytes 98312 | tf_op jit(solution)/shard_map/ppermute | solution.py:235
  173.1 1.5 collective-permute-done.22
  174.7 5.0 %collective-permute-start.23 = (bf16[512,128]{1,0:T(8,128)(2,1)S(1)}, bf16[512,128]{1,0:T(8,128)(2,1)S(1)}, u32[]{:S(2)}, u32[]{:S(2)}) collective-permute-start(bf16[512,128]{1,0:T(8,128)(2,1)S(1)} %fusion.2), channel_id=1, source_target_pairs={{0,0},{1,16},{2,32},{3,48},{4,64},{5,80},{6,96},{7,112},{8,128},{9... | collective-permute-start | bytes 393224 | tf_op jit(solution)/shard_map/ppermute | solution.py:340
  181.0 0.9 reshape.95
  182.5 8.1 %collective-permute-done.23 = bf16[512,128]{1,0:T(8,128)(2,1)S(1)} collective-permute-done((bf16[512,128]{1,0:T(8,128)(2,1)S(1)}, bf16[512,128]{1,0:T(8,128)(2,1)S(1)}, u32[]{:S(2)}, u32[]{:S(2)}) %collective-permute-start.23) | collective-permute-done | bytes 131104 | tf_op jit(solution)/shard_map/ppermute | solution.py:340
  190.9 0.8 copy.43
  (74 shorter events, 4.7 us)
Async XLA Ops:
  7.2 3.3 %copy-start.4 = (bf16[128,512]{1,0:T(8,128)(2,1)S(1)}, bf16[128,512]{1,0:T(8,128)(2,1)}, u32[]{:S(2)}) copy-start(bf16[128,512]{1,0:T(8,128)(2,1)} %x.2) | copy-start | bytes 393220
  7.2 3.3 %copy-start.1 = (bf16[512,256]{1,0:T(8,128)(2,1)S(1)}, bf16[512,256]{1,0:T(8,128)(2,1)}, u32[]{:S(2)}) copy-start(bf16[512,256]{1,0:T(8,128)(2,1)} %u.1) | copy-start | bytes 786436
  7.2 66.7 %all-gather.3.cloned.1.call-start = ((), (), s32[]{:S(2)}) async-start(), calls=%async_computation.2 | async-start | bytes 2297856 | tf_op jit(solution)/shard_map/all_gather | solution.py:248
  11.5 14.7 %all-to-all-start = ((f32[16,2,16,128]{3,2,1,0:T(8,128)}), f32[16,2,16,128]{3,2,1,0:T(8,128)S(1)}, u32[]{:S(2)}, u32[]{:S(2)}) async-start(f32[16,2,16,128]{3,2,1,0:T(8,128)} %get-tuple-element.64), calls=%async_computation | async-start | bytes 524288 | tf_op jit(solution)/shard_map/all_to_all | solution.py:259
  18.4 7.8 %collective-permute-start = (bf16[512,128]{1,0:T(8,128)(2,1)S(1)}, bf16[512,128]{1,0:T(8,128)(2,1)S(1)}, u32[]{:S(2)}, u32[]{:S(2)}) collective-permute-start(bf16[512,128]{1,0:T(8,128)(2,1)S(1)} %get-tuple-element.63), channel_id=1, source_target_pairs={{0,0},{1,16},{2,32},{3,48},{4,64},{5,80},{6,96},{7,112},{8,128},{9... | collective-permute-start | bytes 393224 | tf_op jit(solution)/shard_map/ppermute | solution.py:258
  26.3 10.5 %collective-permute-start.1 = (bf16[2,16,128]{2,1,0:T(8,128)(2,1)S(1)}, bf16[2,16,128]{2,1,0:T(8,128)(2,1)S(1)}, u32[]{:S(2)}, u32[]{:S(2)}) collective-permute-start(bf16[2,16,128]{2,1,0:T(8,128)(2,1)S(1)} %reduce_sum.18), channel_id=1, source_target_pairs={{0,0},{1,16},{2,32},{3,48},{4,64},{5,80},{6,96},{7,112},{8,128},{9... | collective-permute-start | bytes 24584 | tf_op jit(solution)/shard_map/ppermute | solution.py:261
  30.9 13.5 %collective-permute-start.2 = (bf16[512,128]{1,0:T(8,128)(2,1)S(1)}, bf16[512,128]{1,0:T(8,128)(2,1)S(1)}, u32[]{:S(2)}, u32[]{:S(2)}) collective-permute-start(bf16[512,128]{1,0:T(8,128)(2,1)S(1)} %collective-permute-done), channel_id=1, source_target_pairs={{0,16},{16,0},{1,17},{17,1},{2,18},{18,2},{3,19},{19,3},{4,20},{20... | collective-permute-start | bytes 393224 | tf_op jit(solution)/shard_map/ppermute | solution.py:235
  44.3 17.4 %collective-permute-start.5 = (bf16[2,528,128]{2,1,0:T(8,128)(2,1)S(1)}, bf16[2,528,128]{2,1,0:T(8,128)(2,1)S(1)}, u32[]{:S(2)}, u32[]{:S(2)}) collective-permute-start(bf16[2,528,128]{2,1,0:T(8,128)(2,1)S(1)} %bitcast.60), channel_id=1, source_target_pairs={{0,224},{32,0},{64,32},{96,64},{128,96},{160,128},{192,160},{224,1... | collective-permute-start | bytes 811016 | tf_op jit(solution)/shard_map/ppermute | solution.py:230
  55.6 9.6 %collective-permute-start.3 = (bf16[2,528,128]{2,1,0:T(8,128)(2,1)S(1)}, bf16[2,528,128]{2,1,0:T(8,128)(2,1)S(1)}, u32[]{:S(2)}, u32[]{:S(2)}) collective-permute-start(bf16[2,528,128]{2,1,0:T(8,128)(2,1)S(1)} %bitcast.61), channel_id=1, source_target_pairs={{0,32},{32,64},{64,96},{96,128},{128,160},{160,192},{192,224},{224... | collective-permute-start | bytes 811016 | tf_op jit(solution)/shard_map/ppermute | solution.py:230
  61.7 8.7 %collective-permute-start.6 = (bf16[2,528,128]{2,1,0:T(8,128)(2,1)S(1)}, bf16[2,528,128]{2,1,0:T(8,128)(2,1)S(1)}, u32[]{:S(2)}, u32[]{:S(2)}) collective-permute-start(bf16[2,528,128]{2,1,0:T(8,128)(2,1)S(1)} %collective-permute-done.5.refs_1_), channel_id=1, source_target_pairs={{0,224},{32,0},{64,32},{96,64},{128,96},{160,128},{192,160},{224,1... | collective-permute-start | bytes 811016 | tf_op jit(solution)/shard_map/ppermute | solution.py:230
  65.1 8.7 %collective-permute-start.4 = (bf16[2,528,128]{2,1,0:T(8,128)(2,1)S(1)}, bf16[2,528,128]{2,1,0:T(8,128)(2,1)S(1)}, u32[]{:S(2)}, u32[]{:S(2)}) collective-permute-start(bf16[2,528,128]{2,1,0:T(8,128)(2,1)S(1)} %collective-permute-done.3.refs_7_), channel_id=1, source_target_pairs={{0,32},{32,64},{64,96},{96,128},{128,160},{160,192},{192,224},{224... | collective-permute-start | bytes 811016 | tf_op jit(solution)/shard_map/ppermute | solution.py:230
  73.9 7.8 %collective-permute-start.8 = (bf16[2,528,128]{2,1,0:T(8,128)(2,1)S(1)}, bf16[2,528,128]{2,1,0:T(8,128)(2,1)S(1)}, u32[]{:S(2)}, u32[]{:S(2)}) collective-permute-start(bf16[2,528,128]{2,1,0:T(8,128)(2,1)S(1)} %collective-permute-done.4.refs_6_), channel_id=1, source_target_pairs={{0,32},{32,64},{64,96},{96,128},{128,160},{160,192},{192,224},{224... | collective-permute-start | bytes 811016 | tf_op jit(solution)/shard_map/ppermute | solution.py:230
  73.9 10.2 %collective-permute-start.7 = (bf16[2,528,128]{2,1,0:T(8,128)(2,1)S(1)}, bf16[2,528,128]{2,1,0:T(8,128)(2,1)S(1)}, u32[]{:S(2)}, u32[]{:S(2)}) collective-permute-start(bf16[2,528,128]{2,1,0:T(8,128)(2,1)S(1)} %collective-permute-done.6.refs_2_), channel_id=1, source_target_pairs={{0,224},{32,0},{64,32},{96,64},{128,96},{160,128},{192,160},{224,1... | collective-permute-start | bytes 811016 | tf_op jit(solution)/shard_map/ppermute | solution.py:230
  81.7 6.9 %collective-permute-start.9 = (bf16[2,528,128]{2,1,0:T(8,128)(2,1)S(1)}, bf16[2,528,128]{2,1,0:T(8,128)(2,1)S(1)}, u32[]{:S(2)}, u32[]{:S(2)}) collective-permute-start(bf16[2,528,128]{2,1,0:T(8,128)(2,1)S(1)} %collective-permute-done.8.refs_5_), channel_id=1, source_target_pairs={{0,32},{32,64},{64,96},{96,128},{128,160},{160,192},{192,224},{224... | collective-permute-start | bytes 811016 | tf_op jit(solution)/shard_map/ppermute | solution.py:230
  81.8 6.8 %copy-start = (bf16[8448,128]{1,0:T(8,128)(2,1)S(1)}, bf16[8448,128]{1,0:T(8,128)(2,1)}, u32[]{:S(2)}) copy-start(bf16[8448,128]{1,0:T(8,128)(2,1)} %all-gather.3.cloned.1.call-done) | copy-start | bytes 6488068
  81.8 6.8 %copy-start.2 = (bf16[256,2048]{1,0:T(8,128)(2,1)S(1)}, bf16[256,2048]{1,0:T(8,128)(2,1)}, u32[]{:S(2)}) copy-start(bf16[256,2048]{1,0:T(8,128)(2,1)} %refs_9_.1) | copy-start | bytes 3145732
  81.8 6.8 %copy-start.3 = (bf16[128,2048]{1,0:T(8,128)(2,1)S(1)}, bf16[128,2048]{1,0:T(8,128)(2,1)}, u32[]{:S(2)}) copy-start(bf16[128,2048]{1,0:T(8,128)(2,1)} %refs_10_.1) | copy-start | bytes 1572868
  96.4 3.2 %collective-permute-start.10 = (bf16[256,128]{1,0:T(8,128)(2,1)S(1)}, bf16[256,128]{1,0:T(8,128)(2,1)S(1)}, u32[]{:S(2)}, u32[]{:S(2)}) collective-permute-start(bf16[256,128]{1,0:T(8,128)(2,1)S(1)} %convert_element_type.145), channel_id=1, source_target_pairs={{0,32},{32,0},{64,96},{96,64},{128,160},{160,128},{192,224},{224,1... | collective-permute-start | bytes 196616 | tf_op jit(solution)/shard_map/ppermute | solution.py:235
  99.7 6.5 %collective-permute-start.11 = (bf16[256,128]{1,0:T(8,128)(2,1)S(1)}, bf16[256,128]{1,0:T(8,128)(2,1)S(1)}, u32[]{:S(2)}, u32[]{:S(2)}) collective-permute-start(bf16[256,128]{1,0:T(8,128)(2,1)S(1)} %fusion.5), channel_id=1, source_target_pairs={{0,64},{32,96},{64,0},{96,32},{128,192},{160,224},{192,128},{224,1... | collective-permute-start | bytes 196616 | tf_op jit(solution)/shard_map/ppermute | solution.py:235
  99.8 14.1 %collective-permute-start.12 = (bf16[2,512,128]{2,1,0:T(8,128)(2,1)S(1)}, bf16[2,512,128]{2,1,0:T(8,128)(2,1)S(1)}, u32[]{:S(2)}, u32[]{:S(2)}) collective-permute-start(bf16[2,512,128]{2,1,0:T(8,128)(2,1)S(1)} %get-tuple-element.81), channel_id=1, source_target_pairs={{0,32},{32,64},{64,96},{96,128},{128,160},{160,192},{192,224},{224... | collective-permute-start | bytes 786440 | tf_op jit(solution)/shard_map/ppermute | solution.py:230
  100.6 13.2 %collective-permute-start.13 = (bf16[2,512,128]{2,1,0:T(8,128)(2,1)S(1)}, bf16[2,512,128]{2,1,0:T(8,128)(2,1)S(1)}, u32[]{:S(2)}, u32[]{:S(2)}) collective-permute-start(bf16[2,512,128]{2,1,0:T(8,128)(2,1)S(1)} %get-tuple-element.82), channel_id=1, source_target_pairs={{0,224},{32,0},{64,32},{96,64},{128,96},{160,128},{192,160},{224,1... | collective-permute-start | bytes 786440 | tf_op jit(solution)/shard_map/ppermute | solution.py:230
  106.2 7.7 %collective-permute-start.14 = (bf16[256,128]{1,0:T(8,128)(2,1)S(1)}, bf16[256,128]{1,0:T(8,128)(2,1)S(1)}, u32[]{:S(2)}, u32[]{:S(2)}) collective-permute-start(bf16[256,128]{1,0:T(8,128)(2,1)S(1)} %fusion.8), channel_id=1, source_target_pairs={{0,128},{32,160},{64,192},{96,224},{128,0},{160,32},{192,64},{224,... | collective-permute-start | bytes 196616 | tf_op jit(solution)/shard_map/ppermute | solution.py:235
  113.9 9.3 %collective-permute-start.18 = (bf16[8,768,128]{2,1,0:T(8,128)(2,1)S(1)}, bf16[8,768,128]{2,1,0:T(8,128)(2,1)S(1)}, u32[]{:S(2)}, u32[]{:S(2)}) collective-permute-start(bf16[8,768,128]{2,1,0:T(8,128)(2,1)S(1)} %shard_map.105), channel_id=1, source_target_pairs={{0,1},{1,0},{2,3},{3,2},{4,5},{5,4},{6,7},{7,6},{8,9},{9,8},{10,11... | collective-permute-start | bytes 4718600 | tf_op jit(solution)/shard_map/ppermute | solution.py:235
  120.2 8.1 %collective-permute-start.16 = (bf16[2,512,128]{2,1,0:T(8,128)(2,1)S(1)}, bf16[2,512,128]{2,1,0:T(8,128)(2,1)S(1)}, u32[]{:S(2)}, u32[]{:S(2)}) collective-permute-start(bf16[2,512,128]{2,1,0:T(8,128)(2,1)S(1)} %add_convert_fusion.3), channel_id=1, source_target_pairs={{0,224},{32,0},{64,32},{96,64},{128,96},{160,128},{192,160},{224,1... | collective-permute-start | bytes 786440 | tf_op jit(solution)/shard_map/ppermute | solution.py:230
  120.4 9.2 %collective-permute-start.15 = (bf16[2,512,128]{2,1,0:T(8,128)(2,1)S(1)}, bf16[2,512,128]{2,1,0:T(8,128)(2,1)S(1)}, u32[]{:S(2)}, u32[]{:S(2)}) collective-permute-start(bf16[2,512,128]{2,1,0:T(8,128)(2,1)S(1)} %add_convert_fusion.4), channel_id=1, source_target_pairs={{0,32},{32,64},{64,96},{96,128},{128,160},{160,192},{192,224},{224... | collective-permute-start | bytes 786440 | tf_op jit(solution)/shard_map/ppermute | solution.py:230
  122.0 6.3 %collective-permute-start.17 = (bf16[256,128]{1,0:T(8,128)(2,1)S(1)}, bf16[256,128]{1,0:T(8,128)(2,1)S(1)}, u32[]{:S(2)}, u32[]{:S(2)}) collective-permute-start(bf16[256,128]{1,0:T(8,128)(2,1)S(1)} %fusion.6), channel_id=1, source_target_pairs={{0,16},{16,0},{1,17},{17,1},{2,18},{18,2},{3,19},{19,3},{4,20},{20... | collective-permute-start | bytes 196616 | tf_op jit(solution)/shard_map/ppermute | solution.py:235
  129.7 7.1 %collective-permute-start.20 = (bf16[2,512,128]{2,1,0:T(8,128)(2,1)S(1)}, bf16[2,512,128]{2,1,0:T(8,128)(2,1)S(1)}, u32[]{:S(2)}, u32[]{:S(2)}) collective-permute-start(bf16[2,512,128]{2,1,0:T(8,128)(2,1)S(1)} %add_convert_fusion.1), channel_id=1, source_target_pairs={{0,224},{32,0},{64,32},{96,64},{128,96},{160,128},{192,160},{224,1... | collective-permute-start | bytes 786440 | tf_op jit(solution)/shard_map/ppermute | solution.py:230
  129.9 8.2 %collective-permute-start.19 = (bf16[2,512,128]{2,1,0:T(8,128)(2,1)S(1)}, bf16[2,512,128]{2,1,0:T(8,128)(2,1)S(1)}, u32[]{:S(2)}, u32[]{:S(2)}) collective-permute-start(bf16[2,512,128]{2,1,0:T(8,128)(2,1)S(1)} %add_convert_fusion.2), channel_id=1, source_target_pairs={{0,32},{32,64},{64,96},{96,128},{128,160},{160,192},{192,224},{224... | collective-permute-start | bytes 786440 | tf_op jit(solution)/shard_map/ppermute | solution.py:230
  136.8 14.9 %copy-start.5 = (bf16[2,512,128]{2,1,0:T(8,128)(2,1)}, bf16[2,512,128]{2,1,0:T(8,128)(2,1)S(1)}, u32[]{:S(2)}) copy-start(bf16[2,512,128]{2,1,0:T(8,128)(2,1)S(1)} %collective-permute-done.20) | copy-start | bytes 786436
  138.1 30.2 %all-to-all-start.1 = ((bf16[8,896,128]{2,1,0:T(8,128)(2,1)}), bf16[8,896,128]{2,1,0:T(8,128)(2,1)S(1)}, u32[]{:S(2)}, u32[]{:S(2)}) async-start(bf16[8,896,128]{2,1,0:T(8,128)(2,1)} %shard_map.107), calls=%async_computation.1 | async-start | bytes 3670016 | tf_op jit(solution)/shard_map/all_to_all | solution.py:341
  144.9 6.8 %collective-permute-start.21 = (bf16[2,512,128]{2,1,0:T(8,128)(2,1)S(1)}, bf16[2,512,128]{2,1,0:T(8,128)(2,1)S(1)}, u32[]{:S(2)}, u32[]{:S(2)}) collective-permute-start(bf16[2,512,128]{2,1,0:T(8,128)(2,1)S(1)} %add_convert_fusion), channel_id=1, source_target_pairs={{0,32},{32,64},{64,96},{96,128},{128,160},{160,192},{192,224},{224... | collective-permute-start | bytes 786440 | tf_op jit(solution)/shard_map/ppermute | solution.py:230
  145.0 37.5 %collective-permute-start.24 = (bf16[256,128]{1,0:T(8,128)(2,1)S(1)}, bf16[256,128]{1,0:T(8,128)(2,1)S(1)}, u32[]{:S(2)}, u32[]{:S(2)}) collective-permute-start(bf16[256,128]{1,0:T(8,128)(2,1)S(1)} %add_convert_fusion.6), channel_id=1, source_target_pairs={{0,0},{1,16},{2,32},{3,48},{4,64},{5,80},{6,96},{7,112},{8,128},{9... | collective-permute-start | bytes 196616 | tf_op jit(solution)/shard_map/ppermute | solution.py:342
  151.7 0.7 copy-start.7
  152.5 22.1 %copy-start.6 = (bf16[2,512,128]{2,1,0:T(8,128)(2,1)S(1)}, bf16[2,512,128]{2,1,0:T(8,128)(2,1)}, u32[]{:S(2)}) copy-start(bf16[2,512,128]{2,1,0:T(8,128)(2,1)} %copy-done.5) | copy-start | bytes 786436
  152.5 22.1 %collective-permute-start.22 = (bf16[512,128]{1,0:T(8,128)(2,1)S(1)}, bf16[512,128]{1,0:T(8,128)(2,1)S(1)}, u32[]{:S(2)}, u32[]{:S(2)}) collective-permute-start(bf16[512,128]{1,0:T(8,128)(2,1)S(1)} %fusion.4), channel_id=1, source_target_pairs={{0,16},{16,0},{1,17},{17,1},{2,18},{18,2},{3,19},{19,3},{4,20},{20... | collective-permute-start | bytes 393224 | tf_op jit(solution)/shard_map/ppermute | solution.py:235
  168.3 6.3 %copy-start.8 = (bf16[2,512,128]{2,1,0:T(8,128)(2,1)S(1)}, bf16[2,512,128]{2,1,0:T(8,128)(2,1)}, u32[]{:S(2)}) copy-start(bf16[2,512,128]{2,1,0:T(8,128)(2,1)} %copy-done.7) | copy-start | bytes 786436
  168.6 13.3 %collective-permute-start.25 = (f32[64,128]{1,0:T(8,128)S(1)}, f32[64,128]{1,0:T(8,128)S(1)}, u32[]{:S(2)}, u32[]{:S(2)}) collective-permute-start(f32[64,128]{1,0:T(8,128)S(1)} %slice.77), channel_id=1, source_target_pairs={{0,1},{1,0},{2,3},{3,2},{4,5},{5,4},{6,7},{7,6},{8,9},{9,8},{10,11... | collective-permute-start | bytes 98312 | tf_op jit(solution)/shard_map/ppermute | solution.py:235
  174.7 16.0 %collective-permute-start.23 = (bf16[512,128]{1,0:T(8,128)(2,1)S(1)}, bf16[512,128]{1,0:T(8,128)(2,1)S(1)}, u32[]{:S(2)}, u32[]{:S(2)}) collective-permute-start(bf16[512,128]{1,0:T(8,128)(2,1)S(1)} %fusion.2), channel_id=1, source_target_pairs={{0,0},{1,16},{2,32},{3,48},{4,64},{5,80},{6,96},{7,112},{8,128},{9... | collective-permute-start | bytes 393224 | tf_op jit(solution)/shard_map/ppermute | solution.py:340
Sparse Core Ops, SparseCore 0:
  10.6 49.2 all-gather.2

commit v6 on v5

--- a/solution.py
+++ b/solution.py
@@ -57,10 +57,7 @@
 
 def first_kernel(x, u, x_t, p):
     x_t[...] = x[...].T
-    whole = dot(u[...].T, x_t[...], NN)
-    for s in range(SH):
-        for j in range(2):
-            p[s, j] = whole[(s ^ j) * RS : (s ^ j) * RS + RS]
+    p[...] = dot(u[...].T, x_t[...], NN).reshape(SH, RS, TOK)
 
 
 def forward_kernel(place, index, *refs):
@@ -237,6 +234,7 @@
 
 def on_device(inputs, cotangent, sparse_blocks, block_index, u_factor, v_factor):
     turn = [(r * SH + c, c * SH + r) for r in range(SH) for c in range(SH)]
+    turn_pair = [(r * SH + c, (c ^ 1) * SH + r) for r in range(SH) for c in range(SH)]
     place = jnp.stack(
         [lax.axis_index("z"), lax.axis_index("xh"), lax.axis_index("core"), lax.axis_index(ROW)]
     ).astype(jnp.int32)
@@ -249,7 +247,7 @@
 
     mine, p = call(
         first_kernel,
-        (shape(FEAT, TOK), shape(SH, 2, RS, TOK, kind=F32)),
+        (shape(FEAT, TOK), shape(SH, RS, TOK, kind=F32)),
         40_000_000,
         1 << 19,
         (inputs, u_factor),
@@ -258,8 +256,13 @@
     turned = lax.ppermute(mine, ALL, turn)
     p_in = lax.all_to_all(p, COL, 0, 0)
     turned, p_in = lax.optimization_barrier((turned, p_in))
-    p = lax.ppermute(jnp.sum(p_in, axis=0).astype(BF16), ALL, turn)
-    parts = [turned, p[0], meet(turned, "xh", 1), p[1]]
+    p = jnp.sum(p_in, axis=0).astype(BF16)
+    parts = [
+        turned,
+        lax.ppermute(p, ALL, turn),
+        meet(turned, "xh", 1),
+        lax.ppermute(p, ALL, turn_pair),
+    ]
     held = {0: jnp.concatenate(parts).reshape(2, ROWS, TOK)}
     for step in (1, 2, 3):
         held[-step], held[step] = shift(held[1 - step], 1), shift(held[step - 1], -1)
@@ -332,7 +335,7 @@
     up, down = shift(add(back[2], up), 1), shift(add(back[7], down), -1)
     q_t = (q + q_in.astype(F32)).astype(BF16)
     grads = u_call(place, grads, x_all, q_t.reshape(SH, RS, TOK))
-    up, down, grads, q_t = lax.optimization_barrier((up, down, grads, q_t))
+    up, down, _, q_t = lax.optimization_barrier((up, down, grads, q_t))
 
     up = shift(add(back[1], up), 1)
     other = add(back[0][1], up[1], down[1])

time: 199 us -> 193 us (0.970)
  waiting for transfers between devices: 73 us -> 47.7 us
  blocking collectives: 0 us -> 16.1 us
  other arithmetic: 1.75 us -> 4.27 us
    all_to_all x0 -> x1, blocking collectives: none -> 16.1 us  [on_device(): p_in = lax.all_to_all(p, COL, 0, 0)]
    all_to_all x1, waiting for transfers between devices: 13.4 us -> 2.5 us  [on_device(): grads_in = lax.all_to_all(grads, ('xl', 'y'), 0, 0)]
    ppermute x8, waiting for transfers between devices: 12.1 us -> 2.4 us  [meet(): return lax.ppermute(x, axis, [(i, i ^ flip) for i in range(count)])]
    all_to_all x1 -> x0, starting transfers between devices: 6.91 us -> none  [on_device(): p_in = lax.all_to_all(p, COL, 0, 0)]
    ppermute x8, starting transfers between devices: 16.2 us -> 22.5 us  [meet(): return lax.ppermute(x, axis, [(i, i ^ flip) for i in range(count)])]
    ppermute x1, waiting for transfers between devices: 3.46 us -> 0.01 us  [on_device(): turned = lax.ppermute(mine, ALL, turn)]
    convert_element_type x7, other arithmetic: 0.49 us -> 3.02 us  [add(): return sum((t.astype(F32) for t in terms)).astype(BF16)]
    ppermute x1 -> x2, waiting for transfers between devices: 5.85 us -> 3.95 us  [the longest x1 2.41 us: on_device(): lax.ppermute(p, ALL, turn)]
  transfers between devices with their start and end apart: 29 -> 29, of which waited for: 19 -> 15; matrix products, arithmetic and copies ran while one was open for 3% -> 4% of each run, Pallas kernels for 9% -> 8%
where the time goes in v6:
time: 193 us
  starting transfers between devices  75.2 us (39%)
  waiting for transfers between devices  47.7 us (25%)
  Pallas kernels  25.8 us (13%)
  blocking collectives  16.1 us (8%)
  between operations  14.4 us (7%)
  local copies, waits for them, and re-layouts  9.02 us (5%)
  other arithmetic  4.27 us (2%)
    ppermute x14, waiting for transfers between devices, shift(): return lax.ppermute(x, 'z', [(i, (i + by) % NZ) for i in range(NZ)])  30.3 us
    pallas_call x6, Pallas kernels, call(): pl.pallas_call(kernel, out_shape=out_shape, in_specs=[smem] * scalars + [...  23 us
    ppermute x14, starting transfers between devices, shift(): return lax.ppermute(x, 'z', [(i, (i + by) % NZ) for i in range(NZ)])  22.9 us
    ppermute x8, starting transfers between devices, meet(): return lax.ppermute(x, axis, [(i, i ^ flip) for i in range(count)])  22.5 us
    all_to_all x1, blocking collectives, on_device(): p_in = lax.all_to_all(p, COL, 0, 0)  16.1 us
    ppermute x1, waiting for transfers between devices, on_device(): x_grad_t = lax.ppermute(total, ALL, turn)  8.61 us
    ppermute x1, starting transfers between devices, on_device(): x_grad_t = lax.ppermute(total, ALL, turn)  6.24 us
    ppermute x1, starting transfers between devices, on_device(): q_turned = lax.ppermute(q_t, ALL, turn)  6.14 us
  transfers between devices with their start and end apart: 29, of which 15 were waited for; matrix products, arithmetic and copies ran while one was open for 4% of the time, Pallas kernels for 8%

profile of v6, /device:TPU:1, one launch (start us, length us, event | category | flops | bytes accessed | tf_op | source)
XLA Modules:
  0.0 192.8 jit_solution(16136256497207508606)
XLA Ops:
  7.2 0.7 convert_bitcast_fusion
  8.0 1.2 reshape.90
  9.7 0.8 copy.36
  10.8 6.0 %collective-permute-start = (bf16[512,128]{1,0:T(8,128)(2,1)S(1)}, bf16[512,128]{1,0:T(8,128)(2,1)S(1)}, u32[]{:S(2)}, u32[]{:S(2)}) collective-permute-start(bf16[512,128]{1,0:T(8,128)(2,1)S(1)} %get-tuple-element.62), channel_id=1, source_target_pairs={{0,0},{1,16},{2,32},{3,48},{4,64},{5,80},{6,96},{7,112},{8,128},{9... | collective-permute-start | bytes 393224 | tf_op jit(solution)/shard_map/ppermute | solution.py:256
  16.9 16.1 %all_to_all.10 = f32[16,16,128]{2,1,0:T(8,128)S(1)} all-to-all(f32[16,16,128]{2,1,0:T(8,128)S(1)} %get-tuple-element.63), channel_id=1, replica_groups=mesh['z'=8,'xh'=2,'xl'=2,'y'=4,'core'=2] {'xl','y','core'}, dimensions={0} | all-to-all | bytes 262144 | tf_op jit(solution)/shard_map/all_to_all | solution.py:257
  33.0 0.8 collective-permute-start.2
  33.8 5.3 %collective-permute-start.1 = (bf16[16,128]{1,0:T(8,128)(2,1)S(1)}, bf16[16,128]{1,0:T(8,128)(2,1)S(1)}, u32[]{:S(2)}, u32[]{:S(2)}) collective-permute-start(bf16[16,128]{1,0:T(8,128)(2,1)S(1)} %reduce_sum.18), channel_id=1, source_target_pairs={{0,0},{1,16},{2,32},{3,48},{4,64},{5,80},{6,96},{7,112},{8,128},{9... | collective-permute-start | bytes 12296 | tf_op jit(solution)/shard_map/ppermute | solution.py:262
  39.2 2.4 %collective-permute-done.1 = bf16[16,128]{1,0:T(8,128)(2,1)S(1)} collective-permute-done((bf16[16,128]{1,0:T(8,128)(2,1)S(1)}, bf16[16,128]{1,0:T(8,128)(2,1)S(1)}, u32[]{:S(2)}, u32[]{:S(2)}) %collective-permute-start.1) | collective-permute-done | bytes 4128 | tf_op jit(solution)/shard_map/ppermute | solution.py:262
  41.6 1.5 collective-permute-done.3
  43.2 9.5 %collective-permute-start.6 = (bf16[2,528,128]{2,1,0:T(8,128)(2,1)S(1)}, bf16[2,528,128]{2,1,0:T(8,128)(2,1)S(1)}, u32[]{:S(2)}, u32[]{:S(2)}) collective-permute-start(bf16[2,528,128]{2,1,0:T(8,128)(2,1)S(1)} %bitcast.56), channel_id=1, source_target_pairs={{0,224},{32,0},{64,32},{96,64},{128,96},{160,128},{192,160},{224,1... | collective-permute-start | bytes 811016 | tf_op jit(solution)/shard_map/ppermute | solution.py:227
  52.7 5.3 %collective-permute-done.6.refs_1_ = bf16[2,528,128]{2,1,0:T(8,128)(2,1)S(1)} collective-permute-done((bf16[2,528,128]{2,1,0:T(8,128)(2,1)S(1)}, bf16[2,528,128]{2,1,0:T(8,128)(2,1)S(1)}, u32[]{:S(2)}, u32[]{:S(2)}) %collective-permute-start.6) | collective-permute-done | bytes 270368 | tf_op jit(solution)/shard_map/ppermute | solution.py:227
  58.1 3.4 %collective-permute-start.7 = (bf16[2,528,128]{2,1,0:T(8,128)(2,1)S(1)}, bf16[2,528,128]{2,1,0:T(8,128)(2,1)S(1)}, u32[]{:S(2)}, u32[]{:S(2)}) collective-permute-start(bf16[2,528,128]{2,1,0:T(8,128)(2,1)S(1)} %collective-permute-done.6.refs_1_), channel_id=1, source_target_pairs={{0,224},{32,0},{64,32},{96,64},{128,96},{160,128},{192,160},{224,1... | collective-permute-start | bytes 811016 | tf_op jit(solution)/shard_map/ppermute | solution.py:227
  61.5 4.4 %collective-permute-done.7.refs_2_ = bf16[2,528,128]{2,1,0:T(8,128)(2,1)S(1)} collective-permute-done((bf16[2,528,128]{2,1,0:T(8,128)(2,1)S(1)}, bf16[2,528,128]{2,1,0:T(8,128)(2,1)S(1)}, u32[]{:S(2)}, u32[]{:S(2)}) %collective-permute-start.7) | collective-permute-done | bytes 270368 | tf_op jit(solution)/shard_map/ppermute | solution.py:227
  65.9 3.1 %collective-permute-done.5.refs_6_ = bf16[2,528,128]{2,1,0:T(8,128)(2,1)S(1)} collective-permute-done((bf16[2,528,128]{2,1,0:T(8,128)(2,1)S(1)}, bf16[2,528,128]{2,1,0:T(8,128)(2,1)S(1)}, u32[]{:S(2)}, u32[]{:S(2)}) %collective-permute-start.5) | collective-permute-done | bytes 270368 | tf_op jit(solution)/shard_map/ppermute | solution.py:227
  69.0 2.7 %collective-permute-start.8 = (bf16[2,528,128]{2,1,0:T(8,128)(2,1)S(1)}, bf16[2,528,128]{2,1,0:T(8,128)(2,1)S(1)}, u32[]{:S(2)}, u32[]{:S(2)}) collective-permute-start(bf16[2,528,128]{2,1,0:T(8,128)(2,1)S(1)} %collective-permute-done.7.refs_2_), channel_id=1, source_target_pairs={{0,224},{32,0},{64,32},{96,64},{128,96},{160,128},{192,160},{224,1... | collective-permute-start | bytes 811016 | tf_op jit(solution)/shard_map/ppermute | solution.py:227
  71.7 3.8 %collective-permute-done.9.refs_5_ = bf16[2,528,128]{2,1,0:T(8,128)(2,1)S(1)} collective-permute-done((bf16[2,528,128]{2,1,0:T(8,128)(2,1)S(1)}, bf16[2,528,128]{2,1,0:T(8,128)(2,1)S(1)}, u32[]{:S(2)}, u32[]{:S(2)}) %collective-permute-start.9) | collective-permute-done | bytes 270368 | tf_op jit(solution)/shard_map/ppermute | solution.py:227
  75.6 2.3 %copy.37 = bf16[16,528,128]{2,0,1:T(8,128)(2,1)S(1)} copy(bf16[16,528,128]{2,1,0:T(8,128)(2,1)} %bitcast.52) | data formatting | bytes 4325376 | tf_op jit(solution)/shard_map/optimization_barrier | solution.py:270
  78.0 4.1 %collective-permute-done.10.refs_4_ = bf16[2,528,128]{2,1,0:T(8,128)(2,1)S(1)} collective-permute-done((bf16[2,528,128]{2,1,0:T(8,128)(2,1)S(1)}, bf16[2,528,128]{2,1,0:T(8,128)(2,1)S(1)}, u32[]{:S(2)}, u32[]{:S(2)}) %collective-permute-start.10) | collective-permute-done | bytes 270368 | tf_op jit(solution)/shard_map/ppermute | solution.py:227
  82.1 7.8 %shard_map.102 = (bf16[128,2048]{1,0:T(8,128)(2,1)}, bf16[2048,128]{1,0:T(8,128)(2,1)S(1)}, f32[256,128]{1,0:T(8,128)S(1)}, bf16[16,528,128]{2,1,0:T(8,128)(2,1)S(1)}) custom-call(s32[4]{0:T(128)S(1)} %pad_add_fusion.place, s32[16,16]{1,0:T(8,128)S(1)} %fusion.7.index, bf16[2,528,128]{2,1,0:T(8,128)(2,1)S(1)} %bitcast.58, ...), custom_call_target="tpu_custom_call" | custom-call | flops 800000000 | bytes 10485760 | tf_op jit(solution)/shard_map/pallas_call | solution.py:205
  90.0 2.4 %shard_map.103 = (bf16[2,512,128]{2,1,0:T(8,128)(2,1)S(1)}, bf16[2,512,128]{2,1,0:T(8,128)(2,1)S(1)}, bf16[2,512,128]{2,1,0:T(8,128)(2,1)S(1)}) custom-call(s32[4]{0:T(128)S(1)} %pad_add_fusion.place, s32[16,16]{1,0:T(8,128)S(1)} %fusion.7.index, bf16[16,528,128]{2,1,0:T(8,128)(2,1)S(1)} %bitcast.54, bf16[2048,128]{1,0:T(8,128)(2,1)S(1)} %get-tuple-element.84.dz_t), custom_call_target="tpu_custom_call" | custom-call | flops 120000000 | bytes 3145728 | tf_op jit(solution)/shard_map/pallas_call | solution.py:205
  93.4 0.9 collective-permute-start.13
  94.3 1.9 collective-permute-start.14
  96.1 3.6 %shard_map.104 = (bf16[2,512,128]{2,1,0:T(8,128)(2,1)S(1)}, bf16[2,512,128]{2,1,0:T(8,128)(2,1)S(1)}, bf16[2,512,128]{2,1,0:T(8,128)(2,1)S(1)}, bf16[2,512,128]{2,1,0:T(8,128)(2,1)S(1)}, bf16[2,512,128]{2,1,0:T(8,128)(2,1)S(1)}) custom-call(s32[4]{0:T(128)S(1)} %pad_add_fusion.place, s32[16,16]{1,0:T(8,128)S(1)} %fusion.7.index, ...), custom_call_target="tpu_custom_call" | custom-call | flops 200000000 | bytes 5242880 | tf_op jit(solution)/shard_map/pallas_call | solution.py:205
  99.8 4.7 %collective-permute-start.15 = (bf16[256,128]{1,0:T(8,128)(2,1)S(1)}, bf16[256,128]{1,0:T(8,128)(2,1)S(1)}, u32[]{:S(2)}, u32[]{:S(2)}) collective-permute-start(bf16[256,128]{1,0:T(8,128)(2,1)S(1)} %fusion.8), channel_id=1, source_target_pairs={{0,128},{32,160},{64,192},{96,224},{128,0},{160,32},{192,64},{224,... | collective-permute-start | bytes 196616 | tf_op jit(solution)/shard_map/ppermute | solution.py:232
  104.5 3.8 %shard_map.105 = bf16[8,768,128]{2,1,0:T(8,128)(2,1)S(1)} custom-call(s32[4]{0:T(128)S(1)} %pad_add_fusion.place, s32[16,16]{1,0:T(8,128)S(1)} %fusion.7.index, bf16[16,528,128]{2,1,0:T(8,128)(2,1)S(1)} %get-tuple-element.83.x, bf16[2048,128]{1,0:T(8,128)(2,1)S(1)} %get-tuple-element.84.dz_t), custom_call_target="tpu_custom_call" | custom-call | flops 200000000 | bytes 4194304 | tf_op jit(solution)/shard_map/pallas_call | solution.py:205
  108.3 7.8 %collective-permute-start.19 = (bf16[8,768,128]{2,1,0:T(8,128)(2,1)S(1)}, bf16[8,768,128]{2,1,0:T(8,128)(2,1)S(1)}, u32[]{:S(2)}, u32[]{:S(2)}) collective-permute-start(bf16[8,768,128]{2,1,0:T(8,128)(2,1)S(1)} %shard_map.105), channel_id=1, source_target_pairs={{0,1},{1,0},{2,3},{3,2},{4,5},{5,4},{6,7},{7,6},{8,9},{9,8},{10,11... | collective-permute-start | bytes 4718600 | tf_op jit(solution)/shard_map/ppermute | solution.py:232
  116.3 1.5 collective-permute-start.16
  117.9 1.2 collective-permute-start.18
  119.1 5.1 %shard_map.106.grads = bf16[8,896,128]{2,1,0:T(8,128)(2,1)} custom-call(s32[4]{0:T(128)S(1)} %pad_add_fusion.place, s32[16,16]{1,0:T(8,128)S(1)} %fusion.7.index, bf16[16,528,128]{2,1,0:T(8,128)(2,1)S(1)} %get-tuple-element.83.x, bf16[2048,128]{1,0:T(8,128)(2,1)S(1)} %get-tuple-element.84.dz_t, bf16[8,768,128]{2,1,0:T(8,128)(2,1)S(1)} %collective-permute-done.19.other), custom_call_target="tpu_custom_call" | custom-call | flops 200000000 | bytes 6291456 | tf_op jit(solution)/shard_map/pallas_call | solution.py:205
  124.2 1.3 collective-permute-done.16
  126.3 2.8 %shard_map.107 = bf16[8,896,128]{2,1,0:T(8,128)(2,1)} custom-call(s32[4]{0:T(128)S(1)} %pad_add_fusion.place, bf16[8,896,128]{2,1,0:T(8,128)(2,1)} %shard_map.106.grads, bf16[16,528,128]{2,1,0:T(8,128)(2,1)S(1)} %get-tuple-element.83.x, bf16[16,16,128]{2,1,0:T(8,128)(2,1)S(1)} %bitcast.59), custom_call_target="tpu_custom_call", output_to_operand_aliasing={{}: (1, {})} | custom-call | flops 70000000 | bytes 3145728 | tf_op jit(solution)/shard_map/pallas_call | solution.py:186
  129.1 6.0 %all-to-all-start.1 = ((bf16[8,896,128]{2,1,0:T(8,128)(2,1)}), bf16[8,896,128]{2,1,0:T(8,128)(2,1)S(1)}, u32[]{:S(2)}, u32[]{:S(2)}) async-start(bf16[8,896,128]{2,1,0:T(8,128)(2,1)} %shard_map.107), calls=%async_computation.1 | async-start | bytes 3670016 | tf_op jit(solution)/shard_map/all_to_all | solution.py:344
  135.1 2.7 %collective-permute-start.21 = (bf16[2,512,128]{2,1,0:T(8,128)(2,1)S(1)}, bf16[2,512,128]{2,1,0:T(8,128)(2,1)S(1)}, u32[]{:S(2)}, u32[]{:S(2)}) collective-permute-start(bf16[2,512,128]{2,1,0:T(8,128)(2,1)S(1)} %add_convert_fusion.1), channel_id=1, source_target_pairs={{0,224},{32,0},{64,32},{96,64},{128,96},{160,128},{192,160},{224,1... | collective-permute-start | bytes 786440 | tf_op jit(solution)/shard_map/ppermute | solution.py:227
  137.8 1.0 add_convert_fusion.2
  139.0 3.4 %collective-permute-done.21 = bf16[2,512,128]{2,1,0:T(8,128)(2,1)S(1)} collective-permute-done((bf16[2,512,128]{2,1,0:T(8,128)(2,1)S(1)}, bf16[2,512,128]{2,1,0:T(8,128)(2,1)S(1)}, u32[]{:S(2)}, u32[]{:S(2)}) %collective-permute-start.21) | collective-permute-done | bytes 262176 | tf_op jit(solution)/shard_map/ppermute | solution.py:227
  142.3 4.2 %collective-permute-done.20 = bf16[2,512,128]{2,1,0:T(8,128)(2,1)S(1)} collective-permute-done((bf16[2,512,128]{2,1,0:T(8,128)(2,1)S(1)}, bf16[2,512,128]{2,1,0:T(8,128)(2,1)S(1)}, u32[]{:S(2)}, u32[]{:S(2)}) %collective-permute-start.20) | collective-permute-done | bytes 262176 | tf_op jit(solution)/shard_map/ppermute | solution.py:227
  146.7 6.1 %collective-permute-start.25 = (bf16[256,128]{1,0:T(8,128)(2,1)S(1)}, bf16[256,128]{1,0:T(8,128)(2,1)S(1)}, u32[]{:S(2)}, u32[]{:S(2)}) collective-permute-start(bf16[256,128]{1,0:T(8,128)(2,1)S(1)} %add_convert_fusion.6), channel_id=1, source_target_pairs={{0,0},{1,16},{2,32},{3,48},{4,64},{5,80},{6,96},{7,112},{8,128},{9... | collective-permute-start | bytes 196616 | tf_op jit(solution)/shard_map/ppermute | solution.py:345
  153.4 0.7 fusion.4
  154.2 1.7 collective-permute-start.23
  155.9 2.5 %all-to-all-done.1 = bf16[8,896,128]{2,1,0:T(8,128)(2,1)S(1)} async-done(((bf16[8,896,128]{2,1,0:T(8,128)(2,1)}), bf16[8,896,128]{2,1,0:T(8,128)(2,1)S(1)}, u32[]{:S(2)}, u32[]{:S(2)}) %all-to-all-start.1) | async-done | bytes 1835040 | tf_op jit(solution)/shard_map/all_to_all | solution.py:344
  158.7 5.9 %collective-permute-start.26 = (f32[64,128]{1,0:T(8,128)S(1)}, f32[64,128]{1,0:T(8,128)S(1)}, u32[]{:S(2)}, u32[]{:S(2)}) collective-permute-start(f32[64,128]{1,0:T(8,128)S(1)} %slice.67), channel_id=1, source_target_pairs={{0,1},{1,0},{2,3},{3,2},{4,5},{5,4},{6,7},{7,6},{8,9},{9,8},{10,11... | collective-permute-start | bytes 98312 | tf_op jit(solution)/shard_map/ppermute | solution.py:232
  164.6 1.7 collective-permute-done.23
  166.3 1.0 fusion.2
  167.3 6.2 %collective-permute-start.24 = (bf16[512,128]{1,0:T(8,128)(2,1)S(1)}, bf16[512,128]{1,0:T(8,128)(2,1)S(1)}, u32[]{:S(2)}, u32[]{:S(2)}) collective-permute-start(bf16[512,128]{1,0:T(8,128)(2,1)S(1)} %fusion.2), channel_id=1, source_target_pairs={{0,0},{1,16},{2,32},{3,48},{4,64},{5,80},{6,96},{7,112},{8,128},{9... | collective-permute-start | bytes 393224 | tf_op jit(solution)/shard_map/ppermute | solution.py:343
  173.7 0.7 copy.49
  174.8 0.9 reshape.95
  176.3 8.6 %collective-permute-done.24 = bf16[512,128]{1,0:T(8,128)(2,1)S(1)} collective-permute-done((bf16[512,128]{1,0:T(8,128)(2,1)S(1)}, bf16[512,128]{1,0:T(8,128)(2,1)S(1)}, u32[]{:S(2)}, u32[]{:S(2)}) %collective-permute-start.24) | collective-permute-done | bytes 131104 | tf_op jit(solution)/shard_map/ppermute | solution.py:343
  185.2 0.8 copy.43
  (72 shorter events, 5.8 us)
Async XLA Ops:
  7.2 3.3 %copy-start.4 = (bf16[128,512]{1,0:T(8,128)(2,1)S(1)}, bf16[128,512]{1,0:T(8,128)(2,1)}, u32[]{:S(2)}) copy-start(bf16[128,512]{1,0:T(8,128)(2,1)} %x.2) | copy-start | bytes 393220
  7.2 3.3 %copy-start.1 = (bf16[512,256]{1,0:T(8,128)(2,1)S(1)}, bf16[512,256]{1,0:T(8,128)(2,1)}, u32[]{:S(2)}) copy-start(bf16[512,256]{1,0:T(8,128)(2,1)} %u.1) | copy-start | bytes 786436
  7.2 61.8 %all-gather.3.cloned.1.call-start = ((), (), s32[]{:S(2)}) async-start(), calls=%async_computation.2 | async-start | bytes 2297856 | tf_op jit(solution)/shard_map/all_gather | solution.py:246
  10.8 22.2 %collective-permute-start = (bf16[512,128]{1,0:T(8,128)(2,1)S(1)}, bf16[512,128]{1,0:T(8,128)(2,1)S(1)}, u32[]{:S(2)}, u32[]{:S(2)}) collective-permute-start(bf16[512,128]{1,0:T(8,128)(2,1)S(1)} %get-tuple-element.62), channel_id=1, source_target_pairs={{0,0},{1,16},{2,32},{3,48},{4,64},{5,80},{6,96},{7,112},{8,128},{9... | collective-permute-start | bytes 393224 | tf_op jit(solution)/shard_map/ppermute | solution.py:256
  33.0 10.2 %collective-permute-start.2 = (bf16[512,128]{1,0:T(8,128)(2,1)S(1)}, bf16[512,128]{1,0:T(8,128)(2,1)S(1)}, u32[]{:S(2)}, u32[]{:S(2)}) collective-permute-start(bf16[512,128]{1,0:T(8,128)(2,1)S(1)} %collective-permute-done), channel_id=1, source_target_pairs={{0,16},{16,0},{1,17},{17,1},{2,18},{18,2},{3,19},{19,3},{4,20},{20... | collective-permute-start | bytes 393224 | tf_op jit(solution)/shard_map/ppermute | solution.py:232
  33.8 7.8 %collective-permute-start.1 = (bf16[16,128]{1,0:T(8,128)(2,1)S(1)}, bf16[16,128]{1,0:T(8,128)(2,1)S(1)}, u32[]{:S(2)}, u32[]{:S(2)}) collective-permute-start(bf16[16,128]{1,0:T(8,128)(2,1)S(1)} %reduce_sum.18), channel_id=1, source_target_pairs={{0,0},{1,16},{2,32},{3,48},{4,64},{5,80},{6,96},{7,112},{8,128},{9... | collective-permute-start | bytes 12296 | tf_op jit(solution)/shard_map/ppermute | solution.py:262
  39.1 4.0 %collective-permute-start.3 = (bf16[16,128]{1,0:T(8,128)(2,1)S(1)}, bf16[16,128]{1,0:T(8,128)(2,1)S(1)}, u32[]{:S(2)}, u32[]{:S(2)}) collective-permute-start(bf16[16,128]{1,0:T(8,128)(2,1)S(1)} %reduce_sum.18), channel_id=1, source_target_pairs={{0,16},{1,0},{2,48},{3,32},{4,80},{5,64},{6,112},{7,96},{8,144},{9... | collective-permute-start | bytes 12296 | tf_op jit(solution)/shard_map/ppermute | solution.py:264
  43.2 14.9 %collective-permute-start.6 = (bf16[2,528,128]{2,1,0:T(8,128)(2,1)S(1)}, bf16[2,528,128]{2,1,0:T(8,128)(2,1)S(1)}, u32[]{:S(2)}, u32[]{:S(2)}) collective-permute-start(bf16[2,528,128]{2,1,0:T(8,128)(2,1)S(1)} %bitcast.56), channel_id=1, source_target_pairs={{0,224},{32,0},{64,32},{96,64},{128,96},{160,128},{192,160},{224,1... | collective-permute-start | bytes 811016 | tf_op jit(solution)/shard_map/ppermute | solution.py:227
  52.7 8.7 %collective-permute-start.4 = (bf16[2,528,128]{2,1,0:T(8,128)(2,1)S(1)}, bf16[2,528,128]{2,1,0:T(8,128)(2,1)S(1)}, u32[]{:S(2)}, u32[]{:S(2)}) collective-permute-start(bf16[2,528,128]{2,1,0:T(8,128)(2,1)S(1)} %bitcast.57), channel_id=1, source_target_pairs={{0,32},{32,64},{64,96},{96,128},{128,160},{160,192},{192,224},{224... | collective-permute-start | bytes 811016 | tf_op jit(solution)/shard_map/ppermute | solution.py:227
  58.1 7.8 %collective-permute-start.7 = (bf16[2,528,128]{2,1,0:T(8,128)(2,1)S(1)}, bf16[2,528,128]{2,1,0:T(8,128)(2,1)S(1)}, u32[]{:S(2)}, u32[]{:S(2)}) collective-permute-start(bf16[2,528,128]{2,1,0:T(8,128)(2,1)S(1)} %collective-permute-done.6.refs_1_), channel_id=1, source_target_pairs={{0,224},{32,0},{64,32},{96,64},{128,96},{160,128},{192,160},{224,1... | collective-permute-start | bytes 811016 | tf_op jit(solution)/shard_map/ppermute | solution.py:227
  61.5 7.5 %collective-permute-start.5 = (bf16[2,528,128]{2,1,0:T(8,128)(2,1)S(1)}, bf16[2,528,128]{2,1,0:T(8,128)(2,1)S(1)}, u32[]{:S(2)}, u32[]{:S(2)}) collective-permute-start(bf16[2,528,128]{2,1,0:T(8,128)(2,1)S(1)} %collective-permute-done.4.refs_7_), channel_id=1, source_target_pairs={{0,32},{32,64},{64,96},{96,128},{128,160},{160,192},{192,224},{224... | collective-permute-start | bytes 811016 | tf_op jit(solution)/shard_map/ppermute | solution.py:227
  69.0 6.5 %collective-permute-start.9 = (bf16[2,528,128]{2,1,0:T(8,128)(2,1)S(1)}, bf16[2,528,128]{2,1,0:T(8,128)(2,1)S(1)}, u32[]{:S(2)}, u32[]{:S(2)}) collective-permute-start(bf16[2,528,128]{2,1,0:T(8,128)(2,1)S(1)} %collective-permute-done.5.refs_6_), channel_id=1, source_target_pairs={{0,32},{32,64},{64,96},{96,128},{128,160},{160,192},{192,224},{224... | collective-permute-start | bytes 811016 | tf_op jit(solution)/shard_map/ppermute | solution.py:227
  69.0 8.9 %collective-permute-start.8 = (bf16[2,528,128]{2,1,0:T(8,128)(2,1)S(1)}, bf16[2,528,128]{2,1,0:T(8,128)(2,1)S(1)}, u32[]{:S(2)}, u32[]{:S(2)}) collective-permute-start(bf16[2,528,128]{2,1,0:T(8,128)(2,1)S(1)} %collective-permute-done.7.refs_2_), channel_id=1, source_target_pairs={{0,224},{32,0},{64,32},{96,64},{128,96},{160,128},{192,160},{224,1... | collective-permute-start | bytes 811016 | tf_op jit(solution)/shard_map/ppermute | solution.py:227
  75.5 6.5 %collective-permute-start.10 = (bf16[2,528,128]{2,1,0:T(8,128)(2,1)S(1)}, bf16[2,528,128]{2,1,0:T(8,128)(2,1)S(1)}, u32[]{:S(2)}, u32[]{:S(2)}) collective-permute-start(bf16[2,528,128]{2,1,0:T(8,128)(2,1)S(1)} %collective-permute-done.9.refs_5_), channel_id=1, source_target_pairs={{0,32},{32,64},{64,96},{96,128},{128,160},{160,192},{192,224},{224... | collective-permute-start | bytes 811016 | tf_op jit(solution)/shard_map/ppermute | solution.py:227
  75.6 6.4 %copy-start = (bf16[8448,128]{1,0:T(8,128)(2,1)S(1)}, bf16[8448,128]{1,0:T(8,128)(2,1)}, u32[]{:S(2)}) copy-start(bf16[8448,128]{1,0:T(8,128)(2,1)} %all-gather.3.cloned.1.call-done) | copy-start | bytes 6488068
  75.6 6.4 %copy-start.2 = (bf16[256,2048]{1,0:T(8,128)(2,1)S(1)}, bf16[256,2048]{1,0:T(8,128)(2,1)}, u32[]{:S(2)}) copy-start(bf16[256,2048]{1,0:T(8,128)(2,1)} %refs_9_.1) | copy-start | bytes 3145732
  75.6 6.4 %copy-start.3 = (bf16[128,2048]{1,0:T(8,128)(2,1)S(1)}, bf16[128,2048]{1,0:T(8,128)(2,1)}, u32[]{:S(2)}) copy-start(bf16[128,2048]{1,0:T(8,128)(2,1)} %refs_10_.1) | copy-start | bytes 1572868
  89.9 3.2 %collective-permute-start.11 = (bf16[256,128]{1,0:T(8,128)(2,1)S(1)}, bf16[256,128]{1,0:T(8,128)(2,1)S(1)}, u32[]{:S(2)}, u32[]{:S(2)}) collective-permute-start(bf16[256,128]{1,0:T(8,128)(2,1)S(1)} %convert_element_type.145), channel_id=1, source_target_pairs={{0,32},{32,0},{64,96},{96,64},{128,160},{160,128},{192,224},{224,1... | collective-permute-start | bytes 196616 | tf_op jit(solution)/shard_map/ppermute | solution.py:232
  93.1 6.6 %collective-permute-start.12 = (bf16[256,128]{1,0:T(8,128)(2,1)S(1)}, bf16[256,128]{1,0:T(8,128)(2,1)S(1)}, u32[]{:S(2)}, u32[]{:S(2)}) collective-permute-start(bf16[256,128]{1,0:T(8,128)(2,1)S(1)} %fusion.5), channel_id=1, source_target_pairs={{0,64},{32,96},{64,0},{96,32},{128,192},{160,224},{192,128},{224,1... | collective-permute-start | bytes 196616 | tf_op jit(solution)/shard_map/ppermute | solution.py:232
  93.4 14.9 %collective-permute-start.13 = (bf16[2,512,128]{2,1,0:T(8,128)(2,1)S(1)}, bf16[2,512,128]{2,1,0:T(8,128)(2,1)S(1)}, u32[]{:S(2)}, u32[]{:S(2)}) collective-permute-start(bf16[2,512,128]{2,1,0:T(8,128)(2,1)S(1)} %get-tuple-element.80), channel_id=1, source_target_pairs={{0,32},{32,64},{64,96},{96,128},{128,160},{160,192},{192,224},{224... | collective-permute-start | bytes 786440 | tf_op jit(solution)/shard_map/ppermute | solution.py:227
  94.3 14.0 %collective-permute-start.14 = (bf16[2,512,128]{2,1,0:T(8,128)(2,1)S(1)}, bf16[2,512,128]{2,1,0:T(8,128)(2,1)S(1)}, u32[]{:S(2)}, u32[]{:S(2)}) collective-permute-start(bf16[2,512,128]{2,1,0:T(8,128)(2,1)S(1)} %get-tuple-element.81), channel_id=1, source_target_pairs={{0,224},{32,0},{64,32},{96,64},{128,96},{160,128},{192,160},{224,1... | collective-permute-start | bytes 786440 | tf_op jit(solution)/shard_map/ppermute | solution.py:227
  99.8 8.5 %collective-permute-start.15 = (bf16[256,128]{1,0:T(8,128)(2,1)S(1)}, bf16[256,128]{1,0:T(8,128)(2,1)S(1)}, u32[]{:S(2)}, u32[]{:S(2)}) collective-permute-start(bf16[256,128]{1,0:T(8,128)(2,1)S(1)} %fusion.8), channel_id=1, source_target_pairs={{0,128},{32,160},{64,192},{96,224},{128,0},{160,32},{192,64},{224,... | collective-permute-start | bytes 196616 | tf_op jit(solution)/shard_map/ppermute | solution.py:232
  108.3 10.9 %collective-permute-start.19 = (bf16[8,768,128]{2,1,0:T(8,128)(2,1)S(1)}, bf16[8,768,128]{2,1,0:T(8,128)(2,1)S(1)}, u32[]{:S(2)}, u32[]{:S(2)}) collective-permute-start(bf16[8,768,128]{2,1,0:T(8,128)(2,1)S(1)} %shard_map.105), channel_id=1, source_target_pairs={{0,1},{1,0},{2,3},{3,2},{4,5},{5,4},{6,7},{7,6},{8,9},{9,8},{10,11... | collective-permute-start | bytes 4718600 | tf_op jit(solution)/shard_map/ppermute | solution.py:232
  116.2 8.1 %collective-permute-start.17 = (bf16[2,512,128]{2,1,0:T(8,128)(2,1)S(1)}, bf16[2,512,128]{2,1,0:T(8,128)(2,1)S(1)}, u32[]{:S(2)}, u32[]{:S(2)}) collective-permute-start(bf16[2,512,128]{2,1,0:T(8,128)(2,1)S(1)} %add_convert_fusion.3), channel_id=1, source_target_pairs={{0,224},{32,0},{64,32},{96,64},{128,96},{160,128},{192,160},{224,1... | collective-permute-start | bytes 786440 | tf_op jit(solution)/shard_map/ppermute | solution.py:227
  116.3 9.2 %collective-permute-start.16 = (bf16[2,512,128]{2,1,0:T(8,128)(2,1)S(1)}, bf16[2,512,128]{2,1,0:T(8,128)(2,1)S(1)}, u32[]{:S(2)}, u32[]{:S(2)}) collective-permute-start(bf16[2,512,128]{2,1,0:T(8,128)(2,1)S(1)} %add_convert_fusion.4), channel_id=1, source_target_pairs={{0,32},{32,64},{64,96},{96,128},{128,160},{160,192},{192,224},{224... | collective-permute-start | bytes 786440 | tf_op jit(solution)/shard_map/ppermute | solution.py:227
  117.9 6.3 %collective-permute-start.18 = (bf16[256,128]{1,0:T(8,128)(2,1)S(1)}, bf16[256,128]{1,0:T(8,128)(2,1)S(1)}, u32[]{:S(2)}, u32[]{:S(2)}) collective-permute-start(bf16[256,128]{1,0:T(8,128)(2,1)S(1)} %fusion.6), channel_id=1, source_target_pairs={{0,16},{16,0},{1,17},{17,1},{2,18},{18,2},{3,19},{19,3},{4,20},{20... | collective-permute-start | bytes 196616 | tf_op jit(solution)/shard_map/ppermute | solution.py:232
  125.6 0.7 copy-start.5
  129.1 29.3 %all-to-all-start.1 = ((bf16[8,896,128]{2,1,0:T(8,128)(2,1)}), bf16[8,896,128]{2,1,0:T(8,128)(2,1)S(1)}, u32[]{:S(2)}, u32[]{:S(2)}) async-start(bf16[8,896,128]{2,1,0:T(8,128)(2,1)} %shard_map.107), calls=%async_computation.1 | async-start | bytes 3670016 | tf_op jit(solution)/shard_map/all_to_all | solution.py:344
  135.1 7.2 %collective-permute-start.21 = (bf16[2,512,128]{2,1,0:T(8,128)(2,1)S(1)}, bf16[2,512,128]{2,1,0:T(8,128)(2,1)S(1)}, u32[]{:S(2)}, u32[]{:S(2)}) collective-permute-start(bf16[2,512,128]{2,1,0:T(8,128)(2,1)S(1)} %add_convert_fusion.1), channel_id=1, source_target_pairs={{0,224},{32,0},{64,32},{96,64},{128,96},{160,128},{192,160},{224,1... | collective-permute-start | bytes 786440 | tf_op jit(solution)/shard_map/ppermute | solution.py:227
  138.9 7.7 %collective-permute-start.20 = (bf16[2,512,128]{2,1,0:T(8,128)(2,1)S(1)}, bf16[2,512,128]{2,1,0:T(8,128)(2,1)S(1)}, u32[]{:S(2)}, u32[]{:S(2)}) collective-permute-start(bf16[2,512,128]{2,1,0:T(8,128)(2,1)S(1)} %add_convert_fusion.2), channel_id=1, source_target_pairs={{0,32},{32,64},{64,96},{96,128},{128,160},{160,192},{192,224},{224... | collective-permute-start | bytes 786440 | tf_op jit(solution)/shard_map/ppermute | solution.py:227
  146.6 6.8 %collective-permute-start.22 = (bf16[2,512,128]{2,1,0:T(8,128)(2,1)S(1)}, bf16[2,512,128]{2,1,0:T(8,128)(2,1)S(1)}, u32[]{:S(2)}, u32[]{:S(2)}) collective-permute-start(bf16[2,512,128]{2,1,0:T(8,128)(2,1)S(1)} %add_convert_fusion), channel_id=1, source_target_pairs={{0,32},{32,64},{64,96},{96,128},{128,160},{160,192},{192,224},{224... | collective-permute-start | bytes 786440 | tf_op jit(solution)/shard_map/ppermute | solution.py:227
  146.7 29.6 %collective-permute-start.25 = (bf16[256,128]{1,0:T(8,128)(2,1)S(1)}, bf16[256,128]{1,0:T(8,128)(2,1)S(1)}, u32[]{:S(2)}, u32[]{:S(2)}) collective-permute-start(bf16[256,128]{1,0:T(8,128)(2,1)S(1)} %add_convert_fusion.6), channel_id=1, source_target_pairs={{0,0},{1,16},{2,32},{3,48},{4,64},{5,80},{6,96},{7,112},{8,128},{9... | collective-permute-start | bytes 196616 | tf_op jit(solution)/shard_map/ppermute | solution.py:345
  153.4 2.5 %copy-start.6 = (bf16[2,512,128]{2,1,0:T(8,128)(2,1)}, bf16[2,512,128]{2,1,0:T(8,128)(2,1)S(1)}, u32[]{:S(2)}) copy-start(bf16[2,512,128]{2,1,0:T(8,128)(2,1)S(1)} %collective-permute-done.22) | copy-start | bytes 786436
  154.2 12.1 %collective-permute-start.23 = (bf16[512,128]{1,0:T(8,128)(2,1)}, bf16[512,128]{1,0:T(8,128)(2,1)}, u32[]{:S(2)}, u32[]{:S(2)}) collective-permute-start(bf16[512,128]{1,0:T(8,128)(2,1)} %fusion.4), channel_id=1, source_target_pairs={{0,16},{16,0},{1,17},{17,1},{2,18},{18,2},{3,19},{19,3},{4,20},{20... | collective-permute-start | bytes 393224 | tf_op jit(solution)/shard_map/ppermute | solution.py:232
  158.4 7.9 %copy-start.7 = (bf16[2,512,128]{2,1,0:T(8,128)(2,1)S(1)}, bf16[2,512,128]{2,1,0:T(8,128)(2,1)}, u32[]{:S(2)}) copy-start(bf16[2,512,128]{2,1,0:T(8,128)(2,1)} %copy-done.6) | copy-start | bytes 786436
  158.7 17.0 %collective-permute-start.26 = (f32[64,128]{1,0:T(8,128)S(1)}, f32[64,128]{1,0:T(8,128)S(1)}, u32[]{:S(2)}, u32[]{:S(2)}) collective-permute-start(f32[64,128]{1,0:T(8,128)S(1)} %slice.67), channel_id=1, source_target_pairs={{0,1},{1,0},{2,3},{3,2},{4,5},{5,4},{6,7},{7,6},{8,9},{9,8},{10,11... | collective-permute-start | bytes 98312 | tf_op jit(solution)/shard_map/ppermute | solution.py:232
  167.3 17.7 %collective-permute-start.24 = (bf16[512,128]{1,0:T(8,128)(2,1)S(1)}, bf16[512,128]{1,0:T(8,128)(2,1)S(1)}, u32[]{:S(2)}, u32[]{:S(2)}) collective-permute-start(bf16[512,128]{1,0:T(8,128)(2,1)S(1)} %fusion.2), channel_id=1, source_target_pairs={{0,0},{1,16},{2,32},{3,48},{4,64},{5,80},{6,96},{7,112},{8,128},{9... | collective-permute-start | bytes 393224 | tf_op jit(solution)/shard_map/ppermute | solution.py:343
Sparse Core Ops, SparseCore 0:
  10.6 45.3 all-gather.2

commit v7 on v6

--- a/solution.py
+++ b/solution.py
@@ -330,7 +330,7 @@
         6 << 20,
         (place, index, x_all, dz_t, grads_in),
     )
-    up, down, q_in, grads = lax.optimization_barrier((up, down, q_in, grads))
+    up, down, grads = lax.optimization_barrier((up, down, grads))
 
     up, down = shift(add(back[2], up), 1), shift(add(back[7], down), -1)
     q_t = (q + q_in.astype(F32)).astype(BF16)

time: 193 us -> 193 us (level)
    ppermute x14, waiting for transfers between devices: 30.3 us -> 27.3 us  [shift(): return lax.ppermute(x, 'z', [(i, (i + by) % NZ) for i in range(NZ)])]
    all_to_all x1, starting transfers between devices: 5.97 us -> 8.29 us  [on_device(): grads_in = lax.all_to_all(grads, ('xl', 'y'), 0, 0)]
  transfers between devices with their start and end apart: 29 -> 29, of which waited for: 15 -> 14; matrix products, arithmetic and copies ran while one was open for 4% -> 4% of each run, Pallas kernels for 8% -> 8%
where the time goes in v7:
time: 193 us; the launch traced here: 192 us
  starting transfers between devices  76.4 us (40%)
  waiting for transfers between devices  47.2 us (24%)
  Pallas kernels  25.8 us (13%)
  blocking collectives  16.1 us (8%)
  between operations  14.4 us (7%)
  local copies, waits for them, and re-layouts  8.38 us (4%)
  other arithmetic  3.65 us (2%)
    ppermute x14, waiting for transfers between devices, shift(): return lax.ppermute(x, 'z', [(i, (i + by) % NZ) for i in range(NZ)])  27.3 us
    pallas_call x6, Pallas kernels, call(): pl.pallas_call(kernel, out_shape=out_shape, in_specs=[smem] * scalars + [...  23 us
    ppermute x14, starting transfers between devices, shift(): return lax.ppermute(x, 'z', [(i, (i + by) % NZ) for i in range(NZ)])  21.7 us
    ppermute x8, starting transfers between devices, meet(): return lax.ppermute(x, axis, [(i, i ^ flip) for i in range(count)])  21.4 us
    all_to_all x1, blocking collectives, on_device(): p_in = lax.all_to_all(p, COL, 0, 0)  16.1 us
    ppermute x1, waiting for transfers between devices, on_device(): x_grad_t = lax.ppermute(total, ALL, turn)  8.46 us
    all_to_all x1, starting transfers between devices, on_device(): grads_in = lax.all_to_all(grads, ('xl', 'y'), 0, 0)  8.29 us
    ppermute x1, starting transfers between devices, on_device(): x_grad_t = lax.ppermute(total, ALL, turn)  7.25 us
  transfers between devices with their start and end apart: 29, of which 14 were waited for; matrix products, arithmetic and copies ran while one was open for 4% of the time, Pallas kernels for 8%

profile of v7, /device:TPU:1, one launch (start us, length us, event | category | flops | bytes accessed | tf_op | source)
XLA Modules:
  0.0 192.2 jit_solution(9949356621532877640)
XLA Ops:
  7.2 0.7 convert_bitcast_fusion
  8.0 1.2 reshape.90
  9.7 0.8 copy.36
  10.8 6.0 %collective-permute-start = (bf16[512,128]{1,0:T(8,128)(2,1)S(1)}, bf16[512,128]{1,0:T(8,128)(2,1)S(1)}, u32[]{:S(2)}, u32[]{:S(2)}) collective-permute-start(bf16[512,128]{1,0:T(8,128)(2,1)S(1)} %get-tuple-element.61), channel_id=1, source_target_pairs={{0,0},{1,16},{2,32},{3,48},{4,64},{5,80},{6,96},{7,112},{8,128},{9... | collective-permute-start | bytes 393224 | tf_op jit(solution)/shard_map/ppermute | solution.py:256
  16.9 16.1 %all_to_all.10 = f32[16,16,128]{2,1,0:T(8,128)S(1)} all-to-all(f32[16,16,128]{2,1,0:T(8,128)S(1)} %get-tuple-element.62), channel_id=1, replica_groups=mesh['z'=8,'xh'=2,'xl'=2,'y'=4,'core'=2] {'xl','y','core'}, dimensions={0} | all-to-all | bytes 262144 | tf_op jit(solution)/shard_map/all_to_all | solution.py:257
  33.0 0.8 collective-permute-start.2
  33.8 5.3 %collective-permute-start.1 = (bf16[16,128]{1,0:T(8,128)(2,1)S(1)}, bf16[16,128]{1,0:T(8,128)(2,1)S(1)}, u32[]{:S(2)}, u32[]{:S(2)}) collective-permute-start(bf16[16,128]{1,0:T(8,128)(2,1)S(1)} %reduce_sum.18), channel_id=1, source_target_pairs={{0,0},{1,16},{2,32},{3,48},{4,64},{5,80},{6,96},{7,112},{8,128},{9... | collective-permute-start | bytes 12296 | tf_op jit(solution)/shard_map/ppermute | solution.py:262
  39.2 2.4 %collective-permute-done.1 = bf16[16,128]{1,0:T(8,128)(2,1)S(1)} collective-permute-done((bf16[16,128]{1,0:T(8,128)(2,1)S(1)}, bf16[16,128]{1,0:T(8,128)(2,1)S(1)}, u32[]{:S(2)}, u32[]{:S(2)}) %collective-permute-start.1) | collective-permute-done | bytes 4128 | tf_op jit(solution)/shard_map/ppermute | solution.py:262
  41.6 1.5 collective-permute-done.3
  43.2 9.5 %collective-permute-start.6 = (bf16[2,528,128]{2,1,0:T(8,128)(2,1)S(1)}, bf16[2,528,128]{2,1,0:T(8,128)(2,1)S(1)}, u32[]{:S(2)}, u32[]{:S(2)}) collective-permute-start(bf16[2,528,128]{2,1,0:T(8,128)(2,1)S(1)} %bitcast.56), channel_id=1, source_target_pairs={{0,224},{32,0},{64,32},{96,64},{128,96},{160,128},{192,160},{224,1... | collective-permute-start | bytes 811016 | tf_op jit(solution)/shard_map/ppermute | solution.py:227
  52.8 5.3 %collective-permute-done.6.refs_1_ = bf16[2,528,128]{2,1,0:T(8,128)(2,1)S(1)} collective-permute-done((bf16[2,528,128]{2,1,0:T(8,128)(2,1)S(1)}, bf16[2,528,128]{2,1,0:T(8,128)(2,1)S(1)}, u32[]{:S(2)}, u32[]{:S(2)}) %collective-permute-start.6) | collective-permute-done | bytes 270368 | tf_op jit(solution)/shard_map/ppermute | solution.py:227
  58.1 3.4 %collective-permute-start.7 = (bf16[2,528,128]{2,1,0:T(8,128)(2,1)S(1)}, bf16[2,528,128]{2,1,0:T(8,128)(2,1)S(1)}, u32[]{:S(2)}, u32[]{:S(2)}) collective-permute-start(bf16[2,528,128]{2,1,0:T(8,128)(2,1)S(1)} %collective-permute-done.6.refs_1_), channel_id=1, source_target_pairs={{0,224},{32,0},{64,32},{96,64},{128,96},{160,128},{192,160},{224,1... | collective-permute-start | bytes 811016 | tf_op jit(solution)/shard_map/ppermute | solution.py:227
  61.5 4.4 %collective-permute-done.7.refs_2_ = bf16[2,528,128]{2,1,0:T(8,128)(2,1)S(1)} collective-permute-done((bf16[2,528,128]{2,1,0:T(8,128)(2,1)S(1)}, bf16[2,528,128]{2,1,0:T(8,128)(2,1)S(1)}, u32[]{:S(2)}, u32[]{:S(2)}) %collective-permute-start.7) | collective-permute-done | bytes 270368 | tf_op jit(solution)/shard_map/ppermute | solution.py:227
  65.9 3.1 %collective-permute-done.5.refs_6_ = bf16[2,528,128]{2,1,0:T(8,128)(2,1)S(1)} collective-permute-done((bf16[2,528,128]{2,1,0:T(8,128)(2,1)S(1)}, bf16[2,528,128]{2,1,0:T(8,128)(2,1)S(1)}, u32[]{:S(2)}, u32[]{:S(2)}) %collective-permute-start.5) | collective-permute-done | bytes 270368 | tf_op jit(solution)/shard_map/ppermute | solution.py:227
  69.0 2.7 %collective-permute-start.8 = (bf16[2,528,128]{2,1,0:T(8,128)(2,1)S(1)}, bf16[2,528,128]{2,1,0:T(8,128)(2,1)S(1)}, u32[]{:S(2)}, u32[]{:S(2)}) collective-permute-start(bf16[2,528,128]{2,1,0:T(8,128)(2,1)S(1)} %collective-permute-done.7.refs_2_), channel_id=1, source_target_pairs={{0,224},{32,0},{64,32},{96,64},{128,96},{160,128},{192,160},{224,1... | collective-permute-start | bytes 811016 | tf_op jit(solution)/shard_map/ppermute | solution.py:227
  71.7 3.8 %collective-permute-done.9.refs_5_ = bf16[2,528,128]{2,1,0:T(8,128)(2,1)S(1)} collective-permute-done((bf16[2,528,128]{2,1,0:T(8,128)(2,1)S(1)}, bf16[2,528,128]{2,1,0:T(8,128)(2,1)S(1)}, u32[]{:S(2)}, u32[]{:S(2)}) %collective-permute-start.9) | collective-permute-done | bytes 270368 | tf_op jit(solution)/shard_map/ppermute | solution.py:227
  75.6 2.3 %copy.37 = bf16[16,528,128]{2,0,1:T(8,128)(2,1)S(1)} copy(bf16[16,528,128]{2,1,0:T(8,128)(2,1)} %bitcast.52) | data formatting | bytes 4325376 | tf_op jit(solution)/shard_map/optimization_barrier | solution.py:270
  78.0 4.1 %collective-permute-done.10.refs_4_ = bf16[2,528,128]{2,1,0:T(8,128)(2,1)S(1)} collective-permute-done((bf16[2,528,128]{2,1,0:T(8,128)(2,1)S(1)}, bf16[2,528,128]{2,1,0:T(8,128)(2,1)S(1)}, u32[]{:S(2)}, u32[]{:S(2)}) %collective-permute-start.10) | collective-permute-done | bytes 270368 | tf_op jit(solution)/shard_map/ppermute | solution.py:227
  82.1 7.8 %shard_map.102 = (bf16[128,2048]{1,0:T(8,128)(2,1)}, bf16[2048,128]{1,0:T(8,128)(2,1)S(1)}, f32[256,128]{1,0:T(8,128)S(1)}, bf16[16,528,128]{2,1,0:T(8,128)(2,1)S(1)}) custom-call(s32[4]{0:T(128)S(1)} %pad_add_fusion.place, s32[16,16]{1,0:T(8,128)S(1)} %fusion.7.index, bf16[2,528,128]{2,1,0:T(8,128)(2,1)S(1)} %bitcast.58, ...), custom_call_target="tpu_custom_call" | custom-call | flops 800000000 | bytes 10485760 | tf_op jit(solution)/shard_map/pallas_call | solution.py:205
  90.0 2.4 %shard_map.103 = (bf16[2,512,128]{2,1,0:T(8,128)(2,1)S(1)}, bf16[2,512,128]{2,1,0:T(8,128)(2,1)S(1)}, bf16[2,512,128]{2,1,0:T(8,128)(2,1)S(1)}) custom-call(s32[4]{0:T(128)S(1)} %pad_add_fusion.place, s32[16,16]{1,0:T(8,128)S(1)} %fusion.7.index, bf16[16,528,128]{2,1,0:T(8,128)(2,1)S(1)} %bitcast.54, bf16[2048,128]{1,0:T(8,128)(2,1)S(1)} %get-tuple-element.83.dz_t), custom_call_target="tpu_custom_call" | custom-call | flops 120000000 | bytes 3145728 | tf_op jit(solution)/shard_map/pallas_call | solution.py:205
  92.4 0.7 collective-permute-done.11
  93.4 0.9 collective-permute-start.13
  94.3 1.9 collective-permute-start.14
  96.2 3.6 %shard_map.104 = (bf16[2,512,128]{2,1,0:T(8,128)(2,1)S(1)}, bf16[2,512,128]{2,1,0:T(8,128)(2,1)S(1)}, bf16[2,512,128]{2,1,0:T(8,128)(2,1)S(1)}, bf16[2,512,128]{2,1,0:T(8,128)(2,1)S(1)}, bf16[2,512,128]{2,1,0:T(8,128)(2,1)S(1)}) custom-call(s32[4]{0:T(128)S(1)} %pad_add_fusion.place, s32[16,16]{1,0:T(8,128)S(1)} %fusion.7.index, ...), custom_call_target="tpu_custom_call" | custom-call | flops 200000000 | bytes 5242880 | tf_op jit(solution)/shard_map/pallas_call | solution.py:205
  99.8 4.7 %collective-permute-start.15 = (bf16[256,128]{1,0:T(8,128)(2,1)S(1)}, bf16[256,128]{1,0:T(8,128)(2,1)S(1)}, u32[]{:S(2)}, u32[]{:S(2)}) collective-permute-start(bf16[256,128]{1,0:T(8,128)(2,1)S(1)} %fusion.8), channel_id=1, source_target_pairs={{0,128},{32,160},{64,192},{96,224},{128,0},{160,32},{192,64},{224,... | collective-permute-start | bytes 196616 | tf_op jit(solution)/shard_map/ppermute | solution.py:232
  104.5 3.8 %shard_map.105 = bf16[8,768,128]{2,1,0:T(8,128)(2,1)S(1)} custom-call(s32[4]{0:T(128)S(1)} %pad_add_fusion.place, s32[16,16]{1,0:T(8,128)S(1)} %fusion.7.index, bf16[16,528,128]{2,1,0:T(8,128)(2,1)S(1)} %get-tuple-element.82.x, bf16[2048,128]{1,0:T(8,128)(2,1)S(1)} %get-tuple-element.83.dz_t), custom_call_target="tpu_custom_call" | custom-call | flops 200000000 | bytes 4194304 | tf_op jit(solution)/shard_map/pallas_call | solution.py:205
  108.3 7.8 %collective-permute-start.18 = (bf16[8,768,128]{2,1,0:T(8,128)(2,1)S(1)}, bf16[8,768,128]{2,1,0:T(8,128)(2,1)S(1)}, u32[]{:S(2)}, u32[]{:S(2)}) collective-permute-start(bf16[8,768,128]{2,1,0:T(8,128)(2,1)S(1)} %shard_map.105), channel_id=1, source_target_pairs={{0,1},{1,0},{2,3},{3,2},{4,5},{5,4},{6,7},{7,6},{8,9},{9,8},{10,11... | collective-permute-start | bytes 4718600 | tf_op jit(solution)/shard_map/ppermute | solution.py:232
  116.2 1.1 collective-permute-start.21
  117.5 1.5 collective-permute-start.16
  119.0 2.4 %collective-permute-done.21 = bf16[256,128]{1,0:T(8,128)(2,1)S(1)} collective-permute-done((bf16[256,128]{1,0:T(8,128)(2,1)S(1)}, bf16[256,128]{1,0:T(8,128)(2,1)S(1)}, u32[]{:S(2)}, u32[]{:S(2)}) %collective-permute-start.21) | collective-permute-done | bytes 65568 | tf_op jit(solution)/shard_map/ppermute | solution.py:232
  121.5 5.1 %shard_map.106.grads = bf16[8,896,128]{2,1,0:T(8,128)(2,1)} custom-call(s32[4]{0:T(128)S(1)} %pad_add_fusion.place, s32[16,16]{1,0:T(8,128)S(1)} %fusion.7.index, bf16[16,528,128]{2,1,0:T(8,128)(2,1)S(1)} %get-tuple-element.82.x, bf16[2048,128]{1,0:T(8,128)(2,1)S(1)} %get-tuple-element.83.dz_t, bf16[8,768,128]{2,1,0:T(8,128)(2,1)S(1)} %collective-permute-done.18.other), custom_call_target="tpu_custom_call" | custom-call | flops 200000000 | bytes 6291456 | tf_op jit(solution)/shard_map/pallas_call | solution.py:205
  126.6 2.8 %shard_map.107 = bf16[8,896,128]{2,1,0:T(8,128)(2,1)} custom-call(s32[4]{0:T(128)S(1)} %pad_add_fusion.place, bf16[8,896,128]{2,1,0:T(8,128)(2,1)} %shard_map.106.grads, bf16[16,528,128]{2,1,0:T(8,128)(2,1)S(1)} %get-tuple-element.82.x, bf16[16,16,128]{2,1,0:T(8,128)(2,1)S(1)} %bitcast.59), custom_call_target="tpu_custom_call", output_to_operand_aliasing={{}: (1, {})} | custom-call | flops 70000000 | bytes 3145728 | tf_op jit(solution)/shard_map/pallas_call | solution.py:186
  129.4 8.3 %all-to-all-start.1 = ((bf16[8,896,128]{2,1,0:T(8,128)(2,1)}), bf16[8,896,128]{2,1,0:T(8,128)(2,1)S(1)}, u32[]{:S(2)}, u32[]{:S(2)}) async-start(bf16[8,896,128]{2,1,0:T(8,128)(2,1)} %shard_map.107), calls=%async_computation.1 | async-start | bytes 3670016 | tf_op jit(solution)/shard_map/all_to_all | solution.py:344
  137.7 1.0 add_convert_fusion.1
  139.0 1.0 add_convert_fusion.2
  140.0 1.4 collective-permute-start.19
  141.4 3.5 %collective-permute-done.20 = bf16[2,512,128]{2,1,0:T(8,128)(2,1)S(1)} collective-permute-done((bf16[2,512,128]{2,1,0:T(8,128)(2,1)S(1)}, bf16[2,512,128]{2,1,0:T(8,128)(2,1)S(1)}, u32[]{:S(2)}, u32[]{:S(2)}) %collective-permute-start.20) | collective-permute-done | bytes 262176 | tf_op jit(solution)/shard_map/ppermute | solution.py:227
  144.9 2.5 %collective-permute-done.19 = bf16[2,512,128]{2,1,0:T(8,128)(2,1)S(1)} collective-permute-done((bf16[2,512,128]{2,1,0:T(8,128)(2,1)S(1)}, bf16[2,512,128]{2,1,0:T(8,128)(2,1)S(1)}, u32[]{:S(2)}, u32[]{:S(2)}) %collective-permute-start.19) | collective-permute-done | bytes 262176 | tf_op jit(solution)/shard_map/ppermute | solution.py:227
  147.6 6.3 %collective-permute-start.25 = (bf16[256,128]{1,0:T(8,128)(2,1)S(1)}, bf16[256,128]{1,0:T(8,128)(2,1)S(1)}, u32[]{:S(2)}, u32[]{:S(2)}) collective-permute-start(bf16[256,128]{1,0:T(8,128)(2,1)S(1)} %add_convert_fusion.6), channel_id=1, source_target_pairs={{0,0},{1,16},{2,32},{3,48},{4,64},{5,80},{6,96},{7,112},{8,128},{9... | collective-permute-start | bytes 196616 | tf_op jit(solution)/shard_map/ppermute | solution.py:345
  154.4 2.3 %collective-permute-start.23 = (bf16[512,128]{1,0:T(8,128)(2,1)S(1)}, bf16[512,128]{1,0:T(8,128)(2,1)S(1)}, u32[]{:S(2)}, u32[]{:S(2)}) collective-permute-start(bf16[512,128]{1,0:T(8,128)(2,1)S(1)} %fusion.4), channel_id=1, source_target_pairs={{0,16},{16,0},{1,17},{17,1},{2,18},{18,2},{3,19},{19,3},{4,20},{20... | collective-permute-start | bytes 393224 | tf_op jit(solution)/shard_map/ppermute | solution.py:232
  156.7 4.4 %all-to-all-done.1 = bf16[8,896,128]{2,1,0:T(8,128)(2,1)S(1)} async-done(((bf16[8,896,128]{2,1,0:T(8,128)(2,1)}), bf16[8,896,128]{2,1,0:T(8,128)(2,1)S(1)}, u32[]{:S(2)}, u32[]{:S(2)}) %all-to-all-start.1) | async-done | bytes 1835040 | tf_op jit(solution)/shard_map/all_to_all | solution.py:344
  161.3 4.4 %collective-permute-start.26 = (f32[64,128]{1,0:T(8,128)S(1)}, f32[64,128]{1,0:T(8,128)S(1)}, u32[]{:S(2)}, u32[]{:S(2)}) collective-permute-start(f32[64,128]{1,0:T(8,128)S(1)} %slice.67), channel_id=1, source_target_pairs={{0,1},{1,0},{2,3},{3,2},{4,5},{5,4},{6,7},{7,6},{8,9},{9,8},{10,11... | collective-permute-start | bytes 98312 | tf_op jit(solution)/shard_map/ppermute | solution.py:232
  165.8 7.3 %collective-permute-start.24 = (bf16[512,128]{1,0:T(8,128)(2,1)S(1)}, bf16[512,128]{1,0:T(8,128)(2,1)S(1)}, u32[]{:S(2)}, u32[]{:S(2)}) collective-permute-start(bf16[512,128]{1,0:T(8,128)(2,1)S(1)} %fusion.2), channel_id=1, source_target_pairs={{0,0},{1,16},{2,32},{3,48},{4,64},{5,80},{6,96},{7,112},{8,128},{9... | collective-permute-start | bytes 393224 | tf_op jit(solution)/shard_map/ppermute | solution.py:343
  173.2 0.7 copy.49
  174.3 0.9 reshape.95
  175.3 0.6 copy.50
  175.9 8.5 %collective-permute-done.24 = bf16[512,128]{1,0:T(8,128)(2,1)S(1)} collective-permute-done((bf16[512,128]{1,0:T(8,128)(2,1)S(1)}, bf16[512,128]{1,0:T(8,128)(2,1)S(1)}, u32[]{:S(2)}, u32[]{:S(2)}) %collective-permute-start.24) | collective-permute-done | bytes 131104 | tf_op jit(solution)/shard_map/ppermute | solution.py:343
  184.6 0.8 copy.43
  (74 shorter events, 4.0 us)
Async XLA Ops:
  7.2 3.3 %copy-start.4 = (bf16[128,512]{1,0:T(8,128)(2,1)S(1)}, bf16[128,512]{1,0:T(8,128)(2,1)}, u32[]{:S(2)}) copy-start(bf16[128,512]{1,0:T(8,128)(2,1)} %x.2) | copy-start | bytes 393220
  7.2 3.3 %copy-start.1 = (bf16[512,256]{1,0:T(8,128)(2,1)S(1)}, bf16[512,256]{1,0:T(8,128)(2,1)}, u32[]{:S(2)}) copy-start(bf16[512,256]{1,0:T(8,128)(2,1)} %u.1) | copy-start | bytes 786436
  7.2 61.8 %all-gather.3.cloned.1.call-start = ((), (), s32[]{:S(2)}) async-start(), calls=%async_computation.2 | async-start | bytes 2297856 | tf_op jit(solution)/shard_map/all_gather | solution.py:246
  10.8 22.2 %collective-permute-start = (bf16[512,128]{1,0:T(8,128)(2,1)S(1)}, bf16[512,128]{1,0:T(8,128)(2,1)S(1)}, u32[]{:S(2)}, u32[]{:S(2)}) collective-permute-start(bf16[512,128]{1,0:T(8,128)(2,1)S(1)} %get-tuple-element.61), channel_id=1, source_target_pairs={{0,0},{1,16},{2,32},{3,48},{4,64},{5,80},{6,96},{7,112},{8,128},{9... | collective-permute-start | bytes 393224 | tf_op jit(solution)/shard_map/ppermute | solution.py:256
  33.0 10.2 %collective-permute-start.2 = (bf16[512,128]{1,0:T(8,128)(2,1)S(1)}, bf16[512,128]{1,0:T(8,128)(2,1)S(1)}, u32[]{:S(2)}, u32[]{:S(2)}) collective-permute-start(bf16[512,128]{1,0:T(8,128)(2,1)S(1)} %collective-permute-done), channel_id=1, source_target_pairs={{0,16},{16,0},{1,17},{17,1},{2,18},{18,2},{3,19},{19,3},{4,20},{20... | collective-permute-start | bytes 393224 | tf_op jit(solution)/shard_map/ppermute | solution.py:232
  33.8 7.8 %collective-permute-start.1 = (bf16[16,128]{1,0:T(8,128)(2,1)S(1)}, bf16[16,128]{1,0:T(8,128)(2,1)S(1)}, u32[]{:S(2)}, u32[]{:S(2)}) collective-permute-start(bf16[16,128]{1,0:T(8,128)(2,1)S(1)} %reduce_sum.18), channel_id=1, source_target_pairs={{0,0},{1,16},{2,32},{3,48},{4,64},{5,80},{6,96},{7,112},{8,128},{9... | collective-permute-start | bytes 12296 | tf_op jit(solution)/shard_map/ppermute | solution.py:262
  39.1 4.0 %collective-permute-start.3 = (bf16[16,128]{1,0:T(8,128)(2,1)S(1)}, bf16[16,128]{1,0:T(8,128)(2,1)S(1)}, u32[]{:S(2)}, u32[]{:S(2)}) collective-permute-start(bf16[16,128]{1,0:T(8,128)(2,1)S(1)} %reduce_sum.18), channel_id=1, source_target_pairs={{0,16},{1,0},{2,48},{3,32},{4,80},{5,64},{6,112},{7,96},{8,144},{9... | collective-permute-start | bytes 12296 | tf_op jit(solution)/shard_map/ppermute | solution.py:264
  43.2 14.9 %collective-permute-start.6 = (bf16[2,528,128]{2,1,0:T(8,128)(2,1)S(1)}, bf16[2,528,128]{2,1,0:T(8,128)(2,1)S(1)}, u32[]{:S(2)}, u32[]{:S(2)}) collective-permute-start(bf16[2,528,128]{2,1,0:T(8,128)(2,1)S(1)} %bitcast.56), channel_id=1, source_target_pairs={{0,224},{32,0},{64,32},{96,64},{128,96},{160,128},{192,160},{224,1... | collective-permute-start | bytes 811016 | tf_op jit(solution)/shard_map/ppermute | solution.py:227
  52.8 8.7 %collective-permute-start.4 = (bf16[2,528,128]{2,1,0:T(8,128)(2,1)S(1)}, bf16[2,528,128]{2,1,0:T(8,128)(2,1)S(1)}, u32[]{:S(2)}, u32[]{:S(2)}) collective-permute-start(bf16[2,528,128]{2,1,0:T(8,128)(2,1)S(1)} %bitcast.57), channel_id=1, source_target_pairs={{0,32},{32,64},{64,96},{96,128},{128,160},{160,192},{192,224},{224... | collective-permute-start | bytes 811016 | tf_op jit(solution)/shard_map/ppermute | solution.py:227
  58.1 7.8 %collective-permute-start.7 = (bf16[2,528,128]{2,1,0:T(8,128)(2,1)S(1)}, bf16[2,528,128]{2,1,0:T(8,128)(2,1)S(1)}, u32[]{:S(2)}, u32[]{:S(2)}) collective-permute-start(bf16[2,528,128]{2,1,0:T(8,128)(2,1)S(1)} %collective-permute-done.6.refs_1_), channel_id=1, source_target_pairs={{0,224},{32,0},{64,32},{96,64},{128,96},{160,128},{192,160},{224,1... | collective-permute-start | bytes 811016 | tf_op jit(solution)/shard_map/ppermute | solution.py:227
  61.5 7.5 %collective-permute-start.5 = (bf16[2,528,128]{2,1,0:T(8,128)(2,1)S(1)}, bf16[2,528,128]{2,1,0:T(8,128)(2,1)S(1)}, u32[]{:S(2)}, u32[]{:S(2)}) collective-permute-start(bf16[2,528,128]{2,1,0:T(8,128)(2,1)S(1)} %collective-permute-done.4.refs_7_), channel_id=1, source_target_pairs={{0,32},{32,64},{64,96},{96,128},{128,160},{160,192},{192,224},{224... | collective-permute-start | bytes 811016 | tf_op jit(solution)/shard_map/ppermute | solution.py:227
  69.0 6.5 %collective-permute-start.9 = (bf16[2,528,128]{2,1,0:T(8,128)(2,1)S(1)}, bf16[2,528,128]{2,1,0:T(8,128)(2,1)S(1)}, u32[]{:S(2)}, u32[]{:S(2)}) collective-permute-start(bf16[2,528,128]{2,1,0:T(8,128)(2,1)S(1)} %collective-permute-done.5.refs_6_), channel_id=1, source_target_pairs={{0,32},{32,64},{64,96},{96,128},{128,160},{160,192},{192,224},{224... | collective-permute-start | bytes 811016 | tf_op jit(solution)/shard_map/ppermute | solution.py:227
  69.0 8.9 %collective-permute-start.8 = (bf16[2,528,128]{2,1,0:T(8,128)(2,1)S(1)}, bf16[2,528,128]{2,1,0:T(8,128)(2,1)S(1)}, u32[]{:S(2)}, u32[]{:S(2)}) collective-permute-start(bf16[2,528,128]{2,1,0:T(8,128)(2,1)S(1)} %collective-permute-done.7.refs_2_), channel_id=1, source_target_pairs={{0,224},{32,0},{64,32},{96,64},{128,96},{160,128},{192,160},{224,1... | collective-permute-start | bytes 811016 | tf_op jit(solution)/shard_map/ppermute | solution.py:227
  75.5 6.5 %collective-permute-start.10 = (bf16[2,528,128]{2,1,0:T(8,128)(2,1)S(1)}, bf16[2,528,128]{2,1,0:T(8,128)(2,1)S(1)}, u32[]{:S(2)}, u32[]{:S(2)}) collective-permute-start(bf16[2,528,128]{2,1,0:T(8,128)(2,1)S(1)} %collective-permute-done.9.refs_5_), channel_id=1, source_target_pairs={{0,32},{32,64},{64,96},{96,128},{128,160},{160,192},{192,224},{224... | collective-permute-start | bytes 811016 | tf_op jit(solution)/shard_map/ppermute | solution.py:227
  75.6 6.4 %copy-start = (bf16[8448,128]{1,0:T(8,128)(2,1)S(1)}, bf16[8448,128]{1,0:T(8,128)(2,1)}, u32[]{:S(2)}) copy-start(bf16[8448,128]{1,0:T(8,128)(2,1)} %all-gather.3.cloned.1.call-done) | copy-start | bytes 6488068
  75.6 6.4 %copy-start.2 = (bf16[256,2048]{1,0:T(8,128)(2,1)S(1)}, bf16[256,2048]{1,0:T(8,128)(2,1)}, u32[]{:S(2)}) copy-start(bf16[256,2048]{1,0:T(8,128)(2,1)} %refs_9_.1) | copy-start | bytes 3145732
  75.6 6.4 %copy-start.3 = (bf16[128,2048]{1,0:T(8,128)(2,1)S(1)}, bf16[128,2048]{1,0:T(8,128)(2,1)}, u32[]{:S(2)}) copy-start(bf16[128,2048]{1,0:T(8,128)(2,1)} %refs_10_.1) | copy-start | bytes 1572868
  89.9 3.2 %collective-permute-start.11 = (bf16[256,128]{1,0:T(8,128)(2,1)S(1)}, bf16[256,128]{1,0:T(8,128)(2,1)S(1)}, u32[]{:S(2)}, u32[]{:S(2)}) collective-permute-start(bf16[256,128]{1,0:T(8,128)(2,1)S(1)} %convert_element_type.145), channel_id=1, source_target_pairs={{0,32},{32,0},{64,96},{96,64},{128,160},{160,128},{192,224},{224,1... | collective-permute-start | bytes 196616 | tf_op jit(solution)/shard_map/ppermute | solution.py:232
  93.1 6.7 %collective-permute-start.12 = (bf16[256,128]{1,0:T(8,128)(2,1)S(1)}, bf16[256,128]{1,0:T(8,128)(2,1)S(1)}, u32[]{:S(2)}, u32[]{:S(2)}) collective-permute-start(bf16[256,128]{1,0:T(8,128)(2,1)S(1)} %fusion.5), channel_id=1, source_target_pairs={{0,64},{32,96},{64,0},{96,32},{128,192},{160,224},{192,128},{224,1... | collective-permute-start | bytes 196616 | tf_op jit(solution)/shard_map/ppermute | solution.py:232
  93.4 14.9 %collective-permute-start.13 = (bf16[2,512,128]{2,1,0:T(8,128)(2,1)S(1)}, bf16[2,512,128]{2,1,0:T(8,128)(2,1)S(1)}, u32[]{:S(2)}, u32[]{:S(2)}) collective-permute-start(bf16[2,512,128]{2,1,0:T(8,128)(2,1)S(1)} %get-tuple-element.79), channel_id=1, source_target_pairs={{0,32},{32,64},{64,96},{96,128},{128,160},{160,192},{192,224},{224... | collective-permute-start | bytes 786440 | tf_op jit(solution)/shard_map/ppermute | solution.py:227
  94.3 14.0 %collective-permute-start.14 = (bf16[2,512,128]{2,1,0:T(8,128)(2,1)S(1)}, bf16[2,512,128]{2,1,0:T(8,128)(2,1)S(1)}, u32[]{:S(2)}, u32[]{:S(2)}) collective-permute-start(bf16[2,512,128]{2,1,0:T(8,128)(2,1)S(1)} %get-tuple-element.80), channel_id=1, source_target_pairs={{0,224},{32,0},{64,32},{96,64},{128,96},{160,128},{192,160},{224,1... | collective-permute-start | bytes 786440 | tf_op jit(solution)/shard_map/ppermute | solution.py:227
  99.8 8.4 %collective-permute-start.15 = (bf16[256,128]{1,0:T(8,128)(2,1)S(1)}, bf16[256,128]{1,0:T(8,128)(2,1)S(1)}, u32[]{:S(2)}, u32[]{:S(2)}) collective-permute-start(bf16[256,128]{1,0:T(8,128)(2,1)S(1)} %fusion.8), channel_id=1, source_target_pairs={{0,128},{32,160},{64,192},{96,224},{128,0},{160,32},{192,64},{224,... | collective-permute-start | bytes 196616 | tf_op jit(solution)/shard_map/ppermute | solution.py:232
  108.3 13.3 %collective-permute-start.18 = (bf16[8,768,128]{2,1,0:T(8,128)(2,1)S(1)}, bf16[8,768,128]{2,1,0:T(8,128)(2,1)S(1)}, u32[]{:S(2)}, u32[]{:S(2)}) collective-permute-start(bf16[8,768,128]{2,1,0:T(8,128)(2,1)S(1)} %shard_map.105), channel_id=1, source_target_pairs={{0,1},{1,0},{2,3},{3,2},{4,5},{5,4},{6,7},{7,6},{8,9},{9,8},{10,11... | collective-permute-start | bytes 4718600 | tf_op jit(solution)/shard_map/ppermute | solution.py:232
  116.2 5.3 %collective-permute-start.21 = (bf16[256,128]{1,0:T(8,128)(2,1)S(1)}, bf16[256,128]{1,0:T(8,128)(2,1)S(1)}, u32[]{:S(2)}, u32[]{:S(2)}) collective-permute-start(bf16[256,128]{1,0:T(8,128)(2,1)S(1)} %fusion.6), channel_id=1, source_target_pairs={{0,16},{16,0},{1,17},{17,1},{2,18},{18,2},{3,19},{19,3},{4,20},{20... | collective-permute-start | bytes 196616 | tf_op jit(solution)/shard_map/ppermute | solution.py:232
  117.3 9.3 %collective-permute-start.17 = (bf16[2,512,128]{2,1,0:T(8,128)(2,1)S(1)}, bf16[2,512,128]{2,1,0:T(8,128)(2,1)}, u32[]{:S(2)}, u32[]{:S(2)}) collective-permute-start(bf16[2,512,128]{2,1,0:T(8,128)(2,1)S(1)} %add_convert_fusion.3), channel_id=1, source_target_pairs={{0,224},{32,0},{64,32},{96,64},{128,96},{160,128},{192,160},{224,1... | collective-permute-start | bytes 786440 | tf_op jit(solution)/shard_map/ppermute | solution.py:227
  117.5 9.1 %collective-permute-start.16 = (bf16[2,512,128]{2,1,0:T(8,128)(2,1)S(1)}, bf16[2,512,128]{2,1,0:T(8,128)(2,1)}, u32[]{:S(2)}, u32[]{:S(2)}) collective-permute-start(bf16[2,512,128]{2,1,0:T(8,128)(2,1)S(1)} %add_convert_fusion.4), channel_id=1, source_target_pairs={{0,32},{32,64},{64,96},{96,128},{128,160},{160,192},{192,224},{224... | collective-permute-start | bytes 786440 | tf_op jit(solution)/shard_map/ppermute | solution.py:227
  129.4 31.6 %all-to-all-start.1 = ((bf16[8,896,128]{2,1,0:T(8,128)(2,1)}), bf16[8,896,128]{2,1,0:T(8,128)(2,1)S(1)}, u32[]{:S(2)}, u32[]{:S(2)}) async-start(bf16[8,896,128]{2,1,0:T(8,128)(2,1)} %shard_map.107), calls=%async_computation.1 | async-start | bytes 3670016 | tf_op jit(solution)/shard_map/all_to_all | solution.py:344
  138.7 6.2 %collective-permute-start.20 = (bf16[2,512,128]{2,1,0:T(8,128)(2,1)S(1)}, bf16[2,512,128]{2,1,0:T(8,128)(2,1)S(1)}, u32[]{:S(2)}, u32[]{:S(2)}) collective-permute-start(bf16[2,512,128]{2,1,0:T(8,128)(2,1)S(1)} %add_convert_fusion.1), channel_id=1, source_target_pairs={{0,224},{32,0},{64,32},{96,64},{128,96},{160,128},{192,160},{224,1... | collective-permute-start | bytes 786440 | tf_op jit(solution)/shard_map/ppermute | solution.py:227
  140.0 7.4 %collective-permute-start.19 = (bf16[2,512,128]{2,1,0:T(8,128)(2,1)S(1)}, bf16[2,512,128]{2,1,0:T(8,128)(2,1)S(1)}, u32[]{:S(2)}, u32[]{:S(2)}) collective-permute-start(bf16[2,512,128]{2,1,0:T(8,128)(2,1)S(1)} %add_convert_fusion.2), channel_id=1, source_target_pairs={{0,32},{32,64},{64,96},{96,128},{128,160},{160,192},{192,224},{224... | collective-permute-start | bytes 786440 | tf_op jit(solution)/shard_map/ppermute | solution.py:227
  144.9 9.5 %copy-start.5 = (bf16[2,512,128]{2,1,0:T(8,128)(2,1)}, bf16[2,512,128]{2,1,0:T(8,128)(2,1)S(1)}, u32[]{:S(2)}) copy-start(bf16[2,512,128]{2,1,0:T(8,128)(2,1)S(1)} %collective-permute-done.20) | copy-start | bytes 786436
  147.5 6.8 %collective-permute-start.22 = (bf16[2,512,128]{2,1,0:T(8,128)(2,1)S(1)}, bf16[2,512,128]{2,1,0:T(8,128)(2,1)S(1)}, u32[]{:S(2)}, u32[]{:S(2)}) collective-permute-start(bf16[2,512,128]{2,1,0:T(8,128)(2,1)S(1)} %add_convert_fusion), channel_id=1, source_target_pairs={{0,32},{32,64},{64,96},{96,128},{128,160},{160,192},{192,224},{224... | collective-permute-start | bytes 786440 | tf_op jit(solution)/shard_map/ppermute | solution.py:227
  147.6 28.3 %collective-permute-start.25 = (bf16[256,128]{1,0:T(8,128)(2,1)S(1)}, bf16[256,128]{1,0:T(8,128)(2,1)S(1)}, u32[]{:S(2)}, u32[]{:S(2)}) collective-permute-start(bf16[256,128]{1,0:T(8,128)(2,1)S(1)} %add_convert_fusion.6), channel_id=1, source_target_pairs={{0,0},{1,16},{2,32},{3,48},{4,64},{5,80},{6,96},{7,112},{8,128},{9... | collective-permute-start | bytes 196616 | tf_op jit(solution)/shard_map/ppermute | solution.py:345
  154.3 2.3 %copy-start.7 = (bf16[2,512,128]{2,1,0:T(8,128)(2,1)}, bf16[2,512,128]{2,1,0:T(8,128)(2,1)S(1)}, u32[]{:S(2)}) copy-start(bf16[2,512,128]{2,1,0:T(8,128)(2,1)S(1)} %collective-permute-done.22) | copy-start | bytes 786436
  154.4 11.3 %collective-permute-start.23 = (bf16[512,128]{1,0:T(8,128)(2,1)S(1)}, bf16[512,128]{1,0:T(8,128)(2,1)S(1)}, u32[]{:S(2)}, u32[]{:S(2)}) collective-permute-start(bf16[512,128]{1,0:T(8,128)(2,1)S(1)} %fusion.4), channel_id=1, source_target_pairs={{0,16},{16,0},{1,17},{17,1},{2,18},{18,2},{3,19},{19,3},{4,20},{20... | collective-permute-start | bytes 393224 | tf_op jit(solution)/shard_map/ppermute | solution.py:232
  156.7 9.1 %copy-start.6 = (bf16[2,512,128]{2,1,0:T(8,128)(2,1)S(1)}, bf16[2,512,128]{2,1,0:T(8,128)(2,1)}, u32[]{:S(2)}) copy-start(bf16[2,512,128]{2,1,0:T(8,128)(2,1)} %copy-done.5) | copy-start | bytes 786436
  161.0 4.7 %copy-start.8 = (bf16[2,512,128]{2,1,0:T(8,128)(2,1)S(1)}, bf16[2,512,128]{2,1,0:T(8,128)(2,1)}, u32[]{:S(2)}) copy-start(bf16[2,512,128]{2,1,0:T(8,128)(2,1)} %copy-done.7) | copy-start | bytes 786436
  161.3 14.0 %collective-permute-start.26 = (f32[64,128]{1,0:T(8,128)S(1)}, f32[64,128]{1,0:T(8,128)S(1)}, u32[]{:S(2)}, u32[]{:S(2)}) collective-permute-start(f32[64,128]{1,0:T(8,128)S(1)} %slice.67), channel_id=1, source_target_pairs={{0,1},{1,0},{2,3},{3,2},{4,5},{5,4},{6,7},{7,6},{8,9},{9,8},{10,11... | collective-permute-start | bytes 98312 | tf_op jit(solution)/shard_map/ppermute | solution.py:232
  165.8 18.6 %collective-permute-start.24 = (bf16[512,128]{1,0:T(8,128)(2,1)S(1)}, bf16[512,128]{1,0:T(8,128)(2,1)S(1)}, u32[]{:S(2)}, u32[]{:S(2)}) collective-permute-start(bf16[512,128]{1,0:T(8,128)(2,1)S(1)} %fusion.2), channel_id=1, source_target_pairs={{0,0},{1,16},{2,32},{3,48},{4,64},{5,80},{6,96},{7,112},{8,128},{9... | collective-permute-start | bytes 393224 | tf_op jit(solution)/shard_map/ppermute | solution.py:343
Sparse Core Ops, SparseCore 0:
  10.6 45.3 all-gather.2
